TPU v7x, 32 devices: a whole 2x2x4 slice. The times are simulated.
32 devices in a mesh: section: 2 (over x), ctx: 8 (over z, y), tp: 2 (over core).
Axes of the slice: x: 2, y: 2, z: 4, core: 2. Of those that a mesh axis runs over, the one named last changes fastest.
Arguments:
- tokens: bfloat16 [4, 2048, 1024], P(None, 'ctx'), may hold values from -6 to 6
- cotangent: bfloat16 [4, 2048, 1024], P(None, 'ctx'), may hold values from -6 to 6
- block_order: int32 [16], replicated, may hold values from 0 to 15, each once
- first_gain: float32 [2, 1024], P('section'), may hold values from 0.25 to 1.75
- first_bias: float32 [2, 1024], P('section'), may hold values from -1.75 to 1.75
- second_gain: float32 [2, 1024], P('section'), may hold values from 0.25 to 1.75
- second_bias: float32 [2, 1024], P('section'), may hold values from -1.75 to 1.75
- joint_weight: bfloat16 [2, 3, 1024, 1024], P('section', None, None, 'tp'), may hold values from -0.25 to 0.25
- joint_bias: float32 [2, 3, 1024], P('section', None, 'tp'), may hold values from -1.75 to 1.75
- output_weight: bfloat16 [2, 1024, 1024], P('section', 'tp'), may hold values from -0.5 to 0.5
- output_bias: float32 [2, 1024], P('section'), may hold values from -1.75 to 1.75
- up_weight: bfloat16 [2, 1024, 4096], P('section', None, 'tp'), may hold values from -0.1875 to 0.1875
- up_bias: float32 [2, 4096], P('section', 'tp'), may hold values from -1.75 to 1.75
- down_weight: bfloat16 [2, 4096, 1024], P('section', 'tp'), may hold values from -0.125 to 0.125
- down_bias: float32 [2, 1024], P('section'), may hold values from -1.75 to 1.75
Outputs:
- section_out: bfloat16 [2, 4, 2048, 1024], P('section', None, 'ctx')
- section_in_grad: bfloat16 [2, 4, 2048, 1024], P('section', None, 'ctx')
- first_gain_gradient: float32 [2, 1024], P('section')
- first_bias_gradient: float32 [2, 1024], P('section')
- second_gain_gradient: float32 [2, 1024], P('section')
- second_bias_gradient: float32 [2, 1024], P('section')
- joint_weight_gradient: float32 [2, 3, 1024, 1024], P('section', None, 'ctx', 'tp')
- joint_bias_gradient: float32 [2, 3, 1024], P('section', None, 'tp')
- output_weight_gradient: float32 [2, 1024, 1024], P('section', 'tp', 'ctx')
- output_bias_gradient: float32 [2, 1024], P('section')
- up_weight_gradient: float32 [2, 1024, 4096], P('section', 'ctx', 'tp')
- up_bias_gradient: float32 [2, 4096], P('section', 'tp')
- down_weight_gradient: float32 [2, 4096, 1024], P('section', 'tp', 'ctx')
- down_bias_gradient: float32 [2, 1024], P('section')
- root_means: float32 [2, 3], P('section')
Inputs may be any that keep to these rules, and one draw needn't show every extreme that they name: `block_order`: each stored block's place in its sequence, every place once; the same for all sequences.
All inputs are finite; a program needn't handle non-finite values.
Results may differ from a plain program's by a relative error of at most 0.028.
Values may be sent and summed in bfloat16 or wider, within the bound.
A program may use at most 256 MiB of HBM per device.

v0:
```python
import jax
import jax.numpy as jnp
from jax import lax
from jax.sharding import PartitionSpec as P

HEAD = 64
ROT = 16
MICRO = 4


EPS = 1e-05
ROTARY_BASE = 10000.0
NEGATIVE = -1e30


def from_behind(shard, axis, by):
    size = lax.axis_size(axis)
    pairs = [(i, i + by) for i in range(size) if 0 <= i + by < size]
    return lax.ppermute(shard, axis, pairs)


def layer_norm(values, gain, shift):
    middle = jnp.mean(values, axis=-1, keepdims=True)
    centered = values - middle
    spread = jnp.mean(centered * centered, axis=-1, keepdims=True)
    return centered * lax.rsqrt(spread + EPS) * gain + shift


def rotate(values, cosine, sine):
    half = cosine.shape[-1]
    first = values[..., :half]
    second = values[..., half : 2 * half]
    return jnp.concatenate(
        [first * cosine - second * sine, second * cosine + first * sine, values[..., 2 * half :]],
        axis=-1,
    )


def angle_table(block_order, block_len):
    offsets = jnp.arange(block_len, dtype=jnp.int32)
    places = (block_order[:, None] * block_len + offsets[None, :]).reshape(-1)
    exponent = jnp.arange(ROT // 2, dtype=jnp.float32) * (2.0 / ROT)
    inverse = jnp.power(jnp.float32(ROTARY_BASE), -exponent)
    turns = places.astype(jnp.float32)[:, None] * inverse[None, :]
    return (places, jnp.cos(turns)[:, None, :], jnp.sin(turns)[:, None, :])


def project(state, params, cos_local, sin_local):
    (
        gain_one,
        bias_one,
        gain_two,
        bias_two,
        w_joint,
        b_joint,
        w_output,
        b_output,
        w_up,
        b_up,
        w_down,
        b_down,
    ) = params
    first_in = layer_norm(state, gain_one, bias_one).astype(jnp.bfloat16)
    second_in = layer_norm(state, gain_two, bias_two).astype(jnp.bfloat16)
    joined = (
        jnp.einsum("bld,tde->tble", first_in, w_joint, preferred_element_type=jnp.float32)
        + b_joint[:, None, None, :]
    )
    seq_count, row_count, local_width = joined.shape[1:]
    heads_view = joined.reshape(3, seq_count, row_count, local_width // HEAD, HEAD)
    queries = rotate(heads_view[0], cos_local, sin_local).astype(jnp.bfloat16)
    key_rows = (
        rotate(heads_view[1], cos_local, sin_local)
        .astype(jnp.bfloat16)
        .reshape(seq_count, row_count, local_width)
    )
    value_rows = joined[2].astype(jnp.bfloat16)
    hidden = jnp.einsum("bld,df->blf", second_in, w_up, preferred_element_type=jnp.float32) + b_up
    return (first_in, second_in, queries, key_rows, value_rows, hidden)


def attend(queries, key_full, value_full, allowed):
    seq_count, row_count, local_heads, _ = queries.shape
    key_count = key_full.shape[1]
    key_heads = key_full.reshape(seq_count, key_count, local_heads, HEAD)
    value_heads = value_full.reshape(seq_count, key_count, local_heads, HEAD)
    scores = jnp.einsum(
        "bqhc,bkhc->bhqk", queries, key_heads, preferred_element_type=jnp.float32
    ) * HEAD ** (-0.5)
    scores = jnp.where(allowed, scores, NEGATIVE)
    row_top = jnp.max(scores, axis=-1, keepdims=True)
    raised = jnp.exp(scores - row_top)
    row_total = jnp.sum(raised, axis=-1, keepdims=True)
    softmax = raised / row_total
    soft_low = softmax.astype(jnp.bfloat16)
    mixture = jnp.einsum(
        "bhqk,bkhc->bqhc", soft_low, value_heads, preferred_element_type=jnp.float32
    ).astype(jnp.bfloat16)
    return (
        softmax,
        soft_low,
        mixture.reshape(seq_count, row_count, local_heads * HEAD),
        key_heads,
        value_heads,
        row_top,
        row_total,
    )


def forward_step(state, params, cos_local, sin_local, allowed):
    first_in, second_in, queries, key_rows, value_rows, hidden = project(
        state, params, cos_local, sin_local
    )
    key_full, value_full = (
        lax.all_gather(key_rows, "ctx", axis=1, tiled=True),
        lax.all_gather(value_rows, "ctx", axis=1, tiled=True),
    )
    softmax, soft_low, mixture, key_heads, value_heads, row_top, row_total = attend(
        queries, key_full, value_full, allowed
    )
    active = jax.nn.gelu(hidden, approximate=False).astype(jnp.bfloat16)
    attn_part = jnp.einsum("ble,ed->bld", mixture, params[6], preferred_element_type=jnp.float32)
    ffn_part = jnp.einsum("blf,fd->bld", active, params[10], preferred_element_type=jnp.float32)
    attn_total, ffn_total = lax.psum((attn_part, ffn_part), "tp")
    attention = attn_total + params[7]
    feedforward = ffn_total + params[11]
    return (state + attention + feedforward, attention, feedforward, key_full, value_full)


def backward_step(state, upstream, params, cos_local, sin_local, allowed):
    (
        gain_one,
        bias_one,
        gain_two,
        bias_two,
        w_joint,
        b_joint,
        w_output,
        b_output,
        w_up,
        b_up,
        w_down,
        b_down,
    ) = params
    first_in, second_in, queries, key_rows, value_rows, hidden = project(
        state, params, cos_local, sin_local
    )
    key_full, value_full = (
        lax.all_gather(key_rows, "ctx", axis=1, tiled=True),
        lax.all_gather(value_rows, "ctx", axis=1, tiled=True),
    )
    softmax, soft_low, mixture, key_heads, value_heads, row_top, row_total = attend(
        queries, key_full, value_full, allowed
    )
    seq_count, row_count, local_heads, _ = queries.shape
    key_count = key_full.shape[1]
    local_width = local_heads * HEAD
    active_f32, gelu_pull = jax.vjp(lambda inner: jax.nn.gelu(inner, approximate=False), hidden)
    active = active_f32.astype(jnp.bfloat16)
    upstream_f32 = upstream.astype(jnp.float32)
    output_slope = jnp.einsum("ble,bld->ed", mixture, upstream, preferred_element_type=jnp.float32)
    down_slope = jnp.einsum("blf,bld->fd", active, upstream, preferred_element_type=jnp.float32)
    column_sums = jnp.sum(upstream_f32, axis=(0, 1))
    d_active = jnp.einsum("bld,fd->blf", upstream, w_down, preferred_element_type=jnp.float32)
    (d_hidden,) = gelu_pull(d_active)
    d_hidden_low = d_hidden.astype(jnp.bfloat16)
    up_slope = jnp.einsum(
        "bld,blf->df", second_in, d_hidden_low, preferred_element_type=jnp.float32
    )
    up_shift = jnp.sum(d_hidden_low.astype(jnp.float32), axis=(0, 1))
    d_second = jnp.einsum("blf,df->bld", d_hidden_low, w_up, preferred_element_type=jnp.float32)
    d_mixture = jnp.einsum(
        "bld,ed->ble", upstream, w_output, preferred_element_type=jnp.float32
    ).astype(jnp.bfloat16)
    d_mixture = d_mixture.reshape(seq_count, row_count, local_heads, HEAD)
    d_softmax = jnp.einsum(
        "bqhc,bkhc->bhqk", d_mixture, value_heads, preferred_element_type=jnp.float32
    )
    row_inner = jnp.sum(d_softmax * softmax, axis=-1, keepdims=True)
    d_scores = (softmax * (d_softmax - row_inner)).astype(jnp.bfloat16)
    score_scale = HEAD ** (-0.5)
    d_queries = (
        jnp.einsum("bhqk,bkhc->bqhc", d_scores, key_heads, preferred_element_type=jnp.float32)
        * score_scale
    )
    d_values = jnp.einsum(
        "bhqk,bqhc->bkhc", soft_low, d_mixture, preferred_element_type=jnp.float32
    )
    d_keys = (
        jnp.einsum("bhqk,bqhc->bkhc", d_scores, queries, preferred_element_type=jnp.float32)
        * score_scale
    )
    d_keys_own, d_values_own = (
        lax.psum_scatter(
            d_keys.reshape(seq_count, key_count, local_width).astype(jnp.bfloat16),
            "ctx",
            scatter_dimension=1,
            tiled=True,
        ).astype(jnp.float32),
        lax.psum_scatter(
            d_values.reshape(seq_count, key_count, local_width).astype(jnp.bfloat16),
            "ctx",
            scatter_dimension=1,
            tiled=True,
        ).astype(jnp.float32),
    )
    d_queries_pre = rotate(d_queries, cos_local, -sin_local).reshape(
        seq_count, row_count, local_width
    )
    d_keys_pre = rotate(
        d_keys_own.reshape(seq_count, row_count, local_heads, HEAD), cos_local, -sin_local
    ).reshape(seq_count, row_count, local_width)
    d_joined = jnp.stack([d_queries_pre, d_keys_pre, d_values_own]).astype(jnp.bfloat16)
    joint_slope = jnp.einsum(
        "bld,tble->tde", first_in, d_joined, preferred_element_type=jnp.float32
    )
    joint_shift = jnp.sum(d_joined.astype(jnp.float32), axis=(1, 2))
    d_first = jnp.einsum("tble,tde->bld", d_joined, w_joint, preferred_element_type=jnp.float32)
    d_first, d_second = (
        lax.psum(d_first.astype(jnp.bfloat16), "tp").astype(jnp.float32),
        lax.psum(d_second.astype(jnp.bfloat16), "tp").astype(jnp.float32),
    )

    def both_norms(values, first_gain, first_shift, second_gain, second_shift):
        return (
            layer_norm(values, first_gain, first_shift),
            layer_norm(values, second_gain, second_shift),
        )

    _, norm_pull = jax.vjp(both_norms, state, gain_one, bias_one, gain_two, bias_two)
    d_state, d_gain_one, d_bias_one, d_gain_two, d_bias_two = norm_pull((d_first, d_second))
    pieces = (
        d_gain_one,
        d_bias_one,
        d_gain_two,
        d_bias_two,
        joint_slope,
        joint_shift,
        output_slope,
        column_sums,
        up_slope,
        up_shift,
        down_slope,
        column_sums,
    )
    return (upstream_f32 + d_state, pieces)


def store(buffer, value, index, valid):
    previous = lax.dynamic_index_in_dim(buffer, index, 0, keepdims=False)
    return lax.dynamic_update_index_in_dim(buffer, jnp.where(valid, value, previous), index, 0)


def store_rows(buffer, value, start, valid):
    previous = lax.dynamic_slice_in_dim(buffer, start, value.shape[0], 0)
    return lax.dynamic_update_slice_in_dim(buffer, jnp.where(valid, value, previous), start, 0)


def on_device(
    tokens,
    cotangent,
    block_order,
    first_gain,
    first_bias,
    second_gain,
    second_bias,
    joint_weight,
    joint_bias,
    output_weight,
    output_bias,
    up_weight,
    up_bias,
    down_weight,
    down_bias,
):
    section_rank = lax.axis_index("section")
    last_section = lax.axis_size("section") - 1
    context_size = lax.axis_size("ctx")
    context_rank = lax.axis_index("ctx")
    seq_total, local_len, width = tokens.shape
    per_micro = seq_total // MICRO
    block_len = local_len // 2
    places, cosine, sine = angle_table(block_order, block_len)
    start_row = context_rank * local_len
    local_places = lax.dynamic_slice_in_dim(places, start_row, local_len, 0)
    cos_local = lax.dynamic_slice_in_dim(cosine, start_row, local_len, 0)
    sin_local = lax.dynamic_slice_in_dim(sine, start_row, local_len, 0)
    allowed = places[None, :] <= local_places[:, None]
    params = (
        first_gain[0],
        first_bias[0],
        second_gain[0],
        second_bias[0],
        joint_weight[0],
        joint_bias[0],
        output_weight[0],
        output_bias[0],
        up_weight[0],
        up_bias[0],
        down_weight[0],
        down_bias[0],
    )
    incoming = jnp.zeros((per_micro, local_len, width), jnp.bfloat16)
    saved_inputs = jnp.zeros((MICRO, per_micro, local_len, width), jnp.bfloat16)
    outputs_low = jnp.zeros((seq_total, local_len, width), jnp.bfloat16)
    moments = jnp.zeros((3,), jnp.float32)
    kept_rows = ()

    def forward_tick(tick, carry):
        incoming, saved_inputs, outputs_low, moments, kept = carry
        micro_index = tick - section_rank
        valid = (micro_index >= 0) & (micro_index < MICRO)
        safe_index = jnp.clip(micro_index, 0, MICRO - 1)
        own_rows = lax.dynamic_slice_in_dim(tokens, safe_index * per_micro, per_micro, 0)
        source = jnp.where(section_rank == 0, own_rows, incoming)
        state = source.astype(jnp.float32)
        result, attention, feedforward, key_full, value_full = forward_step(
            state, params, cos_local, sin_local, allowed
        )
        result_low = result.astype(jnp.bfloat16)
        fresh = jnp.stack(
            [
                jnp.sum(state * state),
                jnp.sum(attention * attention),
                jnp.sum(feedforward * feedforward),
            ]
        )
        moments = moments + jnp.where(valid, fresh, 0.0)
        saved_inputs = store(saved_inputs, source, safe_index, valid)
        outputs_low = store_rows(outputs_low, result_low, safe_index * per_micro, valid)
        incoming = from_behind(result_low, "section", 1)
        return (incoming, saved_inputs, outputs_low, moments, kept)

    incoming, saved_inputs, outputs_low, moments, kept_rows = lax.fori_loop(
        0, MICRO + 1, forward_tick, (incoming, saved_inputs, outputs_low, moments, kept_rows)
    )
    returned = jnp.zeros((per_micro, local_len, width), jnp.bfloat16)
    input_grads = jnp.zeros((seq_total, local_len, width), jnp.bfloat16)
    running = jax.tree.map(lambda param: jnp.zeros(param.shape, jnp.float32), params)

    def backward_tick(tick, carry):
        returned, input_grads, running = carry
        micro_index = MICRO - 1 - tick + (last_section - section_rank)
        valid = (micro_index >= 0) & (micro_index < MICRO)
        safe_index = jnp.clip(micro_index, 0, MICRO - 1)
        saved = lax.dynamic_index_in_dim(saved_inputs, safe_index, 0, keepdims=False)
        given = lax.dynamic_slice_in_dim(cotangent, safe_index * per_micro, per_micro, 0)
        upstream = jnp.where(section_rank == last_section, given, returned)
        d_input, pieces = backward_step(
            saved.astype(jnp.float32), upstream, params, cos_local, sin_local, allowed
        )
        d_low = d_input.astype(jnp.bfloat16)
        input_grads = store_rows(input_grads, d_low, safe_index * per_micro, valid)
        running = jax.tree.map(
            lambda before, latest: before + jnp.where(valid, latest, 0.0), running, pieces
        )
        returned = from_behind(d_low, "section", -1)
        return (returned, input_grads, running)

    returned, input_grads, running = lax.fori_loop(
        0, MICRO + 1, backward_tick, (returned, input_grads, running)
    )
    joint_total, output_total, up_total, down_total = (
        lax.psum_scatter(
            running[4].astype(jnp.bfloat16), "ctx", scatter_dimension=1, tiled=True
        ).astype(jnp.float32),
        lax.psum_scatter(
            running[6].astype(jnp.bfloat16), "ctx", scatter_dimension=1, tiled=True
        ).astype(jnp.float32),
        lax.psum_scatter(
            running[8].astype(jnp.bfloat16), "ctx", scatter_dimension=0, tiled=True
        ).astype(jnp.float32),
        lax.psum_scatter(
            running[10].astype(jnp.bfloat16), "ctx", scatter_dimension=1, tiled=True
        ).astype(jnp.float32),
    )
    small = (
        lax.psum(running[0].astype(jnp.bfloat16), "ctx").astype(jnp.float32),
        lax.psum(running[1].astype(jnp.bfloat16), "ctx").astype(jnp.float32),
        lax.psum(running[2].astype(jnp.bfloat16), "ctx").astype(jnp.float32),
        lax.psum(running[3].astype(jnp.bfloat16), "ctx").astype(jnp.float32),
        lax.psum(running[5].astype(jnp.bfloat16), "ctx").astype(jnp.float32),
        lax.psum(running[7].astype(jnp.bfloat16), "ctx").astype(jnp.float32),
        lax.psum(running[9].astype(jnp.bfloat16), "ctx").astype(jnp.float32),
        lax.psum(running[11].astype(jnp.bfloat16), "ctx").astype(jnp.float32),
        lax.psum(moments.astype(jnp.bfloat16), "ctx").astype(jnp.float32),
    )
    (
        gain_one_total,
        bias_one_total,
        gain_two_total,
        bias_two_total,
        joint_shift_total,
        output_shift_total,
        up_shift_total,
        down_shift_total,
        moment_total,
    ) = small
    entry_count = seq_total * local_len * context_size * width
    root_means = jnp.sqrt(moment_total / entry_count)
    return (
        outputs_low[None],
        input_grads[None],
        gain_one_total[None],
        bias_one_total[None],
        gain_two_total[None],
        bias_two_total[None],
        joint_total[None],
        joint_shift_total[None],
        output_total[None],
        output_shift_total[None],
        up_total[None],
        up_shift_total[None],
        down_total[None],
        down_shift_total[None],
        root_means[None],
    )


def solution(mesh):
    in_specs = (
        P(None, "ctx", None),
        P(None, "ctx", None),
        P(),
        P("section", None),
        P("section", None),
        P("section", None),
        P("section", None),
        P("section", None, None, "tp"),
        P("section", None, "tp"),
        P("section", "tp", None),
        P("section", None),
        P("section", None, "tp"),
        P("section", "tp"),
        P("section", "tp", None),
        P("section", None),
    )
    out_specs = (
        P("section", None, "ctx", None),
        P("section", None, "ctx", None),
        P("section", None),
        P("section", None),
        P("section", None),
        P("section", None),
        P("section", None, "ctx", "tp"),
        P("section", None, "tp"),
        P("section", "tp", "ctx"),
        P("section", None),
        P("section", "ctx", "tp"),
        P("section", "tp"),
        P("section", "tp", "ctx"),
        P("section", None),
        P("section", None),
    )
    return jax.shard_map(
        on_device, mesh=mesh, in_specs=in_specs, out_specs=out_specs, check_vma=False
    )
```

profile of v0, /device:TPU:0, one launch (start us, length us, event | category | flops | bytes accessed | tf_op | source)
XLA Modules:
  0.0 2856.5 jit_solution(653437939894250515)
XLA Ops:
  13.6 845.2 %while.63 = (s32[]{:T(128)}, bf16[1,256,1024]{2,1,0:T(8,128)(2,1)S(1)}, bf16[4,1,256,1024]{3,2,1,0:T(8,128)(2,1)S(1)}, bf16[4,256,1024]{2,1,0:T(8,128)(2,1)}, f3...) while((s32[]{:T(128)}, ...), condition=%wide.region_10.11_spmd.clone, body=%wide.region_0.10_spmd.clone.sunk | while | flops 4375709696 | bytes 164072080 | solution.py:334
  41.1 38.8 %all-gather.15.cloned.1.call-done = bf16[1,2048,512]{1,2,0:T(8,128)(2,1)} async-done(((bf16[1,256,512]{1,2,0:T(8,128)(2,1)}), bf16[1,2048,512]{1,2,0:T(8,128)(2,1)}) %all-gather.15.cloned.1.call-update) | async-done | bytes 2097168 | tf_op jit(solution)/shard_map/while/body/eval_jaxpr/all_gather | solution.py:115
  210.8 37.9 %all-gather.15.cloned.1.call-done = bf16[1,2048,512]{1,2,0:T(8,128)(2,1)} async-done(((bf16[1,256,512]{1,2,0:T(8,128)(2,1)}), bf16[1,2048,512]{1,2,0:T(8,128)(2,1)}) %all-gather.15.cloned.1.call-update) | async-done | bytes 2097168 | tf_op jit(solution)/shard_map/while/body/eval_jaxpr/all_gather | solution.py:115
  258.5 21.4 fusion.313
  379.6 37.9 %all-gather.15.cloned.1.call-done = bf16[1,2048,512]{1,2,0:T(8,128)(2,1)} async-done(((bf16[1,256,512]{1,2,0:T(8,128)(2,1)}), bf16[1,2048,512]{1,2,0:T(8,128)(2,1)}) %all-gather.15.cloned.1.call-update) | async-done | bytes 2097168 | tf_op jit(solution)/shard_map/while/body/eval_jaxpr/all_gather | solution.py:115
  548.5 37.9 %all-gather.15.cloned.1.call-done = bf16[1,2048,512]{1,2,0:T(8,128)(2,1)} async-done(((bf16[1,256,512]{1,2,0:T(8,128)(2,1)}), bf16[1,2048,512]{1,2,0:T(8,128)(2,1)}) %all-gather.15.cloned.1.call-update) | async-done | bytes 2097168 | tf_op jit(solution)/shard_map/while/body/eval_jaxpr/all_gather | solution.py:115
  596.1 21.4 fusion.313
  717.4 37.9 %all-gather.15.cloned.1.call-done = bf16[1,2048,512]{1,2,0:T(8,128)(2,1)} async-done(((bf16[1,256,512]{1,2,0:T(8,128)(2,1)}), bf16[1,2048,512]{1,2,0:T(8,128)(2,1)}) %all-gather.15.cloned.1.call-update) | async-done | bytes 2097168 | tf_op jit(solution)/shard_map/while/body/eval_jaxpr/all_gather | solution.py:115
  861.2 1657.7 %while.64 = (s32[]{:T(128)}, bf16[1,256,1024]{2,1,0:T(8,128)(2,1)}, bf16[4,256,1024]{2,1,0:T(8,128)(2,1)}, f32[1024]{0:T(1024)}, f32[1024]{0:T(1024)}, /*index=5...) while((s32[]{:T(128)}, bf16[1,256,1024]{2,1,0:T(8,128)(2,1)}, ...), condition=%wide.region_32.33_spmd.clone, body=%wide.region_11.32_spmd.clone.sunk | while | flops 11742368768 | bytes 576063744 | solution.py:360
  900.1 44.7 %all-gather.17.cloned.1.call-done = bf16[1,2048,512]{1,2,0:T(8,128)(2,1)} async-done(((bf16[1,256,512]{1,2,0:T(8,128)(2,1)}), bf16[1,2048,512]{1,2,0:T(8,128)(2,1)}) %all-gather.17.cloned.1.call-update) | async-done | bytes 2097168 | tf_op jit(solution)/shard_map/while/body/eval_jaxpr/all_gather | solution.py:149
  954.6 22.0 fusion.350
  1067.0 26.4 reduce-scatter.21.cloned.1.call-done
  1098.2 65.5 %reduce-scatter.19.cloned.1.call-done = bf16[1,256,512]{2,1,0:T(8,128)(2,1)} async-done(((bf16[1,2048,512]{2,1,0:T(8,128)(2,1)}), bf16[1,256,512]{2,1,0:T(8,128)(2,1)}) %reduce-scatter.19.cloned.1.call-update) | async-done | bytes 262160 | tf_op jit(solution)/shard_map/while/body/eval_jaxpr/reduce_scatter | solution.py:200
  1227.7 43.2 %all-gather.17.cloned.1.call-done = bf16[1,2048,512]{1,2,0:T(8,128)(2,1)} async-done(((bf16[1,256,512]{1,2,0:T(8,128)(2,1)}), bf16[1,2048,512]{1,2,0:T(8,128)(2,1)}) %all-gather.17.cloned.1.call-update) | async-done | bytes 2097168 | tf_op jit(solution)/shard_map/while/body/eval_jaxpr/all_gather | solution.py:149
  1280.7 22.0 fusion.350
  1398.3 21.4 reduce-scatter.21.cloned.1.call-done
  1424.5 65.3 %reduce-scatter.19.cloned.1.call-done = bf16[1,256,512]{2,1,0:T(8,128)(2,1)} async-done(((bf16[1,2048,512]{2,1,0:T(8,128)(2,1)}), bf16[1,256,512]{2,1,0:T(8,128)(2,1)}) %reduce-scatter.19.cloned.1.call-update) | async-done | bytes 262160 | tf_op jit(solution)/shard_map/while/body/eval_jaxpr/reduce_scatter | solution.py:200
  1554.5 42.5 %all-gather.17.cloned.1.call-done = bf16[1,2048,512]{1,2,0:T(8,128)(2,1)} async-done(((bf16[1,256,512]{1,2,0:T(8,128)(2,1)}), bf16[1,2048,512]{1,2,0:T(8,128)(2,1)}) %all-gather.17.cloned.1.call-update) | async-done | bytes 2097168 | tf_op jit(solution)/shard_map/while/body/eval_jaxpr/all_gather | solution.py:149
  1606.8 22.0 fusion.350
  1724.2 21.5 reduce-scatter.21.cloned.1.call-done
  1750.4 65.4 %reduce-scatter.19.cloned.1.call-done = bf16[1,256,512]{2,1,0:T(8,128)(2,1)} async-done(((bf16[1,2048,512]{2,1,0:T(8,128)(2,1)}), bf16[1,256,512]{2,1,0:T(8,128)(2,1)}) %reduce-scatter.19.cloned.1.call-update) | async-done | bytes 262160 | tf_op jit(solution)/shard_map/while/body/eval_jaxpr/reduce_scatter | solution.py:200
  1880.6 42.4 %all-gather.17.cloned.1.call-done = bf16[1,2048,512]{1,2,0:T(8,128)(2,1)} async-done(((bf16[1,256,512]{1,2,0:T(8,128)(2,1)}), bf16[1,2048,512]{1,2,0:T(8,128)(2,1)}) %all-gather.17.cloned.1.call-update) | async-done | bytes 2097168 | tf_op jit(solution)/shard_map/while/body/eval_jaxpr/all_gather | solution.py:149
  1932.8 22.0 fusion.350
  2076.6 65.5 %reduce-scatter.19.cloned.1.call-done = bf16[1,256,512]{2,1,0:T(8,128)(2,1)} async-done(((bf16[1,2048,512]{2,1,0:T(8,128)(2,1)}), bf16[1,256,512]{2,1,0:T(8,128)(2,1)}) %reduce-scatter.19.cloned.1.call-update) | async-done | bytes 262160 | tf_op jit(solution)/shard_map/while/body/eval_jaxpr/reduce_scatter | solution.py:200
  2206.8 42.5 %all-gather.17.cloned.1.call-done = bf16[1,2048,512]{1,2,0:T(8,128)(2,1)} async-done(((bf16[1,256,512]{1,2,0:T(8,128)(2,1)}), bf16[1,2048,512]{1,2,0:T(8,128)(2,1)}) %all-gather.17.cloned.1.call-update) | async-done | bytes 2097168 | tf_op jit(solution)/shard_map/while/body/eval_jaxpr/all_gather | solution.py:149
  2259.1 22.0 fusion.350
  2376.6 21.4 reduce-scatter.21.cloned.1.call-done
  2402.8 65.4 %reduce-scatter.19.cloned.1.call-done = bf16[1,256,512]{2,1,0:T(8,128)(2,1)} async-done(((bf16[1,2048,512]{2,1,0:T(8,128)(2,1)}), bf16[1,256,512]{2,1,0:T(8,128)(2,1)}) %reduce-scatter.19.cloned.1.call-update) | async-done | bytes 262160 | tf_op jit(solution)/shard_map/while/body/eval_jaxpr/reduce_scatter | solution.py:200
  2547.3 37.2 %all-reduce.2 = (bf16[1,1024]{1,0:T(2,128)(2,1)S(1)}, bf16[1,1024]{1,0:T(2,128)(2,1)S(1)}, bf16[1,1024]{1,0:T(2,128)(2,1)S(1)}, bf16[1,1024]{1,0:T(2,128)(2,1)S(...) all-reduce(bf16[1,1024]{1,0:T(2,128)(2,1)S(1)} %broadcast_in_dim.34, ...), channel_id=1, replica_groups=mesh['section'=2,'ctx'=8,'tp'=2] {'ctx'}, use_global_device_ids=true, to_apply=%region_33.34 | all-reduce | flops 9731 | bytes 38924 | tf_op jit(solution)/shard_map/psum | solution.py:378
  2591.6 72.8 %reduce-scatter.11.cloned.1.call-done = bf16[3,128,512]{2,1,0:T(8,128)(2,1)} async-done(((bf16[3,1024,512]{2,1,0:T(8,128)(2,1)}), bf16[3,128,512]{2,1,0:T(8,128)(2,1)}) %reduce-scatter.11.cloned.1.call-update) | async-done | bytes 393232 | tf_op jit(solution)/shard_map/reduce_scatter | solution.py:364
  2666.3 88.9 %reduce-scatter.17.cloned.1.call-done = bf16[128,2048]{1,0:T(8,128)(2,1)} async-done(((bf16[1024,2048]{1,0:T(8,128)(2,1)}), bf16[128,2048]{1,0:T(8,128)(2,1)}) %reduce-scatter.17.cloned.1.call-update) | async-done | bytes 524304
  2757.6 89.0 %reduce-scatter.13.cloned.1.call-done = bf16[128,2048]{1,0:T(8,128)(2,1)} async-done(((bf16[1024,2048]{1,0:T(8,128)(2,1)}), bf16[128,2048]{1,0:T(8,128)(2,1)}) %reduce-scatter.13.cloned.1.call-update) | async-done | bytes 524304 | tf_op jit(solution)/shard_map/reduce_scatter | solution.py:370
  (1271 shorter events, 1546.5 us)
Async XLA Ops:
  25.9 104.3 %all-gather.13.cloned.1.call-start = ((), (), s32[]{:S(2)}) async-start(), calls=%async_computation.10 | async-start | bytes 2359296 | tf_op jit(solution)/shard_map/while/body/eval_jaxpr/all_gather | solution.py:116
  27.8 137.0 %all-reduce.10.cloned.1.call-start = ((), (), s32[]{:S(2)}) async-start(), calls=%async_computation.12 | async-start | bytes 4194304 | tf_op jit(solution)/shard_map/while/body/eval_jaxpr/psum | solution.py:124
  195.7 103.3 %all-gather.13.cloned.1.call-start = ((), (), s32[]{:S(2)}) async-start(), calls=%async_computation.10 | async-start | bytes 2359296 | tf_op jit(solution)/shard_map/while/body/eval_jaxpr/all_gather | solution.py:116
  197.5 136.0 %all-reduce.10.cloned.1.call-start = ((), (), s32[]{:S(2)}) async-start(), calls=%async_computation.12 | async-start | bytes 4194304 | tf_op jit(solution)/shard_map/while/body/eval_jaxpr/psum | solution.py:124
  364.4 103.5 %all-gather.13.cloned.1.call-start = ((), (), s32[]{:S(2)}) async-start(), calls=%async_computation.10 | async-start | bytes 2359296 | tf_op jit(solution)/shard_map/while/body/eval_jaxpr/all_gather | solution.py:116
  366.3 136.1 %all-reduce.10.cloned.1.call-start = ((), (), s32[]{:S(2)}) async-start(), calls=%async_computation.12 | async-start | bytes 4194304 | tf_op jit(solution)/shard_map/while/body/eval_jaxpr/psum | solution.py:124
  533.3 103.5 %all-gather.13.cloned.1.call-start = ((), (), s32[]{:S(2)}) async-start(), calls=%async_computation.10 | async-start | bytes 2359296 | tf_op jit(solution)/shard_map/while/body/eval_jaxpr/all_gather | solution.py:116
  535.2 136.2 %all-reduce.10.cloned.1.call-start = ((), (), s32[]{:S(2)}) async-start(), calls=%async_computation.12 | async-start | bytes 4194304 | tf_op jit(solution)/shard_map/while/body/eval_jaxpr/psum | solution.py:124
  702.2 103.3 %all-gather.13.cloned.1.call-start = ((), (), s32[]{:S(2)}) async-start(), calls=%async_computation.10 | async-start | bytes 2359296 | tf_op jit(solution)/shard_map/while/body/eval_jaxpr/all_gather | solution.py:116
  704.1 136.0 %all-reduce.10.cloned.1.call-start = ((), (), s32[]{:S(2)}) async-start(), calls=%async_computation.12 | async-start | bytes 4194304 | tf_op jit(solution)/shard_map/while/body/eval_jaxpr/psum | solution.py:124
  891.7 102.5 %all-gather.19.cloned.1.call-start = ((), (), s32[]{:S(2)}) async-start(), calls=%async_computation.15 | async-start | bytes 2359296 | tf_op jit(solution)/shard_map/while/body/eval_jaxpr/all_gather | solution.py:150
  893.6 199.8 %reduce-scatter.21.cloned.1.call-start = ((), (), s32[]{:S(2)}) async-start(), calls=%async_computation.16 | async-start | bytes 2359296 | tf_op jit(solution)/shard_map/while/body/eval_jaxpr/reduce_scatter | solution.py:194
  1026.7 136.9 %reduce-scatter.19.cloned.1.call-start = ((), (), s32[]{:S(2)}) async-start(), calls=%async_computation.14 | async-start | bytes 2359296 | tf_op jit(solution)/shard_map/while/body/eval_jaxpr/reduce_scatter | solution.py:200
  1045.3 141.1 %all-reduce.12.cloned.1.call-start = ((), (), s32[]{:S(2)}) async-start(), calls=%async_computation.17 | async-start | bytes 2097152 | tf_op jit(solution)/shard_map/while/body/eval_jaxpr/psum | solution.py:221
  1219.4 101.2 %all-gather.19.cloned.1.call-start = ((), (), s32[]{:S(2)}) async-start(), calls=%async_computation.15 | async-start | bytes 2359296 | tf_op jit(solution)/shard_map/while/body/eval_jaxpr/all_gather | solution.py:150
  1221.2 198.5 %reduce-scatter.21.cloned.1.call-start = ((), (), s32[]{:S(2)}) async-start(), calls=%async_computation.16 | async-start | bytes 2359296 | tf_op jit(solution)/shard_map/while/body/eval_jaxpr/reduce_scatter | solution.py:194
  1353.0 136.8 %reduce-scatter.19.cloned.1.call-start = ((), (), s32[]{:S(2)}) async-start(), calls=%async_computation.14 | async-start | bytes 2359296 | tf_op jit(solution)/shard_map/while/body/eval_jaxpr/reduce_scatter | solution.py:200
  1371.5 144.3 %all-reduce.12.cloned.1.call-start = ((), (), s32[]{:S(2)}) async-start(), calls=%async_computation.17 | async-start | bytes 2097152 | tf_op jit(solution)/shard_map/while/body/eval_jaxpr/psum | solution.py:221
  1548.0 197.7 %reduce-scatter.21.cloned.1.call-start = ((), (), s32[]{:S(2)}) async-start(), calls=%async_computation.16 | async-start | bytes 2359296 | tf_op jit(solution)/shard_map/while/body/eval_jaxpr/reduce_scatter | solution.py:194
  1678.9 136.9 %reduce-scatter.19.cloned.1.call-start = ((), (), s32[]{:S(2)}) async-start(), calls=%async_computation.14 | async-start | bytes 2359296 | tf_op jit(solution)/shard_map/while/body/eval_jaxpr/reduce_scatter | solution.py:200
  1697.4 144.5 %all-reduce.12.cloned.1.call-start = ((), (), s32[]{:S(2)}) async-start(), calls=%async_computation.17 | async-start | bytes 2097152 | tf_op jit(solution)/shard_map/while/body/eval_jaxpr/psum | solution.py:221
  1872.2 100.5 %all-gather.19.cloned.1.call-start = ((), (), s32[]{:S(2)}) async-start(), calls=%async_computation.15 | async-start | bytes 2359296 | tf_op jit(solution)/shard_map/while/body/eval_jaxpr/all_gather | solution.py:150
  1874.1 197.8 %reduce-scatter.21.cloned.1.call-start = ((), (), s32[]{:S(2)}) async-start(), calls=%async_computation.16 | async-start | bytes 2359296 | tf_op jit(solution)/shard_map/while/body/eval_jaxpr/reduce_scatter | solution.py:194
  2005.2 136.9 %reduce-scatter.19.cloned.1.call-start = ((), (), s32[]{:S(2)}) async-start(), calls=%async_computation.14 | async-start | bytes 2359296 | tf_op jit(solution)/shard_map/while/body/eval_jaxpr/reduce_scatter | solution.py:200
  2023.7 144.5 %all-reduce.12.cloned.1.call-start = ((), (), s32[]{:S(2)}) async-start(), calls=%async_computation.17 | async-start | bytes 2097152 | tf_op jit(solution)/shard_map/while/body/eval_jaxpr/psum | solution.py:221
  2198.4 100.3 %all-gather.19.cloned.1.call-start = ((), (), s32[]{:S(2)}) async-start(), calls=%async_computation.15 | async-start | bytes 2359296 | tf_op jit(solution)/shard_map/while/body/eval_jaxpr/all_gather | solution.py:150
  2200.3 197.7 %reduce-scatter.21.cloned.1.call-start = ((), (), s32[]{:S(2)}) async-start(), calls=%async_computation.16 | async-start | bytes 2359296 | tf_op jit(solution)/shard_map/while/body/eval_jaxpr/reduce_scatter | solution.py:194
  2331.2 136.9 %reduce-scatter.19.cloned.1.call-start = ((), (), s32[]{:S(2)}) async-start(), calls=%async_computation.14 | async-start | bytes 2359296 | tf_op jit(solution)/shard_map/while/body/eval_jaxpr/reduce_scatter | solution.py:200
  2349.8 144.5 %all-reduce.12.cloned.1.call-start = ((), (), s32[]{:S(2)}) async-start(), calls=%async_computation.17 | async-start | bytes 2097152 | tf_op jit(solution)/shard_map/while/body/eval_jaxpr/psum | solution.py:221
  2522.0 142.4 %reduce-scatter.11.cloned.1.call-start = ((), (), s32[]{:S(2)}) async-start(), calls=%async_computation.6 | async-start | bytes 3538944 | tf_op jit(solution)/shard_map/reduce_scatter | solution.py:364
  2527.4 227.8 %reduce-scatter.17.cloned.1.call-start = ((), (), s32[]{:S(2)}) async-start(), calls=%async_computation.9 | async-start | bytes 4718592
  2540.2 306.4 %reduce-scatter.13.cloned.1.call-start = ((), (), s32[]{:S(2)}) async-start(), calls=%async_computation.7 | async-start | bytes 4718592 | tf_op jit(solution)/shard_map/reduce_scatter | solution.py:370
  (352 other events, 4545.3 us)
Sparse Core Ops, SparseCore 0:
  26.0 53.7 all-gather.14
  82.7 47.4 all-gather.12
  195.8 52.8 all-gather.14
  251.5 47.4 all-gather.12
  313.7 19.7 all-reduce.9
  364.5 52.8 all-gather.14
  420.4 47.4 all-gather.12
  533.4 52.8 all-gather.14
  589.3 47.4 all-gather.12
  651.5 19.7 all-reduce.9
  702.4 52.8 all-gather.14
  758.1 47.4 all-gather.12
  891.9 52.8 all-gather.16
  946.8 47.4 all-gather.18
  1026.9 66.5 reduce-scatter.20
  1097.0 66.6 reduce-scatter.18
  1219.5 51.4 all-gather.16
  1273.0 47.4 all-gather.18
  1353.1 66.5 reduce-scatter.20
  1423.1 66.6 reduce-scatter.18
  1546.2 50.6 all-gather.16
  1599.0 47.4 all-gather.18
  1679.1 66.6 reduce-scatter.20
  1749.2 66.5 reduce-scatter.18
  1872.3 50.6 all-gather.16
  1925.2 47.4 all-gather.18
  2005.3 66.5 reduce-scatter.20
  2075.4 66.6 reduce-scatter.18
  2198.5 50.6 all-gather.16
  2251.3 47.4 all-gather.18
  2331.4 66.6 reduce-scatter.20
  2401.4 66.6 reduce-scatter.18
  (8 shorter events, 152.0 us)
Sparse Core Ops, SparseCore 1:
  2523.3 63.3 reduce-scatter.14
  2590.6 73.7 reduce-scatter.10
  2668.3 86.8 reduce-scatter.16
  2758.9 87.6 reduce-scatter.12
where the time goes:
time: 2880 us; the launch traced here: 2860 us
  waiting for transfers between devices  1480 us (51%)
  matrix products  638 us (22%)
  other arithmetic  420 us (15%)
  local copies, waits for them, and re-layouts  208 us (7%)
  blocking collectives  37.2 us (1%)
  loops' own time  29.9 us (1%)
    reduce_scatter x5, waiting for transfers between devices, backward_step(): lax.psum_scatter(d_values.reshape(seq_count, key_count, local_width).asty...  327 us
    sub x10, other arithmetic, attend(): raised = jnp.exp(scores - row_top)  217 us
    all_gather x5, waiting for transfers between devices, backward_step(): lax.all_gather(key_rows, 'ctx', axis=1, tiled=True)  215 us
    all_gather x5, waiting for transfers between devices, forward_step(): lax.all_gather(key_rows, 'ctx', axis=1, tiled=True)  190 us
    reduce_scatter x5, waiting for transfers between devices, backward_step(): lax.psum_scatter(d_keys.reshape(seq_count, key_count, local_width).astype...  112 us
    psum x5, waiting for transfers between devices, forward_step(): attn_total, ffn_total = lax.psum((attn_part, ffn_part), 'tp')  99.6 us
    ppermute x10, waiting for transfers between devices, from_behind(): return lax.ppermute(shard, axis, pairs)  98.9 us
    dot_general x10, matrix products, attend(): jnp.einsum('bqhc,bkhc->bhqk', queries, key_heads, preferred_element_type=...  97.8 us
  transfers between devices with their start and end apart: 54, of which 49 were waited for; matrix products, arithmetic and copies ran while one was open for 29% of the time, Pallas kernels for 0%

commit v1 on v0

v1 whole, which is shorter than its diff:
```python
import functools

import jax
import jax.numpy as jnp
from jax import lax
from jax.experimental import pallas as pl
from jax.experimental.pallas import tpu as pltpu
from jax.sharding import PartitionSpec as P

HEAD = 64
ROT = 16
EPS = 1e-05
ROTARY_BASE = 10000.0
NEGATIVE = -1e30
STACK = 4
GROUP = STACK * HEAD
KEY_TILE = 512
VMEM_LIMIT = 56 * 1024 * 1024
BF16 = jnp.bfloat16
F32 = jnp.float32


def dot(a, b):
    return jnp.dot(a, b, preferred_element_type=F32)


def dot_nt(a, b):
    return lax.dot_general(a, b, (((1,), (1,)), ((), ())), preferred_element_type=F32)


def params_of(**more):
    return pltpu.CompilerParams(vmem_limit_bytes=VMEM_LIMIT, **more)


def whole(shape):
    return pl.BlockSpec(shape, lambda *_: (0,) * len(shape))


def rows_of(tile, *rest):
    return pl.BlockSpec((tile, *rest), lambda r, *_: (r,) + (0,) * len(rest))


def cost(flops, size):
    return pl.CostEstimate(flops=int(flops), bytes_accessed=int(size), transcendentals=0)


def normalize(values):
    middle = jnp.mean(values, axis=-1, keepdims=True)
    centered = values - middle
    spread = jnp.mean(centered * centered, axis=-1, keepdims=True)
    inverse = lax.rsqrt(spread + EPS)
    return centered * inverse, inverse


def turn(values, cosine, sine_up, sine_down):
    pieces = []
    for start in range(0, values.shape[1], 128):
        part = values[:, start : start + 128]
        ahead = pltpu.roll(part, 128 - ROT // 2, 1)
        behind = pltpu.roll(part, ROT // 2, 1)
        pieces.append(part * cosine + ahead * sine_up + behind * sine_down)
    return jnp.concatenate(pieces, axis=1)


def joint_kernel(with_queries, h_ref, gain_ref, shift_ref, w_ref, b_ref, cos_ref, up_ref, down_ref, n_ref, k_ref, v_ref, *maybe_q):
    scaled, _ = normalize(h_ref[...].astype(F32))
    low = (scaled * gain_ref[...] + shift_ref[...]).astype(BF16)
    n_ref[...] = low
    cosine, sine_up, sine_down = cos_ref[...], up_ref[...], down_ref[...]
    keys = dot(low, w_ref[1]) + b_ref[1:2]
    k_ref[...] = turn(keys, cosine, sine_up, sine_down).astype(BF16)
    v_ref[...] = (dot(low, w_ref[2]) + b_ref[2:3]).astype(BF16)
    if with_queries:
        queries = dot(low, w_ref[0]) + b_ref[0:1]
        queries = turn(queries, cosine, sine_up, sine_down)
        maybe_q[0][...] = queries.astype(BF16) * jnp.asarray(HEAD ** (-0.5), BF16)


def joint_call(h, gain, shift, w_joint, b_joint, table, with_queries):
    rows, width = h.shape
    local = w_joint.shape[2]
    tile = min(256, rows)
    count = 3 if with_queries else 2
    out = [jax.ShapeDtypeStruct((rows, width), BF16)] + [jax.ShapeDtypeStruct((rows, local), BF16)] * count
    return pl.pallas_call(
        functools.partial(joint_kernel, with_queries),
        grid=(rows // tile,),
        in_specs=[
            rows_of(tile, width),
            whole((1, width)),
            whole((1, width)),
            whole(w_joint.shape),
            whole(b_joint.shape),
            rows_of(tile, 128),
            rows_of(tile, 128),
            rows_of(tile, 128),
        ],
        out_specs=[rows_of(tile, width)] + [rows_of(tile, local)] * count,
        out_shape=out,
        compiler_params=params_of(),
        cost_estimate=cost(2 * rows * width * local * count, 4 * rows * width + 2 * w_joint.size),
        name="joint_projection",
    )(h, gain, shift, w_joint, b_joint, *table)


def gelu_parts(x):
    size = jnp.abs(x)
    t = 1.0 / (1.0 + (0.3275911 * 0.5**0.5) * size)
    bell = jnp.exp(-0.5 * x * x)
    poly = t * (0.5 * 0.254829592 + t * (-0.5 * 0.284496736 + t * (0.5 * 1.421413741 + t * (-0.5 * 1.453152027 + t * (0.5 * 1.061405429)))))
    tail = poly * bell
    return jnp.where(x < 0, tail, 1.0 - tail), bell


def ffn_kernel(save, h_ref, gain_ref, shift_ref, up_ref, b_ref, down_ref, part_ref, *saved):
    scaled, _ = normalize(h_ref[...].astype(F32))
    low = (scaled * gain_ref[...] + shift_ref[...]).astype(BF16)
    if save:
        saved[0][...] = low
    units = up_ref.shape[1]
    total = None
    for start in range(0, units, 512):
        cut = pl.ds(start, 512)
        hidden = dot(low, up_ref[:, cut]) + b_ref[:, cut]
        share, bell = gelu_parts(hidden)
        active = (hidden * share).astype(BF16)
        if save:
            saved[1][:, cut] = active
            saved[2][:, cut] = (share + hidden * bell * 0.3989422804014327).astype(BF16)
        term = dot(active, down_ref[cut, :])
        total = term if total is None else total + term
    part_ref[...] = total.astype(BF16)


def ffn_call(h, gain, shift, w_up, b_up, w_down, save):
    rows, width = h.shape
    units = w_up.shape[1]
    tile = min(256, rows)
    out = [jax.ShapeDtypeStruct((rows, width), BF16)]
    out_specs = [rows_of(tile, width)]
    if save:
        out += [jax.ShapeDtypeStruct((rows, width), BF16)] + [jax.ShapeDtypeStruct((rows, units), BF16)] * 2
        out_specs += [rows_of(tile, width), rows_of(tile, units), rows_of(tile, units)]
    return pl.pallas_call(
        functools.partial(ffn_kernel, save),
        grid=(rows // tile,),
        in_specs=[
            rows_of(tile, width),
            whole((1, width)),
            whole((1, width)),
            whole(w_up.shape),
            whole((1, units)),
            whole(w_down.shape),
        ],
        out_specs=out_specs,
        out_shape=out,
        compiler_params=params_of(),
        cost_estimate=cost(4 * rows * width * units, 4 * w_up.size + 4 * rows * width),
        name="feed_forward",
    )(h, gain, shift, w_up, b_up, w_down)


def ffn_back_kernel(g_ref, slope_ref, up_ref, down_ref, part_ref, hidden_ref, sums_ref):
    upstream = g_ref[...]
    units = up_ref.shape[1]

    @pl.when(pl.program_id(0) == 0)
    def _():
        sums_ref[...] = jnp.zeros_like(sums_ref)

    total = None
    for start in range(0, units, 512):
        cut = pl.ds(start, 512)
        d_active = dot_nt(upstream, down_ref[cut, :])
        d_hidden = (d_active * slope_ref[:, cut].astype(F32)).astype(BF16)
        hidden_ref[:, cut] = d_hidden
        sums_ref[:, cut] += jnp.sum(d_hidden.astype(F32), axis=0, keepdims=True)
        term = dot_nt(d_hidden, up_ref[:, cut])
        total = term if total is None else total + term
    part_ref[...] = total.astype(BF16)


def ffn_back_call(g, slope, w_up, w_down):
    rows, width = g.shape
    units = w_up.shape[1]
    tile = min(256, rows)
    return pl.pallas_call(
        ffn_back_kernel,
        grid=(rows // tile,),
        in_specs=[rows_of(tile, width), rows_of(tile, units), whole(w_up.shape), whole(w_down.shape)],
        out_specs=[rows_of(tile, width), rows_of(tile, units), whole((1, units))],
        out_shape=[
            jax.ShapeDtypeStruct((rows, width), BF16),
            jax.ShapeDtypeStruct((rows, units), BF16),
            jax.ShapeDtypeStruct((1, units), F32),
        ],
        compiler_params=params_of(),
        cost_estimate=cost(4 * rows * width * units, 4 * w_up.size + 4 * rows * (width + units)),
        name="feed_forward_back",
    )(g, slope, w_up, w_down)


def load_sorted(places_ref, parts, targets, sem, block):
    copies = []
    for refs, target in zip(parts, targets):
        index = 0
        for ref in refs:
            for local in range(ref.shape[0] // block):
                place = places_ref[index]
                copies.append(
                    pltpu.make_async_copy(
                        ref.at[pl.ds(local * block, block)],
                        target.at[pl.ds(pl.multiple_of(place * block, block), block)],
                        sem,
                    )
                )
                index += 1
    for copy in copies:
        copy.start()
    for copy in copies:
        copy.wait()


def transpose_into(source, target):
    rows, columns = source.shape

    def step(index, _):
        start = pl.multiple_of(index * 256, 256)
        for column in range(0, columns, 256):
            target[column : column + 256, pl.ds(start, 256)] = source[pl.ds(start, 256), column : column + 256].T
        return 0

    lax.fori_loop(0, rows // 256, step, 0)


def stacked(values):
    owner = lax.broadcasted_iota(jnp.int32, values.shape, 1) // HEAD
    zero = jnp.zeros_like(values)
    return jnp.concatenate([jnp.where(owner == a, values, zero) for a in range(STACK)], axis=0)


def unstacked(total, tile):
    picked = [total[a * HEAD : (a + 1) * HEAD, a * tile : (a + 1) * tile] for a in range(STACK)]
    return jnp.concatenate(picked, axis=0).T


def attend_kernel(
    block, remote, places_ref, limits_ref, q_ref, spots_ref, wo_ref, *refs
):
    key_refs, value_refs = refs[: 1 + remote], refs[1 + remote : 2 + 2 * remote]
    part_ref, mix_ref, lse_ref, keys, values, values_t, total, sem = refs[2 + 2 * remote :]
    step = pl.program_id(0)
    tile = q_ref.shape[0]
    groups = q_ref.shape[1] // GROUP

    @pl.when(step == 0)
    def _():
        load_sorted(places_ref, (key_refs, value_refs), (keys, values), sem, block)
        transpose_into(values, values_t)

    spots = spots_ref[0]
    lanes = [slice(g * GROUP, (g + 1) * GROUP) for g in range(groups)]
    heads = [stacked(q_ref[:, lane]) for lane in lanes]
    total[...] = jnp.zeros_like(total)

    def tile_step(masked, index, carry):
        start = pl.multiple_of(index * KEY_TILE, KEY_TILE)
        fresh = []
        for g, lane in enumerate(lanes):
            top, mass = carry[g]
            scores = dot_nt(keys[pl.ds(start, KEY_TILE), lane], heads[g])
            if masked:
                spot = start + lax.broadcasted_iota(jnp.int32, scores.shape, 0)
                scores = jnp.where(spot <= spots, scores, NEGATIVE)
            later = jnp.maximum(top, jnp.max(scores, axis=0, keepdims=True))
            shrink = jnp.exp(top - later)
            raised = jnp.exp(scores - later)
            mass = mass * shrink + jnp.sum(raised, axis=0, keepdims=True)
            total[lane, :] = total[lane, :] * shrink + dot(
                values_t[lane, pl.ds(start, KEY_TILE)], raised.astype(BF16)
            )
            fresh.append((later, mass))
        return tuple(fresh)

    first = jnp.full((1, STACK * tile), NEGATIVE, F32)
    carry = tuple((first, jnp.zeros_like(first)) for _ in lanes)
    carry = lax.fori_loop(0, limits_ref[step, 0], functools.partial(tile_step, False), carry)
    carry = lax.fori_loop(limits_ref[step, 0], limits_ref[step, 1], functools.partial(tile_step, True), carry)
    pieces = []
    for g, lane in enumerate(lanes):
        top, mass = carry[g]
        lse_ref[0, g : g + 1, :] = top + jnp.log(mass)
        pieces.append(unstacked(total[lane, :] * (1.0 / mass), tile))
    mixture = jnp.concatenate(pieces, axis=1).astype(BF16)
    mix_ref[...] = mixture
    part_ref[...] = dot(mixture, wo_ref[...]).astype(BF16)


def attend_call(queries, key_parts, value_parts, spots, places, limits, w_output, block):
    rows, local = queries.shape
    width = w_output.shape[1]
    tile = rows // limits.shape[0]
    length = sum(part.shape[0] for part in key_parts)
    groups = local // GROUP
    anywhere = pl.BlockSpec(memory_space=pl.ANY)
    return pl.pallas_call(
        functools.partial(attend_kernel, block, len(key_parts) - 1),
        grid_spec=pltpu.PrefetchScalarGridSpec(
            num_scalar_prefetch=2,
            grid=(rows // tile,),
            in_specs=[
                rows_of(tile, local),
                rows_of(1, 1, STACK * tile),
                whole(w_output.shape),
            ]
            + [anywhere] * (2 * len(key_parts)),
            out_specs=[rows_of(tile, width), rows_of(tile, local), rows_of(1, groups, STACK * tile)],
            scratch_shapes=[
                pltpu.VMEM((length, local), BF16),
                pltpu.VMEM((length, local), BF16),
                pltpu.VMEM((local, length), BF16),
                pltpu.VMEM((local, STACK * tile), F32),
                pltpu.SemaphoreType.DMA,
            ],
        ),
        out_shape=[
            jax.ShapeDtypeStruct((rows, width), BF16),
            jax.ShapeDtypeStruct((rows, local), BF16),
            jax.ShapeDtypeStruct((rows // tile, groups, STACK * tile), F32),
        ],
        compiler_params=params_of(),
        cost_estimate=cost(12 * rows * length * local, 2 * length * local * 4),
        name="attend",
    )(places, limits, queries, spots, w_output, *key_parts, *value_parts)


def attend_back_kernel(
    block, remote, places_ref, limits_ref, q_ref, g_ref, mix_ref, lse_ref, spots_ref, wo_ref,
    cos_ref, up_ref, down_ref, cos_all, up_all, down_all, *refs
):
    key_refs, value_refs = refs[: 1 + remote], refs[1 + remote : 2 + 2 * remote]
    dq_ref, dk_ref, dv_ref, sums_ref, keys, values, keys_t, d_keys, d_values, total, sem = refs[2 + 2 * remote :]
    step = pl.program_id(0)
    tile = q_ref.shape[0]
    groups = q_ref.shape[1] // GROUP

    @pl.when(step == 0)
    def _():
        load_sorted(places_ref, (key_refs, value_refs), (keys, values), sem, block)
        transpose_into(keys, keys_t)
        d_keys[...] = jnp.zeros_like(d_keys)
        d_values[...] = jnp.zeros_like(d_values)
        sums_ref[...] = jnp.zeros_like(sums_ref)

    spots = spots_ref[0]
    lanes = [slice(g * GROUP, (g + 1) * GROUP) for g in range(groups)]
    d_mixture = dot_nt(g_ref[...], wo_ref[...]).astype(BF16)
    product = d_mixture.astype(F32) * mix_ref[...].astype(F32)
    high = product.astype(BF16)
    rest = (product - high.astype(F32)).astype(BF16)
    picker = jnp.where(
        lax.broadcasted_iota(jnp.int32, (8, GROUP), 0) == lax.broadcasted_iota(jnp.int32, (8, GROUP), 1) // HEAD, 1.0, 0.0
    ).astype(BF16)
    heads, sides, inner, lse = [], [], [], []
    for g, lane in enumerate(lanes):
        heads.append(stacked(q_ref[:, lane]))
        sides.append(stacked(d_mixture[:, lane]))
        sums = dot_nt(picker, high[:, lane]) + dot_nt(picker, rest[:, lane])
        inner.append(jnp.concatenate([sums[a : a + 1] for a in range(STACK)], axis=1))
        lse.append(lse_ref[0, g : g + 1, :])
    total[...] = jnp.zeros_like(total)

    def tile_step(masked, index, carry):
        start = pl.multiple_of(index * KEY_TILE, KEY_TILE)
        cut = pl.ds(start, KEY_TILE)
        for g, lane in enumerate(lanes):
            scores = dot_nt(keys[cut, lane], heads[g])
            if masked:
                spot = start + lax.broadcasted_iota(jnp.int32, scores.shape, 0)
                scores = jnp.where(spot <= spots, scores, NEGATIVE)
            weights = jnp.exp(scores - lse[g])
            d_weights = dot_nt(values[cut, lane], sides[g])
            d_scores = (weights * (d_weights - inner[g])).astype(BF16)
            d_values[cut, lane] += dot(weights.astype(BF16), sides[g])
            d_keys[cut, lane] += dot(d_scores, heads[g])
            total[lane, :] += dot(keys_t[lane, cut], d_scores)
        return carry

    lax.fori_loop(0, limits_ref[step, 0], functools.partial(tile_step, False), 0)
    lax.fori_loop(limits_ref[step, 0], limits_ref[step, 1], functools.partial(tile_step, True), 0)
    pieces = [unstacked(total[lane, :], tile) for lane in lanes]
    d_queries = jnp.concatenate(pieces, axis=1) * HEAD ** (-0.5)
    d_queries = turn(d_queries, cos_ref[...], -up_ref[...], -down_ref[...]).astype(BF16)
    dq_ref[...] = d_queries
    sums_ref[0:1, :] += jnp.sum(d_queries.astype(F32), axis=0, keepdims=True)

    @pl.when(step == pl.num_programs(0) - 1)
    def _():
        for index in range(dk_ref.shape[0] // block):
            place = pl.ds(pl.multiple_of(places_ref[index] * block, block), block)
            rows = pl.ds(index * block, block)
            turned = turn(d_keys[place, :], cos_all[rows, :], -up_all[rows, :], -down_all[rows, :]).astype(BF16)
            dk_ref[rows, :] = turned
            low = d_values[place, :].astype(BF16)
            dv_ref[rows, :] = low
            sums_ref[1:2, :] += jnp.sum(turned.astype(F32), axis=0, keepdims=True)
            sums_ref[2:3, :] += jnp.sum(low.astype(F32), axis=0, keepdims=True)


def attend_back_call(queries, g, mixture, lse, key_parts, value_parts, spots, places, limits, w_output, table, block):
    rows, local = queries.shape
    width = w_output.shape[1]
    tile = rows // limits.shape[0]
    length = sum(part.shape[0] for part in key_parts)
    groups = local // GROUP
    anywhere = pl.BlockSpec(memory_space=pl.ANY)
    return pl.pallas_call(
        functools.partial(attend_back_kernel, block, len(key_parts) - 1),
        grid_spec=pltpu.PrefetchScalarGridSpec(
            num_scalar_prefetch=2,
            grid=(rows // tile,),
            in_specs=[
                rows_of(tile, local),
                rows_of(tile, width),
                rows_of(tile, local),
                rows_of(1, groups, STACK * tile),
                rows_of(1, 1, STACK * tile),
                whole(w_output.shape),
            ]
            + [rows_of(tile, 128)] * 3
            + [whole((length, 128))] * 3
            + [anywhere] * (2 * len(key_parts)),
            out_specs=[rows_of(tile, local), whole((length, local)), whole((length, local)), whole((8, local))],
            scratch_shapes=[
                pltpu.VMEM((length, local), BF16),
                pltpu.VMEM((length, local), BF16),
                pltpu.VMEM((local, length), BF16),
                pltpu.VMEM((length, local), F32),
                pltpu.VMEM((length, local), F32),
                pltpu.VMEM((local, STACK * tile), F32),
                pltpu.SemaphoreType.DMA,
            ],
        ),
        out_shape=[
            jax.ShapeDtypeStruct((rows, local), BF16),
            jax.ShapeDtypeStruct((length, local), BF16),
            jax.ShapeDtypeStruct((length, local), BF16),
            jax.ShapeDtypeStruct((8, local), F32),
        ],
        compiler_params=params_of(),
        cost_estimate=cost(24 * rows * length * local, 2 * length * local * 8),
        name="attend_back",
    )(
        places, limits, queries, g, mixture, lse, spots, w_output,
        *(part[:rows] for part in table), *table, *key_parts, *value_parts,
    )


def joint_back_kernel(count, *refs):
    w_ref, part_ref = refs[count], refs[count + 1]
    total = None
    for index in range(count):
        term = dot_nt(refs[index][...], w_ref[3 - count + index])
        total = term if total is None else total + term
    part_ref[...] = total.astype(BF16)


def joint_back_call(grads, offset, rows, w_joint):
    width, local = w_joint.shape[1:]
    tile = min(256, rows)
    first = offset // tile
    return pl.pallas_call(
        functools.partial(joint_back_kernel, len(grads)),
        grid=(rows // tile,),
        in_specs=[pl.BlockSpec((tile, local), lambda r: (first + r, 0))] * len(grads) + [whole(w_joint.shape)],
        out_specs=rows_of(tile, width),
        out_shape=jax.ShapeDtypeStruct((rows, width), BF16),
        compiler_params=params_of(),
        cost_estimate=cost(2 * rows * width * local * len(grads), 2 * rows * (width + 3 * local) + 2 * w_joint.size),
        name="joint_projection_back",
    )(*grads, w_joint)


def norm_back_kernel(h_ref, g_ref, first_ref, second_ref, gains_ref, out_ref, sums_ref):
    @pl.when(pl.program_id(0) == 0)
    def _():
        sums_ref[...] = jnp.zeros_like(sums_ref)

    scaled, inverse = normalize(h_ref[...].astype(F32))
    upstream = g_ref[...].astype(F32)
    d_first = first_ref[0].astype(F32)
    for index in range(1, first_ref.shape[0]):
        d_first += first_ref[index].astype(F32)
    d_second = second_ref[0].astype(F32) + second_ref[1].astype(F32)
    for row, term in enumerate((d_first * scaled, d_first, d_second * scaled, d_second, upstream)):
        sums_ref[row : row + 1, :] += jnp.sum(term, axis=0, keepdims=True)
    d_scaled = d_first * gains_ref[0:1] + d_second * gains_ref[1:2]
    middle = jnp.mean(d_scaled, axis=-1, keepdims=True)
    along = jnp.mean(d_scaled * scaled, axis=-1, keepdims=True)
    out_ref[...] = (upstream + inverse * (d_scaled - middle - scaled * along)).astype(BF16)


def norm_back_call(h, g, firsts, seconds, gains):
    rows, width = h.shape
    tile = min(128, rows)

    def piled(count):
        return pl.BlockSpec((count, tile, width), lambda r: (0, r, 0))

    return pl.pallas_call(
        norm_back_kernel,
        grid=(rows // tile,),
        in_specs=[rows_of(tile, width), rows_of(tile, width), piled(firsts.shape[0]), piled(2), whole(gains.shape)],
        out_specs=[rows_of(tile, width), whole((8, width))],
        out_shape=[jax.ShapeDtypeStruct((rows, width), BF16), jax.ShapeDtypeStruct((8, width), F32)],
        compiler_params=params_of(),
        cost_estimate=cost(20 * rows * width, 2 * rows * width * 8),
        name="norm_back",
    )(h, g, firsts, seconds, gains)


def swap_core(shard):
    return lax.ppermute(shard, "tp", [(0, 1), (1, 0)])


def swap_ctx(shard, mask):
    return lax.ppermute(shard, "ctx", [(c, c ^ mask) for c in range(lax.axis_size("ctx"))])


def next_section(shard, by):
    size = lax.axis_size("section")
    return lax.ppermute(shard, "section", [(s, s + by) for s in range(size) if 0 <= s + by < size])


def reduce_ctx(pieces, masks):
    for mask in masks:
        half = pieces.shape[0] // 2
        arrived = swap_ctx(pieces[half:], mask)
        total = pieces[:half].astype(F32) + arrived.astype(F32)
        pieces = total.astype(BF16)
    return total[0]


def mask_order(masks):
    order = [0]
    for mask in reversed(masks):
        order = order + [value ^ mask for value in order]
    return order


def by_owner(values, masks, rank):
    share = values.shape[1] // (1 << len(masks))
    parts = [lax.dynamic_slice_in_dim(values, (rank ^ m) * share, share, 1) for m in mask_order(masks)]
    return jnp.concatenate(parts, axis=1)


def tn(a, b):
    return lax.dot_general(a, b, (((0,), (0,)), ((), ())), preferred_element_type=F32)


def on_device(
    tokens,
    cotangent,
    block_order,
    first_gain,
    first_bias,
    second_gain,
    second_bias,
    joint_weight,
    joint_bias,
    output_weight,
    output_bias,
    up_weight,
    up_bias,
    down_weight,
    down_bias,
):
    section = lax.axis_index("section")
    sections = lax.axis_size("section")
    ctx = lax.axis_index("ctx")
    ctx_size = lax.axis_size("ctx")
    core = lax.axis_index("tp")
    seqs, local_len, width = tokens.shape
    block = local_len // 2
    chips = ctx_size // seqs
    seq, member = ctx // chips, ctx % chips
    rows = seqs * block
    chip_rows = 2 * rows
    length = chips * chip_rows
    seq_masks = [chips << b for b in range((seqs - 1).bit_length())]
    member_masks = [1 << b for b in range((chips - 1).bit_length())]

    k, u, a = jnp.meshgrid(jnp.arange(chips), jnp.arange(2), jnp.arange(seqs), indexing="ij")
    stored = (2 * ((seq ^ a) * chips + (member ^ k)) + (core ^ u)).reshape(-1)
    places = block_order[stored]
    spots = (places[:, None] * block + jnp.arange(block, dtype=jnp.int32)).reshape(-1)
    exponent = jnp.arange(ROT // 2, dtype=F32) * (2.0 / ROT)
    inverse = jnp.power(jnp.float32(ROTARY_BASE), -exponent)
    turns = spots.astype(F32)[:, None] * inverse[None, :]
    cosine, sine = jnp.cos(turns), jnp.sin(turns)
    half = ROT // 2
    blank = jnp.zeros((length, HEAD - ROT), F32)
    none = jnp.zeros((length, half), F32)
    table = (
        jnp.tile(jnp.concatenate([cosine, cosine, blank + 1.0], 1), (1, 128 // HEAD)),
        jnp.tile(jnp.concatenate([-sine, none, blank], 1), (1, 128 // HEAD)),
        jnp.tile(jnp.concatenate([none, sine, blank], 1), (1, 128 // HEAD)),
    )
    near = tuple(part[:chip_rows] for part in table)
    far = tuple(part[chip_rows:] for part in table)

    tile = max(block, 128)
    per_tile = tile // block
    tile_places = places[: chip_rows // block].reshape(-1, per_tile)
    lowest, highest = jnp.min(tile_places, 1), jnp.max(tile_places, 1)
    limits = jnp.stack([(lowest * block + 1) // KEY_TILE, (highest * block + block - 1) // KEY_TILE + 1], 1)
    spot_rows = jnp.tile(spots[:chip_rows].reshape(-1, 1, tile), (1, 1, STACK))

    gain_one, shift_one, gain_two, shift_two = first_gain, first_bias, second_gain, second_bias
    w_joint, b_joint = joint_weight[0], joint_bias[0]
    w_output, b_output = output_weight[0], output_bias
    w_up, b_up = up_weight[0], up_bias
    w_down, b_down = down_weight[0], down_bias
    gains = jnp.concatenate([gain_one, gain_two], 0)

    def to_planes(values):
        mine = lax.dynamic_slice_in_dim(values, core * block, block, 1)
        parts = []
        for shift in range(seqs):
            part = lax.dynamic_index_in_dim(mine, seq ^ shift, 0, keepdims=False)
            parts.append(part if shift == 0 else swap_ctx(part, shift * chips))
        return jnp.concatenate(parts, axis=0)

    def from_planes(values):
        parts = values.reshape(seqs, block, width)
        parts = jnp.stack([parts[s] if s == 0 else swap_ctx(parts[s], s * chips) for s in range(seqs)])
        both = jnp.stack([parts, swap_core(parts)], 1)
        ordered = [
            lax.dynamic_index_in_dim(lax.dynamic_index_in_dim(both, s ^ seq, 0, False), v ^ core, 0, False)
            for s in range(seqs)
            for v in range(2)
        ]
        return jnp.stack(ordered).reshape(1, seqs, local_len, width)

    def forward(own, save):
        others = [swap_ctx(own, k) for k in range(1, chips)]
        chip = jnp.concatenate([own, swap_core(own)], 0)
        outs = joint_call(chip, gain_one, shift_one, w_joint, b_joint, near, True)
        normal, keys, values, queries = outs
        ffn_part, *kept_ffn = ffn_call(chip, gain_two, shift_two, w_up, b_up, w_down, save)
        key_parts, value_parts, normal_parts = [keys], [values], [normal]
        if chips > 1:
            rest = jnp.concatenate([x for other in others for x in (other, swap_core(other))], 0)
            far_normal, far_keys, far_values = joint_call(rest, gain_one, shift_one, w_joint, b_joint, far, False)
            key_parts.append(far_keys)
            value_parts.append(far_values)
            normal_parts.append(far_normal)
        attn_part, mixture, lse = attend_call(
            queries, key_parts, value_parts, spot_rows, places, limits, w_output, block
        )
        attention = attn_part[:rows].astype(F32) + swap_core(attn_part[rows:]).astype(F32) + b_output
        feedforward = ffn_part[:rows].astype(F32) + swap_core(ffn_part[rows:]).astype(F32) + b_down
        state = own.astype(F32)
        result = (state + attention + feedforward).astype(BF16)
        if not save:
            return result
        moments = jnp.stack(
            [jnp.sum(state * state), jnp.sum(attention * attention), jnp.sum(feedforward * feedforward)]
        )
        return result, moments, (normal_parts, queries, key_parts, value_parts, mixture, lse, *kept_ffn)

    def backward(own, g_own, kept):
        normal_parts, queries, key_parts, value_parts, mixture, lse, second_in, active, slope = kept
        g = jnp.concatenate([g_own, swap_core(g_own)], 0)
        d_queries, d_keys, d_values, joint_sums = attend_back_call(
            queries, g, mixture, lse, key_parts, value_parts, spot_rows, places, limits, w_output, table, block
        )
        near_part = joint_back_call([d_queries, d_keys, d_values], 0, chip_rows, w_joint)
        firsts = [near_part[:rows], swap_core(near_part[rows:])]
        if chips > 1:
            far_part = joint_back_call([d_keys, d_values], chip_rows, length - chip_rows, w_joint)
            far_part = far_part.reshape(chips - 1, 2, rows, width)
            far_sum = (far_part[:, 0].astype(F32) + swap_core(far_part[:, 1]).astype(F32)).astype(BF16)
            firsts += [swap_ctx(far_sum[k - 1], k) for k in range(1, chips)]
        second_part, d_hidden, up_sums = ffn_back_call(g, slope, w_up, w_down)
        seconds = [second_part[:rows], swap_core(second_part[rows:])]
        d_own, norm_sums = norm_back_call(own, g_own, jnp.stack(firsts), jnp.stack(seconds), gains)
        return d_own, norm_sums, (g, d_queries, d_keys, d_values, joint_sums, d_hidden, up_sums)

    token_rows = to_planes(tokens)
    g_rows = to_planes(cotangent)
    own = token_rows
    for tick in range(sections):
        last = tick == sections - 1
        if not last:
            result = forward(own, False)
            own = jnp.where(section == 0, token_rows, next_section(result, 1))
        else:
            result, moments, kept = forward(own, True)
    section_out = from_planes(result)
    g_own = g_rows
    for tick in range(sections):
        d_own, norm_sums, grads = backward(own, g_own, kept)
        if tick < sections - 1:
            g_own = jnp.where(section == sections - 1, g_rows, next_section(d_own, -1))
    section_in_grad = from_planes(d_own)

    normal_parts, queries, key_parts, value_parts, mixture, lse, second_in, active, slope = kept
    g, d_queries, d_keys, d_values, joint_sums, d_hidden, up_sums = grads
    late = member_masks + seq_masks
    early = seq_masks + member_masks
    local = w_output.shape[0]
    units = w_up.shape[1]

    g_late = by_owner(g, late, ctx)
    down_pieces = tn(g_late, active).astype(BF16).reshape(ctx_size, -1, units)
    down_total = reduce_ctx(down_pieces, late).T
    output_pieces = tn(g_late, mixture).astype(BF16).reshape(ctx_size, -1, local)
    output_total = reduce_ctx(output_pieces, late).T
    up_pieces = tn(by_owner(second_in, early, ctx), d_hidden).astype(BF16).reshape(ctx_size, -1, units)
    up_total = reduce_ctx(up_pieces, early)
    near_normal = by_owner(normal_parts[0], late, ctx)
    query_pieces = tn(near_normal, d_queries)
    key_pieces = tn(near_normal, d_keys[:chip_rows])
    value_pieces = tn(near_normal, d_values[:chip_rows])
    if chips > 1:
        far_normal = by_owner(normal_parts[1], late, ctx)
        key_pieces += tn(far_normal, d_keys[chip_rows:])
        value_pieces += tn(far_normal, d_values[chip_rows:])
    joint_pieces = jnp.stack([query_pieces, key_pieces, value_pieces]).astype(BF16)
    joint_pieces = joint_pieces.reshape(3, ctx_size, -1, local).transpose(1, 0, 2, 3)
    joint_total = reduce_ctx(joint_pieces, late)

    both = jnp.concatenate([norm_sums[:5].reshape(-1), moments])
    both = both + swap_core(both)
    small = jnp.concatenate([both, joint_sums[:3].reshape(-1), up_sums.reshape(-1)])
    for mask in late:
        small = small + swap_ctx(small, mask)
    norm_total = small[: 5 * width].reshape(5, 1, width)
    moment_total = small[5 * width : 5 * width + 3]
    joint_shift = small[5 * width + 3 : 5 * width + 3 + 3 * local].reshape(1, 3, local)
    up_shift = small[5 * width + 3 + 3 * local :].reshape(1, units)
    root_means = jnp.sqrt(moment_total / (length * seqs * width))
    return (
        section_out,
        section_in_grad,
        norm_total[0],
        norm_total[1],
        norm_total[2],
        norm_total[3],
        joint_total[None],
        joint_shift,
        output_total[None],
        norm_total[4],
        up_total[None],
        up_shift,
        down_total[None],
        norm_total[4],
        root_means[None],
    )


def solution(mesh):
    in_specs = (
        P(None, "ctx", None),
        P(None, "ctx", None),
        P(),
        P("section", None),
        P("section", None),
        P("section", None),
        P("section", None),
        P("section", None, None, "tp"),
        P("section", None, "tp"),
        P("section", "tp", None),
        P("section", None),
        P("section", None, "tp"),
        P("section", "tp"),
        P("section", "tp", None),
        P("section", None),
    )
    out_specs = (
        P("section", None, "ctx", None),
        P("section", None, "ctx", None),
        P("section", None),
        P("section", None),
        P("section", None),
        P("section", None),
        P("section", None, "ctx", "tp"),
        P("section", None, "tp"),
        P("section", "tp", "ctx"),
        P("section", None),
        P("section", "ctx", "tp"),
        P("section", "tp"),
        P("section", "tp", "ctx"),
        P("section", None),
        P("section", None),
    )
    return jax.shard_map(
        on_device, mesh=mesh, in_specs=in_specs, out_specs=out_specs, check_vma=False
    )
```

time: 2880 us -> 847 us (0.29)
  waiting for transfers between devices: 1480 us -> 252 us
  matrix products: 638 us -> 31.3 us
  other arithmetic: 420 us -> 61.3 us
  Pallas kernels: 0 us -> 335 us
  local copies, waits for them, and re-layouts: 208 us -> 107 us
  blocking collectives: 37.2 us -> 0 us
  loops' own time: 29.9 us -> 0 us
    dot_general x105 -> x8, matrix products: 638 us -> 31.3 us  [tn(): lax.dot_general(a, b, (((0,), (0,)), ((), ())), preferred_element_type=F32)]
    reduce_scatter x12 -> x0, waiting for transfers between devices: 601 us -> none  [the longest x5 327 us: backward_step(): lax.psum_scatter(d_values.reshape(seq_count, key_count, local_width).asty...]
    all_gather x20 -> x0, waiting for transfers between devices: 591 us -> none  [the longest x5 215 us: backward_step(): lax.all_gather(key_rows, 'ctx', axis=1, tiled=True)]
    pallas_call x0 -> x18, Pallas kernels: none -> 335 us  [the longest x2 109 us: attend_back_call(): pl.pallas_call(functools.partial(attend_back_kernel, block, len(key_parts...]
    sub x15 -> x0, other arithmetic: 217 us -> none  [the longest x10 217 us: attend(): raised = jnp.exp(scores - row_top)]
    ppermute x10 -> x52, waiting for transfers between devices: 98.9 us -> 252 us  [the longest x31 248 us: swap_ctx(): lax.ppermute(shard, 'ctx', [(c, c ^ mask) for c in range(lax.axis_size('c...]
    psum x10 -> x0, waiting for transfers between devices: 100 us -> none  [the longest x5 99.6 us: forward_step(): attn_total, ffn_total = lax.psum((attn_part, ffn_part), 'tp')]
    unnamed x6 -> x0, waiting for transfers between devices: 88.9 us -> none
  transfers between devices with their start and end apart: 54 -> 52, of which waited for: 49 -> 22; matrix products, arithmetic and copies ran while one was open for 29% -> 21% of each run, Pallas kernels for 0% -> 30%
where the time goes in v1:
time: 847 us; the launch traced here: 839 us
  Pallas kernels  335 us (40%)
  waiting for transfers between devices  252 us (30%)
  local copies, waits for them, and re-layouts  107 us (13%)
  other arithmetic  61.3 us (7%)
  starting transfers between devices  49.6 us (6%)
  matrix products  31.3 us (4%)
    ppermute x31, waiting for transfers between devices, swap_ctx(): lax.ppermute(shard, 'ctx', [(c, c ^ mask) for c in range(lax.axis_size('c...  248 us
    pallas_call x2, Pallas kernels, attend_back_call(): pl.pallas_call(functools.partial(attend_back_kernel, block, len(key_parts...  109 us
    pallas_call x2, Pallas kernels, attend_call(): pl.pallas_call(functools.partial(attend_kernel, block, len(key_parts) - 1...  78.2 us
    pallas_call x2, Pallas kernels, ffn_call(): pl.pallas_call(functools.partial(ffn_kernel, save), grid=(rows // tile,),...  41.2 us
    ppermute x31, starting transfers between devices, swap_ctx(): lax.ppermute(shard, 'ctx', [(c, c ^ mask) for c in range(lax.axis_size('c...  39.7 us
    pallas_call x4, Pallas kernels, joint_call(): pl.pallas_call(functools.partial(joint_kernel, with_queries), grid=(rows...  34.2 us
    pallas_call x2, Pallas kernels, ffn_back_call(): pl.pallas_call(ffn_back_kernel, grid=(rows // tile,), in_specs=[rows_of(t...  31.5 us
    dot_general x8, matrix products, tn(): lax.dot_general(a, b, (((0,), (0,)), ((), ())), preferred_element_type=F32)  31.3 us
  transfers between devices with their start and end apart: 52, of which 22 were waited for; matrix products, arithmetic and copies ran while one was open for 21% of the time, Pallas kernels for 30%

profile of v1, /device:TPU:0, one launch (start us, length us, event | category | flops | bytes accessed | tf_op | source)
XLA Modules:
  0.0 838.8 jit_solution(11006522532368051114)
XLA Ops:
  16.3 10.2 %collective-permute-done.1 = bf16[128,1024]{1,0:T(8,128)(2,1)S(1)} collective-permute-done((bf16[128,1024]{1,0:T(8,128)(2,1)S(1)}, bf16[128,1024]{1,0:T(8,128)(2,1)S(1)}, u32[]{:S(2)}, u32[]{:S(2)}) %collective-permute-start.1) | collective-permute-done | bytes 262176 | tf_op jit(solution)/shard_map/ppermute | solution.py:527
  40.1 13.3 %collective-permute-done.4 = bf16[512,1024]{1,0:T(8,128)(2,1)} collective-permute-done((bf16[512,1024]{1,0:T(8,128)(2,1)}, bf16[512,1024]{1,0:T(8,128)(2,1)}, u32[]{:S(2)}, u32[]{:S(2)}) %collective-permute-start.4) | collective-permute-done | bytes 1048608 | tf_op jit(solution)/shard_map/ppermute | solution.py:527
  55.7 19.8 %feed_forward.2 = bf16[1024,1024]{1,0:T(8,128)(2,1)} custom-call(bf16[1024,1024]{1,0:T(8,128)(2,1)} %constant_dynamic-update-slice_fusion.h_ref, f32[1,1024]{1,0:T(1,128)} %gain_ref.11, f32[1,1024]{1,0:T(1,128)} %shift_ref.11, bf16[1024,2048]{1,0:T(8,128)(2,1)} %bitcast.259, f32[1,2048]{1,0:T(1,128)} %b_ref.3, bf16[2048,1024]{1,0:T(8,128)(2,1)} %bitcast.263), custom_call_target="tpu_custom_call" | custom-call | flops 8589934592 | bytes 12582912 | tf_op jit(solution)/shard_map/feed_forward/pallas_call | solution.py:144
  77.4 9.5 %joint_projection.4 = (bf16[1024,1024]{1,0:T(8,128)(2,1)}, bf16[1024,512]{1,0:T(8,128)(2,1)}, bf16[1024,512]{1,0:T(8,128)(2,1)}, bf16[1024,512]{1,0:T(8,128)(2,1)}) custom-call(bf16[1024,1024]{1,0:T(8,128)(2,1)} %constant_dynamic-update-slice_fusion.h_ref, f32[1,1024]{1,0:T(1,128)} %gain_ref.10, f32[1,1024]{1,0:T(1,128)} %shift_ref.10, ...), custom_call_target="tpu_custom_call" | custom-call | flops 3221225472 | bytes 7340032 | tf_op jit(solution)/shard_map/joint_projection/pallas_call | solution.py:85
  89.8 7.5 joint_projection.5
  97.9 39.2 %attend.2 = (bf16[1024,1024]{1,0:T(8,128)(2,1)}, bf16[1024,512]{1,0:T(8,128)(2,1)}, f32[8,2,512]{2,1,0:T(2,128)}) custom-call(s32[16]{0:T(128)} %copy-done.58, s32[8,2]{1,0:T(8,128)} %copy.78.limits_ref, bf16[1024,512]{1,0:T(8,128)(2,1)} %get-tuple-element.49.q_ref, s32[8,1,512]{2,1,0:T(1,128)} %bitcast.239, bf16[512,1024]{1,0:T(8,128)(2,1)} %bitcast.267, ...), custom_call_target="tpu_custom_call" | custom-call | flops 12884901888 | bytes 8388608 | tf_op jit(solution)/shard_map/attend/pallas_call | solution.py:306
  162.7 15.7 %collective-permute-done.19 = bf16[128,1024]{1,0:T(8,128)(2,1)S(1)} collective-permute-done((bf16[128,1024]{1,0:T(8,128)(2,1)}, bf16[128,1024]{1,0:T(8,128)(2,1)S(1)}, u32[]{:S(2)}, u32[]{:S(2)}) %collective-permute-start.19) | collective-permute-done | bytes 262176 | tf_op jit(solution)/shard_map/ppermute | solution.py:527
  198.0 21.4 %feed_forward.3 = (bf16[1024,1024]{1,0:T(8,128)(2,1)}, bf16[1024,1024]{1,0:T(8,128)(2,1)}, bf16[1024,2048]{1,0:T(8,128)(2,1)}, bf16[1024,2048]{1,0:T(8,128)(2,1)}) custom-call(bf16[1024,1024]{1,0:T(8,128)(2,1)} %pad_maximum_fusion.4.h_ref, f32[1,1024]{1,0:T(1,128)} %gain_ref.11, f32[1,1024]{1,0:T(1,128)} %shift_ref.11, bf16[1024,2048]{1,0:T(8,128)(2,1)} %bitcast.260, ...), custom_call_target="tpu_custom_call" | custom-call | flops 8589934592 | bytes 12582912 | tf_op jit(solution)/shard_map/feed_forward/pallas_call | solution.py:144
  221.8 15.7 %feed_forward_back.2 = (bf16[1024,1024]{1,0:T(8,128)(2,1)}, bf16[1024,2048]{1,0:T(8,128)(2,1)}, f32[1,2048]{1,0:T(1,128)}) custom-call(bf16[1024,1024]{1,0:T(8,128)(2,1)} %constant_dynamic-update-slice_fusion.5.g_ref, bf16[1024,2048]{1,0:T(8,128)(2,1)} %get-tuple-element.67.slope_ref, bf16[1024,2048]{1,0:T(8,128)(2,1)} %bitcast.261, bf16[2048,1024]{1,0:T(8,128)(2,1)} %bitcast.265), custom_call_target="tpu_custom_call" | custom-call | flops 8589934592 | bytes 20971520 | tf_op jit(solution)/shard_map/feed_forward_back/pallas_call | solution.py:187
  240.9 9.6 %joint_projection.6 = (bf16[1024,1024]{1,0:T(8,128)(2,1)}, bf16[1024,512]{1,0:T(8,128)(2,1)}, bf16[1024,512]{1,0:T(8,128)(2,1)}, bf16[1024,512]{1,0:T(8,128)(2,1)}) custom-call(bf16[1024,1024]{1,0:T(8,128)(2,1)} %pad_maximum_fusion.4.h_ref, f32[1,1024]{1,0:T(1,128)} %gain_ref.10, f32[1,1024]{1,0:T(1,128)} %shift_ref.10, bf16[3,1024,512]{2,1,0:T(8,128)(2,1)} %bitcast.204, ...), custom_call_target="tpu_custom_call" | custom-call | flops 3221225472 | bytes 7340032 | tf_op jit(solution)/shard_map/joint_projection/pallas_call | solution.py:85
  261.0 7.5 joint_projection.7
  268.5 39.0 %attend.3 = (bf16[1024,1024]{1,0:T(8,128)(2,1)}, bf16[1024,512]{1,0:T(8,128)(2,1)}, f32[8,2,512]{2,1,0:T(2,128)}) custom-call(s32[16]{0:T(128)} %copy-done.58, s32[8,2]{1,0:T(8,128)} %copy.78.limits_ref, bf16[1024,512]{1,0:T(8,128)(2,1)} %get-tuple-element.55.q_ref, s32[8,1,512]{2,1,0:T(1,128)} %bitcast.240, bf16[512,1024]{1,0:T(8,128)(2,1)} %bitcast.268, ...), custom_call_target="tpu_custom_call" | custom-call | flops 12884901888 | bytes 8388608 | tf_op jit(solution)/shard_map/attend/pallas_call | solution.py:306
  307.5 54.6 %attend_back.2 = (bf16[1024,512]{1,0:T(8,128)(2,1)}, bf16[2048,512]{1,0:T(8,128)(2,1)}, bf16[2048,512]{1,0:T(8,128)(2,1)}, f32[8,512]{1,0:T(8,128)}) custom-call(s32[16]{0:T(128)} %copy-done.58, s32[8,2]{1,0:T(8,128)} %copy.78.limits_ref, bf16[1024,512]{1,0:T(8,128)(2,1)} %get-tuple-element.55.q_ref, ...), custom_call_target="tpu_custom_call" | custom-call | flops 25769803776 | bytes 16777216 | tf_op jit(solution)/shard_map/attend_back/pallas_call | solution.py:417
  362.1 6.5 joint_projection_back.5
  375.7 7.5 joint_projection_back.4
  396.6 15.9 %collective-permute-done.24 = bf16[512,1024]{1,0:T(8,128)(2,1)S(1)} collective-permute-done((bf16[512,1024]{1,0:T(8,128)(2,1)S(1)}, bf16[512,1024]{1,0:T(8,128)(2,1)S(1)}, u32[]{:S(2)}, u32[]{:S(2)}) %collective-permute-start.24) | collective-permute-done | bytes 1048608 | tf_op jit(solution)/shard_map/ppermute | solution.py:527
  414.6 6.0 norm_back.2
  433.3 12.6 %collective-permute-done.15 = bf16[128,1024]{1,0:T(8,128)(2,1)S(1)} collective-permute-done((bf16[128,1024]{1,0:T(8,128)(2,1)S(1)}, bf16[128,1024]{1,0:T(8,128)(2,1)S(1)}, u32[]{:S(2)}, u32[]{:S(2)}) %collective-permute-start.15) | collective-permute-done | bytes 262176 | tf_op jit(solution)/shard_map/ppermute | solution.py:527
  452.3 54.7 %attend_back.3 = (bf16[1024,512]{1,0:T(8,128)(2,1)}, bf16[2048,512]{1,0:T(8,128)(2,1)}, bf16[2048,512]{1,0:T(8,128)(2,1)}, f32[8,512]{1,0:T(8,128)}) custom-call(s32[16]{0:T(128)} %copy-done.58, s32[8,2]{1,0:T(8,128)} %copy.78.limits_ref, bf16[1024,512]{1,0:T(8,128)(2,1)} %get-tuple-element.55.q_ref, bf16[1024,1024]{1,0:T(8,128)(2,1)} %pad_maximum_fusion.g_ref, ...), custom_call_target="tpu_custom_call" | custom-call | flops 25769803776 | bytes 16777216 | tf_op jit(solution)/shard_map/attend_back/pallas_call | solution.py:417
  507.1 15.8 %feed_forward_back.3 = (bf16[1024,1024]{1,0:T(8,128)(2,1)}, bf16[1024,2048]{1,0:T(8,128)(2,1)}, f32[1,2048]{1,0:T(1,128)}) custom-call(bf16[1024,1024]{1,0:T(8,128)(2,1)} %pad_maximum_fusion.g_ref, bf16[1024,2048]{1,0:T(8,128)(2,1)} %get-tuple-element.67.slope_ref, bf16[1024,2048]{1,0:T(8,128)(2,1)} %bitcast.262, bf16[2048,1024]{1,0:T(8,128)(2,1)} %bitcast.266), custom_call_target="tpu_custom_call" | custom-call | flops 8589934592 | bytes 20971520 | tf_op jit(solution)/shard_map/feed_forward_back/pallas_call | solution.py:187
  522.9 6.5 joint_projection_back.7
  537.7 7.7 joint_projection_back.6
  571.1 7.5 convolution_convert_fusion
  578.7 6.4 convolution_convert_fusion.1
  585.1 24.5 %collective-permute-done.43 = bf16[4,128,512]{1,2,0:T(8,128)(2,1)S(1)} collective-permute-done((bf16[4,128,512]{1,2,0:T(8,128)(2,1)}, bf16[4,128,512]{1,2,0:T(8,128)(2,1)S(1)}, u32[]{:S(2)}, u32[]{:S(2)}) %collective-permute-start.43) | collective-permute-done | bytes 524320 | tf_op jit(solution)/shard_map/ppermute | solution.py:527
  628.3 4.8 fusion.54
  643.5 44.2 %collective-permute-done.30 = bf16[512,1024]{1,0:T(8,128)(2,1)} collective-permute-done((bf16[512,1024]{1,0:T(8,128)(2,1)S(1)}, bf16[512,1024]{1,0:T(8,128)(2,1)}, u32[]{:S(2)}, u32[]{:S(2)}) %collective-permute-start.30) | collective-permute-done | bytes 1048608 | tf_op jit(solution)/shard_map/ppermute | solution.py:527
  691.2 6.4 norm_back.3
  715.4 20.3 %collective-permute-done.38 = f32[8707]{0:T(1024)S(1)} collective-permute-done((f32[8707]{0:T(1024)S(1)}, f32[8707]{0:T(1024)S(1)}, u32[]{:S(2)}, u32[]{:S(2)}) %collective-permute-start.38) | collective-permute-done | bytes 34860 | tf_op jit(solution)/shard_map/ppermute | solution.py:527
  755.8 52.6 %collective-permute-done.42 = bf16[1,3,128,512]{3,2,1,0:T(8,128)(2,1)} collective-permute-done((bf16[1,3,128,512]{3,2,1,0:T(8,128)(2,1)S(1)}, bf16[1,3,128,512]{3,2,1,0:T(8,128)(2,1)}, u32[]{:S(2)}, u32[]{:S(2)}) %collective-permute-start.42) | collective-permute-done | bytes 393248 | tf_op jit(solution)/shard_map/ppermute | solution.py:527
  814.6 9.6 %collective-permute-done.48 = bf16[1,128,2048]{2,1,0:T(8,128)(2,1)S(1)} collective-permute-done((bf16[1,128,2048]{2,1,0:T(8,128)(2,1)S(1)}, bf16[1,128,2048]{2,1,0:T(8,128)(2,1)S(1)}, u32[]{:S(2)}, u32[]{:S(2)}) %collective-permute-start.48) | collective-permute-done | bytes 524320 | tf_op jit(solution)/shard_map/ppermute | solution.py:527
  825.3 11.6 %collective-permute-done.51 = bf16[1,128,2048]{1,2,0:T(8,128)(2,1)S(1)} collective-permute-done((bf16[1,128,2048]{1,2,0:T(8,128)(2,1)S(1)}, bf16[1,128,2048]{1,2,0:T(8,128)(2,1)S(1)}, u32[]{:S(2)}, u32[]{:S(2)}) %collective-permute-start.51) | collective-permute-done | bytes 524320 | tf_op jit(solution)/shard_map/ppermute | solution.py:527
  (406 shorter events, 252.2 us)
Async XLA Ops:
  5.2 21.4 %collective-permute-start.1 = (bf16[128,1024]{1,0:T(8,128)(2,1)S(1)}, bf16[128,1024]{1,0:T(8,128)(2,1)S(1)}, u32[]{:S(2)}, u32[]{:S(2)}) collective-permute-start(bf16[128,1024]{1,0:T(8,128)(2,1)S(1)} %get-tuple-element.109), channel_id=1, source_target_pairs={{0,8},{2,10},{4,12},{6,14},{8,0},{10,2},{12,4},{14,6},{1,9},{3,11}... | collective-permute-start | bytes 786440 | tf_op jit(solution)/shard_map/ppermute | solution.py:527
  27.6 25.9 %collective-permute-start.3 = (bf16[512,1024]{1,0:T(8,128)(2,1)}, bf16[512,1024]{1,0:T(8,128)(2,1)}, u32[]{:S(2)}, u32[]{:S(2)}) collective-permute-start(bf16[512,1024]{1,0:T(8,128)(2,1)} %pad_maximum_fusion.8), channel_id=1, source_target_pairs={{0,1},{1,0},{2,3},{3,2},{4,5},{5,4},{6,7},{7,6},{8,9},{9,8},{10,11... | collective-permute-start | bytes 3145736 | tf_op jit(solution)/shard_map/ppermute | solution.py:523
  27.6 25.9 %collective-permute-start.4 = (bf16[512,1024]{1,0:T(8,128)(2,1)}, bf16[512,1024]{1,0:T(8,128)(2,1)}, u32[]{:S(2)}, u32[]{:S(2)}) collective-permute-start(bf16[512,1024]{1,0:T(8,128)(2,1)} %pad_maximum_fusion.8), channel_id=1, source_target_pairs={{0,2},{2,0},{4,6},{6,4},{8,10},{10,8},{12,14},{14,12},{1,3},{3,1},... | collective-permute-start | bytes 3145736 | tf_op jit(solution)/shard_map/ppermute | solution.py:527
  53.5 33.5 %collective-permute-start.5 = (bf16[512,1024]{1,0:T(8,128)(2,1)}, bf16[512,1024]{1,0:T(8,128)(2,1)S(1)}, u32[]{:S(2)}, u32[]{:S(2)}) collective-permute-start(bf16[512,1024]{1,0:T(8,128)(2,1)} %collective-permute-done.4), channel_id=1, source_target_pairs={{0,1},{1,0},{2,3},{3,2},{4,5},{5,4},{6,7},{7,6},{8,9},{9,8},{10,11... | collective-permute-start | bytes 3145736 | tf_op jit(solution)/shard_map/ppermute | solution.py:523
  76.9 61.8 %collective-permute-start.7 = (bf16[512,1024]{1,0:T(8,128)(2,1)S(1)}, bf16[512,1024]{1,0:T(8,128)(2,1)S(1)}, u32[]{:S(2)}, u32[]{:S(2)}) collective-permute-start(bf16[512,1024]{1,0:T(8,128)(2,1)S(1)} %slice.369), channel_id=1, source_target_pairs={{0,1},{1,0},{2,3},{3,2},{4,5},{5,4},{6,7},{7,6},{8,9},{9,8},{10,11... | collective-permute-start | bytes 3145736 | tf_op jit(solution)/shard_map/ppermute | solution.py:523
  144.7 35.0 %collective-permute-start.8 = (bf16[512,1024]{1,0:T(8,128)(2,1)}, bf16[512,1024]{1,0:T(8,128)(2,1)}, u32[]{:S(2)}, u32[]{:S(2)}) collective-permute-start(bf16[512,1024]{1,0:T(8,128)(2,1)} %add_convert_fusion.6), channel_id=1, source_target_pairs={{0,16},{1,17},{2,18},{3,19},{4,20},{5,21},{6,22},{7,23},{8,24},{9,... | collective-permute-start | bytes 3145736 | tf_op jit(solution)/shard_map/ppermute | solution.py:532
  154.1 24.4 %collective-permute-start.19 = (bf16[128,1024]{1,0:T(8,128)(2,1)}, bf16[128,1024]{1,0:T(8,128)(2,1)S(1)}, u32[]{:S(2)}, u32[]{:S(2)}) collective-permute-start(bf16[128,1024]{1,0:T(8,128)(2,1)} %get-tuple-element.106), channel_id=1, source_target_pairs={{0,8},{2,10},{4,12},{6,14},{8,0},{10,2},{12,4},{14,6},{1,9},{3,11}... | collective-permute-start | bytes 786440 | tf_op jit(solution)/shard_map/ppermute | solution.py:527
  157.8 20.7 %collective-permute-start.18 = (bf16[128,1024]{1,0:T(8,128)(2,1)}, bf16[128,1024]{1,0:T(8,128)(2,1)S(1)}, u32[]{:S(2)}, u32[]{:S(2)}) collective-permute-start(bf16[128,1024]{1,0:T(8,128)(2,1)} %get-tuple-element.104), channel_id=1, source_target_pairs={{0,4},{2,6},{4,0},{6,2},{8,12},{10,14},{12,8},{14,10},{1,5},{3,7},... | collective-permute-start | bytes 786440 | tf_op jit(solution)/shard_map/ppermute | solution.py:527
  195.2 42.4 %collective-permute-start.10 = (bf16[512,1024]{1,0:T(8,128)(2,1)S(1)}, bf16[512,1024]{1,0:T(8,128)(2,1)S(1)}, u32[]{:S(2)}, u32[]{:S(2)}) collective-permute-start(bf16[512,1024]{1,0:T(8,128)(2,1)S(1)} %get-tuple-element.84.h_ref), channel_id=1, source_target_pairs={{0,2},{2,0},{4,6},{6,4},{8,10},{10,8},{12,14},{14,12},{1,3},{3,1},... | collective-permute-start | bytes 3145736 | tf_op jit(solution)/shard_map/ppermute | solution.py:527
  221.7 171.7 %collective-permute-start.13 = (bf16[512,1024]{1,0:T(8,128)(2,1)}, bf16[512,1024]{1,0:T(8,128)(2,1)}, u32[]{:S(2)}, u32[]{:S(2)}) collective-permute-start(bf16[512,1024]{1,0:T(8,128)(2,1)} %slice.295), channel_id=1, source_target_pairs={{0,1},{1,0},{2,3},{3,2},{4,5},{5,4},{6,7},{7,6},{8,9},{9,8},{10,11... | collective-permute-start | bytes 3145736 | tf_op jit(solution)/shard_map/ppermute | solution.py:523
  240.7 149.8 %collective-permute-start.25 = (bf16[512,1024]{1,0:T(8,128)(2,1)}, bf16[512,1024]{1,0:T(8,128)(2,1)}, u32[]{:S(2)}, u32[]{:S(2)}) collective-permute-start(bf16[512,1024]{1,0:T(8,128)(2,1)} %get-tuple-element.101), channel_id=1, source_target_pairs={{0,1},{1,0},{2,3},{3,2},{4,5},{5,4},{6,7},{7,6},{8,9},{9,8},{10,11... | collective-permute-start | bytes 3145736 | tf_op jit(solution)/shard_map/ppermute | solution.py:523
  387.0 25.4 %collective-permute-start.24 = (bf16[512,1024]{1,0:T(8,128)(2,1)S(1)}, bf16[512,1024]{1,0:T(8,128)(2,1)S(1)}, u32[]{:S(2)}, u32[]{:S(2)}) collective-permute-start(bf16[512,1024]{1,0:T(8,128)(2,1)S(1)} %fusion.6), channel_id=1, source_target_pairs={{0,2},{2,0},{4,6},{6,4},{8,10},{10,8},{12,14},{14,12},{1,3},{3,1},... | collective-permute-start | bytes 3145736 | tf_op jit(solution)/shard_map/ppermute | solution.py:527
  420.6 26.8 %collective-permute-start.26 = (bf16[512,1024]{1,0:T(8,128)(2,1)}, bf16[512,1024]{1,0:T(8,128)(2,1)S(1)}, u32[]{:S(2)}, u32[]{:S(2)}) collective-permute-start(bf16[512,1024]{1,0:T(8,128)(2,1)} %get-tuple-element.69), channel_id=1, source_target_pairs={{16,0},{17,1},{18,2},{19,3},{20,4},{21,5},{22,6},{23,7},{24,8},{25... | collective-permute-start | bytes 3145736 | tf_op jit(solution)/shard_map/ppermute | solution.py:532
  424.7 21.3 %collective-permute-start.15 = (bf16[128,1024]{1,0:T(8,128)(2,1)S(1)}, bf16[128,1024]{1,0:T(8,128)(2,1)S(1)}, u32[]{:S(2)}, u32[]{:S(2)}) collective-permute-start(bf16[128,1024]{1,0:T(8,128)(2,1)S(1)} %get-tuple-element.122), channel_id=1, source_target_pairs={{0,8},{2,10},{4,12},{6,14},{8,0},{10,2},{12,4},{14,6},{1,9},{3,11}... | collective-permute-start | bytes 786440 | tf_op jit(solution)/shard_map/ppermute | solution.py:527
  424.7 21.3 %collective-permute-start.14 = (bf16[128,1024]{1,0:T(8,128)(2,1)S(1)}, bf16[128,1024]{1,0:T(8,128)(2,1)S(1)}, u32[]{:S(2)}, u32[]{:S(2)}) collective-permute-start(bf16[128,1024]{1,0:T(8,128)(2,1)S(1)} %get-tuple-element.123), channel_id=1, source_target_pairs={{0,4},{2,6},{4,0},{6,2},{8,12},{10,14},{12,8},{14,10},{1,5},{3,7},... | collective-permute-start | bytes 786440 | tf_op jit(solution)/shard_map/ppermute | solution.py:527
  537.6 81.5 %collective-permute-start.29 = (bf16[1,512,1024]{2,1,0:T(8,128)(2,1)}, bf16[1,512,1024]{2,1,0:T(8,128)(2,1)}, u32[]{:S(2)}, u32[]{:S(2)}) collective-permute-start(bf16[1,512,1024]{2,1,0:T(8,128)(2,1)} %slice_bitcast_fusion), channel_id=1, source_target_pairs={{0,1},{1,0},{2,3},{3,2},{4,5},{5,4},{6,7},{7,6},{8,9},{9,8},{10,11... | collective-permute-start | bytes 3145736 | tf_op jit(solution)/shard_map/ppermute | solution.py:523
  548.5 94.9 %collective-permute-start.28 = (bf16[512,1024]{1,0:T(8,128)(2,1)}, bf16[512,1024]{1,0:T(8,128)(2,1)}, u32[]{:S(2)}, u32[]{:S(2)}) collective-permute-start(bf16[512,1024]{1,0:T(8,128)(2,1)} %get-tuple-element.99), channel_id=1, source_target_pairs={{0,1},{1,0},{2,3},{3,2},{4,5},{5,4},{6,7},{7,6},{8,9},{9,8},{10,11... | collective-permute-start | bytes 3145736 | tf_op jit(solution)/shard_map/ppermute | solution.py:523
  550.5 82.6 %collective-permute-start.31 = (bf16[512,1024]{1,0:T(8,128)(2,1)}, bf16[512,1024]{1,0:T(8,128)(2,1)}, u32[]{:S(2)}, u32[]{:S(2)}) collective-permute-start(bf16[512,1024]{1,0:T(8,128)(2,1)} %get-tuple-element.97), channel_id=1, source_target_pairs={{0,1},{1,0},{2,3},{3,2},{4,5},{5,4},{6,7},{7,6},{8,9},{9,8},{10,11... | collective-permute-start | bytes 3145736 | tf_op jit(solution)/shard_map/ppermute | solution.py:523
  561.4 139.0 %collective-permute-start.40 = (bf16[4,3,128,512]{3,2,1,0:T(8,128)(2,1)}, bf16[4,3,128,512]{3,2,1,0:T(8,128)(2,1)}, u32[]{:S(2)}, u32[]{:S(2)}) collective-permute-start(bf16[4,3,128,512]{3,2,1,0:T(8,128)(2,1)} %slice.387), channel_id=1, source_target_pairs={{0,2},{2,0},{4,6},{6,4},{8,10},{10,8},{12,14},{14,12},{1,3},{3,1},... | collective-permute-start | bytes 4718600 | tf_op jit(solution)/shard_map/ppermute | solution.py:527
  569.8 39.8 %collective-permute-start.43 = (bf16[4,128,512]{1,2,0:T(8,128)(2,1)}, bf16[4,128,512]{1,2,0:T(8,128)(2,1)S(1)}, u32[]{:S(2)}, u32[]{:S(2)}) collective-permute-start(bf16[4,128,512]{1,2,0:T(8,128)(2,1)} %copy.103), channel_id=1, source_target_pairs={{0,2},{2,0},{4,6},{6,4},{8,10},{10,8},{12,14},{14,12},{1,3},{3,1},... | collective-permute-start | bytes 1572872 | tf_op jit(solution)/shard_map/ppermute | solution.py:527
  618.5 92.0 %collective-permute-start.49 = (bf16[4,128,2048]{1,2,0:T(8,128)(2,1)}, bf16[4,128,2048]{1,2,0:T(8,128)(2,1)}, u32[]{:S(2)}, u32[]{:S(2)}) collective-permute-start(bf16[4,128,2048]{1,2,0:T(8,128)(2,1)} %copy.105), channel_id=1, source_target_pairs={{0,2},{2,0},{4,6},{6,4},{8,10},{10,8},{12,14},{14,12},{1,3},{3,1},... | collective-permute-start | bytes 6291464 | tf_op jit(solution)/shard_map/ppermute | solution.py:527
  627.0 60.6 %collective-permute-start.30 = (bf16[512,1024]{1,0:T(8,128)(2,1)S(1)}, bf16[512,1024]{1,0:T(8,128)(2,1)}, u32[]{:S(2)}, u32[]{:S(2)}) collective-permute-start(bf16[512,1024]{1,0:T(8,128)(2,1)S(1)} %fusion.7), channel_id=1, source_target_pairs={{0,2},{2,0},{4,6},{6,4},{8,10},{10,8},{12,14},{14,12},{1,3},{3,1},... | collective-permute-start | bytes 3145736 | tf_op jit(solution)/shard_map/ppermute | solution.py:527
  633.1 103.9 %collective-permute-start.46 = (bf16[4,128,2048]{2,1,0:T(8,128)(2,1)}, bf16[4,128,2048]{2,1,0:T(8,128)(2,1)}, u32[]{:S(2)}, u32[]{:S(2)}) collective-permute-start(bf16[4,128,2048]{2,1,0:T(8,128)(2,1)} %bitcast.98), channel_id=1, source_target_pairs={{0,4},{2,6},{4,0},{6,2},{8,12},{10,14},{12,8},{14,10},{1,5},{3,7},... | collective-permute-start | bytes 6291464 | tf_op jit(solution)/shard_map/ppermute | solution.py:527
  703.6 43.3 %collective-permute-start.41 = (bf16[2,3,128,512]{3,2,1,0:T(8,128)(2,1)S(1)}, bf16[2,3,128,512]{3,2,1,0:T(8,128)(2,1)}, u32[]{:S(2)}, u32[]{:S(2)}) collective-permute-start(bf16[2,3,128,512]{3,2,1,0:T(8,128)(2,1)S(1)} %slice.389), channel_id=1, source_target_pairs={{0,4},{2,6},{4,0},{6,2},{8,12},{10,14},{12,8},{14,10},{1,5},{3,7},... | collective-permute-start | bytes 2359304 | tf_op jit(solution)/shard_map/ppermute | solution.py:527
  706.5 43.8 %collective-permute-start.34 = (bf16[128,1024]{1,0:T(8,128)(2,1)}, bf16[128,1024]{1,0:T(8,128)(2,1)}, u32[]{:S(2)}, u32[]{:S(2)}) collective-permute-start(bf16[128,1024]{1,0:T(8,128)(2,1)} %get-tuple-element.115), channel_id=1, source_target_pairs={{0,12},{2,14},{4,8},{6,10},{8,4},{10,6},{12,0},{14,2},{1,13},{3,15... | collective-permute-start | bytes 786440 | tf_op jit(solution)/shard_map/ppermute | solution.py:527
  709.1 45.4 %collective-permute-start.33 = (bf16[128,1024]{1,0:T(8,128)(2,1)}, bf16[128,1024]{1,0:T(8,128)(2,1)}, u32[]{:S(2)}, u32[]{:S(2)}) collective-permute-start(bf16[128,1024]{1,0:T(8,128)(2,1)} %get-tuple-element.116), channel_id=1, source_target_pairs={{0,8},{2,10},{4,12},{6,14},{8,0},{10,2},{12,4},{14,6},{1,9},{3,11}... | collective-permute-start | bytes 786440 | tf_op jit(solution)/shard_map/ppermute | solution.py:527
  710.6 25.1 %collective-permute-start.38 = (f32[8707]{0:T(1024)S(1)}, f32[8707]{0:T(1024)S(1)}, u32[]{:S(2)}, u32[]{:S(2)}) collective-permute-start(f32[8707]{0:T(1024)S(1)} %add.437), channel_id=1, source_target_pairs={{0,4},{2,6},{4,0},{6,2},{8,12},{10,14},{12,8},{14,10},{1,5},{3,7},... | collective-permute-start | bytes 104492 | tf_op jit(solution)/shard_map/ppermute | solution.py:527
  743.5 67.0 %collective-permute-start.47 = (bf16[2,128,2048]{2,1,0:T(8,128)(2,1)}, bf16[2,128,2048]{2,1,0:T(8,128)(2,1)}, u32[]{:S(2)}, u32[]{:S(2)}) collective-permute-start(bf16[2,128,2048]{2,1,0:T(8,128)(2,1)} %slice.403), channel_id=1, source_target_pairs={{0,8},{2,10},{4,12},{6,14},{8,0},{10,2},{12,4},{14,6},{1,9},{3,11}... | collective-permute-start | bytes 3145736 | tf_op jit(solution)/shard_map/ppermute | solution.py:527
  748.3 60.1 %collective-permute-start.42 = (bf16[1,3,128,512]{3,2,1,0:T(8,128)(2,1)S(1)}, bf16[1,3,128,512]{3,2,1,0:T(8,128)(2,1)}, u32[]{:S(2)}, u32[]{:S(2)}) collective-permute-start(bf16[1,3,128,512]{3,2,1,0:T(8,128)(2,1)S(1)} %slice.391), channel_id=1, source_target_pairs={{0,8},{2,10},{4,12},{6,14},{8,0},{10,2},{12,4},{14,6},{1,9},{3,11}... | collective-permute-start | bytes 1179656 | tf_op jit(solution)/shard_map/ppermute | solution.py:527
  750.4 62.5 %collective-permute-start.50 = (bf16[2,128,2048]{1,2,0:T(8,128)(2,1)}, bf16[2,128,2048]{1,2,0:T(8,128)(2,1)S(1)}, u32[]{:S(2)}, u32[]{:S(2)}) collective-permute-start(bf16[2,128,2048]{1,2,0:T(8,128)(2,1)} %slice.410), channel_id=1, source_target_pairs={{0,4},{2,6},{4,0},{6,2},{8,12},{10,14},{12,8},{14,10},{1,5},{3,7},... | collective-permute-start | bytes 3145736 | tf_op jit(solution)/shard_map/ppermute | solution.py:527
  755.7 57.5 %collective-permute-start.35 = (bf16[4,128,1024]{2,1,0:T(8,128)(2,1)S(1)}, bf16[4,128,1024]{2,1,0:T(8,128)(2,1)S(1)}, u32[]{:S(2)}, u32[]{:S(2)}) collective-permute-start(bf16[4,128,1024]{2,1,0:T(8,128)(2,1)S(1)} %get-tuple-element.113), channel_id=1, source_target_pairs={{0,1},{1,0},{2,3},{3,2},{4,5},{5,4},{6,7},{7,6},{8,9},{9,8},{10,11... | collective-permute-start | bytes 3145736 | tf_op jit(solution)/shard_map/ppermute | solution.py:523
  813.2 23.7 %collective-permute-start.51 = (bf16[1,128,2048]{1,2,0:T(8,128)(2,1)S(1)}, bf16[1,128,2048]{1,2,0:T(8,128)(2,1)S(1)}, u32[]{:S(2)}, u32[]{:S(2)}) collective-permute-start(bf16[1,128,2048]{1,2,0:T(8,128)(2,1)S(1)} %slice.412), channel_id=1, source_target_pairs={{0,8},{2,10},{4,12},{6,14},{8,0},{10,2},{12,4},{14,6},{1,9},{3,11}... | collective-permute-start | bytes 1572872 | tf_op jit(solution)/shard_map/ppermute | solution.py:527
  (84 other events, 1274.3 us)

commit v2 on v1

v2 whole, which is shorter than its diff:
```python
import functools

import jax
import jax.numpy as jnp
from jax import lax
from jax.experimental import pallas as pl
from jax.experimental.pallas import tpu as pltpu
from jax.sharding import PartitionSpec as P

HEAD = 64
ROT = 16
EPS = 1e-05
ROTARY_BASE = 10000.0
NEGATIVE = -1e30
STACK = 4
GROUP = STACK * HEAD
KEY_TILE = 512
VMEM_LIMIT = 56 * 1024 * 1024
BF16 = jnp.bfloat16
F32 = jnp.float32


def dot(a, b):
    return jnp.dot(a, b, preferred_element_type=F32)


def dot_nt(a, b):
    return lax.dot_general(a, b, (((1,), (1,)), ((), ())), preferred_element_type=F32)


def params_of(**more):
    return pltpu.CompilerParams(vmem_limit_bytes=VMEM_LIMIT, **more)


def whole(shape):
    return pl.BlockSpec(shape, lambda *_: (0,) * len(shape))


def rows_of(tile, *rest):
    return pl.BlockSpec((tile, *rest), lambda r, *_: (r,) + (0,) * len(rest))


def halves_of(tile, count, *rest):
    return [
        pl.BlockSpec((tile, *rest), lambda r, *_: (jnp.minimum(r, count - 1),) + (0,) * len(rest)),
        pl.BlockSpec((tile, *rest), lambda r, *_: (jnp.maximum(r - count, 0),) + (0,) * len(rest)),
    ]


def pick(refs):
    return jnp.where(pl.program_id(0) < pl.num_programs(0) // 2, refs[0][...], refs[1][...])


def put(refs, value):
    first = pl.program_id(0) < pl.num_programs(0) // 2
    for ref, here in zip(refs, (first, jnp.logical_not(first))):

        @pl.when(here)
        def _():
            ref[...] = value


def waiting(kernel, inputs, deps):
    return lambda *refs: kernel(*refs[:inputs], *refs[inputs + len(deps) :])


def exchanged(position, mask):
    for bit in range(mask.bit_length()):
        if mask >> bit & 1:
            position = position + (1 << bit) - (2 << bit) * (position // (1 << bit) % 2)
    return position


def carrying(kernel, inputs, outputs, moves):
    count = len(moves)

    def body(*refs):
        sources = refs[inputs : inputs + count]
        outs = refs[inputs + count : inputs + count + outputs]
        targets = refs[inputs + count + outputs : inputs + 2 * count + outputs]
        *scratch, send, receive = refs[inputs + 2 * count + outputs :]
        partners = [{axis: exchanged(lax.axis_index(axis), mask)} for axis, mask in moves]
        copies = [
            pltpu.make_async_remote_copy(
                source, target, send.at[n], receive.at[n], device_id=partner, device_id_type=pl.DeviceIdType.MESH
            )
            for n, (source, target, partner) in enumerate(zip(sources, targets, partners))
        ]

        @pl.when(pl.program_id(0) == 0)
        def _():
            barrier = pltpu.get_barrier_semaphore()
            for partner in partners:
                pl.semaphore_signal(barrier, inc=1, device_id=partner, device_id_type=pl.DeviceIdType.MESH)
            pl.semaphore_wait(barrier, count)
            for copy in copies:
                copy.start()

        kernel(*refs[:inputs], *outs, *scratch)

        @pl.when(pl.program_id(0) == pl.num_programs(0) - 1)
        def _():
            for copy in copies:
                copy.wait()

    return body


def carrier_semaphores(count):
    return [pltpu.SemaphoreType.DMA((count,)), pltpu.SemaphoreType.DMA((count,))]


def anywhere(count):
    return [pl.BlockSpec(memory_space=pl.ANY)] * count


def cost(flops, size):
    return pl.CostEstimate(flops=int(flops), bytes_accessed=int(size), transcendentals=0)


def shape_of(*shape, dtype=BF16):
    return jax.ShapeDtypeStruct(shape, dtype)


def normalize(values):
    middle = jnp.mean(values, axis=-1, keepdims=True)
    centered = values - middle
    spread = jnp.mean(centered * centered, axis=-1, keepdims=True)
    inverse = lax.rsqrt(spread + EPS)
    return centered * inverse, inverse


def turn(values, cosine, sine):
    pieces = []
    for start in range(0, values.shape[1], 128):
        part = values[:, start : start + 128]
        ahead = pltpu.roll(part, 128 - ROT // 2, 1)
        behind = pltpu.roll(part, ROT // 2, 1)
        entry = lax.broadcasted_iota(jnp.int32, part.shape, 1) % HEAD
        pieces.append(part * cosine + jnp.where(entry < ROT // 2, -ahead, behind) * sine)
    return jnp.concatenate(pieces, axis=1)


def joint_kernel(h0_ref, h1_ref, gain_ref, shift_ref, w_ref, b_ref, cos_ref, sin_ref, n_ref, k_ref, v_ref):
    scaled, _ = normalize(pick((h0_ref, h1_ref)).astype(F32))
    low = (scaled * gain_ref[...] + shift_ref[...]).astype(BF16)
    n_ref[...] = low
    cosine, sine = cos_ref[...], sin_ref[...]
    keys = dot(low, w_ref[1]) + b_ref[1:2]
    values = dot(low, w_ref[2]) + b_ref[2:3]
    k_ref[...] = turn(keys, cosine, sine).astype(BF16)
    v_ref[...] = values.astype(BF16)


def joint_call(pair, gain, shift, w_joint, b_joint, table, offset, deps=()):
    rows, width = pair[0].shape
    local = w_joint.shape[2]
    tile = min(512, rows)
    first = offset // tile
    count = 2
    turns = pl.BlockSpec((tile, 128), lambda r: (first + r, 0))
    return pl.pallas_call(
        waiting(joint_kernel, 8, deps),
        grid=(2 * rows // tile,),
        in_specs=halves_of(tile, rows // tile, width)
        + [whole((1, width)), whole((1, width)), whole(w_joint.shape), whole(b_joint.shape), turns, turns]
        + anywhere(len(deps)),
        out_specs=[rows_of(tile, width)] + [rows_of(tile, local)] * count,
        out_shape=[shape_of(2 * rows, width)] + [shape_of(2 * rows, local)] * count,
        compiler_params=params_of(),
        cost_estimate=cost(4 * rows * width * local * count, 8 * rows * width + 2 * w_joint.size),
        name="joint_projection",
    )(*pair, gain, shift, w_joint, b_joint, *table, *deps)


def gelu_parts(x):
    return 0.5 + 0.5 * lax.erf(x * 0.5**0.5), jnp.exp(-0.5 * x * x)


def front_kernel(
    save, h0_ref, h1_ref, norms_ref, w_ref, b_ref, cos_ref, sin_ref, up_ref, up_b_ref, down_ref,
    n_ref, k_ref, v_ref, q_ref, part0_ref, part1_ref, *saved
):
    scaled, _ = normalize(pick((h0_ref, h1_ref)).astype(F32))
    low = (scaled * norms_ref[0:1] + norms_ref[1:2]).astype(BF16)
    n_ref[...] = low
    cosine, sine = cos_ref[...], sin_ref[...]
    keys = dot(low, w_ref[1]) + b_ref[1:2]
    values = dot(low, w_ref[2]) + b_ref[2:3]
    queries = dot(low, w_ref[0]) + b_ref[0:1]
    q_ref[...] = (turn(queries, cosine, sine) * HEAD ** (-0.5)).astype(BF16)
    k_ref[...] = turn(keys, cosine, sine).astype(BF16)
    v_ref[...] = values.astype(BF16)
    low = (scaled * norms_ref[2:3] + norms_ref[3:4]).astype(BF16)
    if save:
        saved[0][...] = low
    total = None
    for start in range(0, up_ref.shape[1], 512):
        cut = pl.ds(start, 512)
        hidden = dot(low, up_ref[:, cut]) + up_b_ref[:, cut]
        share, bell = gelu_parts(hidden)
        active = (hidden * share).astype(BF16)
        if save:
            saved[1][:, cut] = active
            saved[2][:, cut] = (share + hidden * bell * 0.3989422804014327).astype(BF16)
        term = dot(active, down_ref[cut, :])
        total = term if total is None else total + term
    put((part0_ref, part1_ref), total.astype(BF16))


def front_call(pair, norms, w_joint, b_joint, table, w_up, b_up, w_down, save, moves, moved, name, number):
    rows, width = pair[0].shape
    local = w_joint.shape[2]
    units = w_up.shape[1]
    tile = min(512, rows)
    out = [shape_of(2 * rows, width)] + [shape_of(2 * rows, local)] * 3 + [shape_of(rows, width)] * 2
    out_specs = [rows_of(tile, width)] + [rows_of(tile, local)] * 3 + halves_of(tile, rows // tile, width)
    if save:
        out += [shape_of(2 * rows, width)] + [shape_of(2 * rows, units)] * 2
        out_specs += [rows_of(tile, width), rows_of(tile, units), rows_of(tile, units)]
    ins = (norms, w_joint, b_joint, *table, w_up, b_up, w_down)
    turns = rows_of(tile, 128)
    specs = [turns if x is table[0] or x is table[1] else whole(x.shape) for x in ins]
    outs = pl.pallas_call(
        carrying(functools.partial(front_kernel, save), 2 + len(ins), len(out), moves),
        grid=(2 * rows // tile,),
        in_specs=halves_of(tile, rows // tile, width) + specs + anywhere(len(moves)),
        out_specs=out_specs + anywhere(len(moves)),
        out_shape=out + [shape_of(*x.shape) for x in moved],
        scratch_shapes=carrier_semaphores(len(moves)),
        compiler_params=params_of(collective_id=number, has_side_effects=True),
        cost_estimate=cost(4 * rows * width * (3 * local + 2 * units), 4 * w_up.size + 16 * rows * width),
        name=name,
    )(*pair, *ins, *moved)
    return outs[: len(out)], outs[len(out) :]


def ffn_back_kernel(g0_ref, g1_ref, slope_ref, up_ref, down_ref, part0_ref, part1_ref, hidden_ref, sums_ref):
    upstream = pick((g0_ref, g1_ref))
    units = up_ref.shape[1]

    @pl.when(pl.program_id(0) == 0)
    def _():
        sums_ref[...] = jnp.zeros_like(sums_ref)

    total = None
    for start in range(0, units, 512):
        cut = pl.ds(start, 512)
        d_active = dot_nt(upstream, down_ref[cut, :])
        d_hidden = (d_active * slope_ref[:, cut].astype(F32)).astype(BF16)
        hidden_ref[:, cut] = d_hidden
        sums_ref[:, cut] += jnp.sum(d_hidden.astype(F32), axis=0, keepdims=True)
        term = dot_nt(d_hidden, up_ref[:, cut])
        total = term if total is None else total + term
    put((part0_ref, part1_ref), total.astype(BF16))


def ffn_back_call(pair, slope, w_up, w_down, deps=()):
    rows, width = pair[0].shape
    units = w_up.shape[1]
    tile = min(512, rows)
    return pl.pallas_call(
        waiting(ffn_back_kernel, 5, deps),
        grid=(2 * rows // tile,),
        in_specs=halves_of(tile, rows // tile, width) + [rows_of(tile, units), whole(w_up.shape), whole(w_down.shape)]
        + anywhere(len(deps)),
        out_specs=halves_of(tile, rows // tile, width) + [rows_of(tile, units), whole((1, units))],
        out_shape=[shape_of(rows, width)] * 2 + [shape_of(2 * rows, units), shape_of(1, units, dtype=F32)],
        compiler_params=params_of(),
        cost_estimate=cost(8 * rows * width * units, 4 * w_up.size + 8 * rows * (width + units)),
        name="feed_forward_back",
    )(*pair, slope, w_up, w_down, *deps)


def start_sorted(places_ref, parts, targets, sem, block):
    copies = []
    for refs, target in zip(parts, targets):
        index = 0
        for ref in refs:
            for local in range(ref.shape[0] // block):
                place = pl.ds(pl.multiple_of(places_ref[index] * block, block), block)
                copies.append(pltpu.make_async_copy(ref.at[pl.ds(local * block, block)], target.at[place], sem))
                index += 1
    for copy in copies:
        copy.start()
    return copies


def transpose_into(source, target):
    rows, columns = source.shape

    def step(index, _):
        start = pl.multiple_of(index * 256, 256)
        for column in range(0, columns, 256):
            target[column : column + 256, pl.ds(start, 256)] = source[pl.ds(start, 256), column : column + 256].T
        return 0

    lax.fori_loop(0, rows // 256, step, 0)


def stacked(values):
    owner = lax.broadcasted_iota(jnp.int32, values.shape, 1) // HEAD
    zero = jnp.zeros_like(values)
    return jnp.concatenate([jnp.where(owner == a, values, zero) for a in range(STACK)], axis=0)


def spots_of(places_ref, step, tile, block, shape, axis):
    at = lax.broadcasted_iota(jnp.int32, shape, axis) % tile
    count = tile // block
    spot = at + places_ref[step * count] * block
    for s in range(1, count):
        spot = jnp.where(at >= s * block, at - s * block + places_ref[step * count + s] * block, spot)
    return spot


def attend_kernel(block, tile, remote, places_ref, limits_ref, q_ref, wo_ref, *refs):
    key_refs, value_refs = refs[: 1 + remote], refs[1 + remote : 2 + 2 * remote]
    part0_ref, part1_ref, mix_ref, lse_ref, keys, values, scores_ref, sem = refs[2 + 2 * remote :]
    groups = q_ref.shape[1] // GROUP
    half = part0_ref.shape[0]
    rows = STACK * tile
    lanes = [slice(g * GROUP, (g + 1) * GROUP) for g in range(groups)]
    for copy in start_sorted(places_ref, (key_refs, value_refs), (keys, values), sem, block):
        copy.wait()

    def tile_step(step, _):
        mine = pl.ds(pl.multiple_of(step * tile, tile), tile)
        heads = [stacked(q_ref[mine, lane]) for lane in lanes]
        spots = spots_of(places_ref, step, tile, block, (rows, 128), 0)

        def attend_to(count):
            open_end = (count - 1) * KEY_TILE if tile == block else 0
            tops = []
            for g, lane in enumerate(lanes):
                top = None
                for start in range(0, count * KEY_TILE, KEY_TILE):
                    scores = dot_nt(heads[g], keys[start : start + KEY_TILE, lane])
                    for column in range(0, KEY_TILE, 128):
                        piece = scores[:, column : column + 128]
                        if start + column >= open_end:
                            spot = start + column + lax.broadcasted_iota(jnp.int32, piece.shape, 1)
                            piece = jnp.where(spot <= spots, piece, NEGATIVE)
                        scores_ref[g, :, start + column : start + column + 128] = piece
                        top = piece if top is None else jnp.maximum(top, piece)
                tops.append(jnp.broadcast_to(jnp.max(top, axis=1, keepdims=True), (rows, 128)))
            for g, lane in enumerate(lanes):
                mass, total = None, None
                for start in range(0, count * KEY_TILE, KEY_TILE):
                    raised = []
                    for column in range(start, start + KEY_TILE, 128):
                        piece = jnp.exp(scores_ref[g, :, column : column + 128] - tops[g])
                        mass = piece if mass is None else mass + piece
                        raised.append(piece.astype(BF16))
                    term = dot(jnp.concatenate(raised, axis=1), values[start : start + KEY_TILE, lane])
                    total = term if total is None else total + term
                mass = jnp.broadcast_to(jnp.sum(mass, axis=1, keepdims=True), (rows, 128))
                total = total * jnp.concatenate([1.0 / mass] * (GROUP // 128), axis=1)
                owner = lax.broadcasted_iota(jnp.int32, (tile, GROUP), 1) // HEAD
                mixture = total[:tile]
                for a in range(1, STACK):
                    mixture = jnp.where(owner == a, total[a * tile : (a + 1) * tile], mixture)
                mix_ref[mine, lane] = mixture.astype(BF16)
                lse = tops[g] + jnp.log(mass)
                for a in range(STACK):
                    lse_ref[step, g : g + 1, a * tile : (a + 1) * tile] = lse[a * tile : (a + 1) * tile].T[0:1]

        for count in range(1, keys.shape[0] // KEY_TILE + 1):
            pl.when(limits_ref[step, 1] == count)(functools.partial(attend_to, count))
        return 0

    lax.fori_loop(0, q_ref.shape[0] // tile, tile_step, 0)
    part0_ref[...] = dot(mix_ref[:half], wo_ref[...]).astype(BF16)
    part1_ref[...] = dot(mix_ref[half:], wo_ref[...]).astype(BF16)


def attend_call(queries, key_parts, value_parts, places, limits, w_output, block, deps=()):
    rows, local = queries.shape
    width = w_output.shape[1]
    tile = rows // limits.shape[0]
    length = sum(part.shape[0] for part in key_parts)
    groups = local // GROUP
    outs = [(rows // 2, width), (rows // 2, width), (rows, local), (rows // tile, groups, STACK * tile)]
    return pl.pallas_call(
        waiting(functools.partial(attend_kernel, block, tile, len(key_parts) - 1), 4 + 2 * len(key_parts), deps),
        grid_spec=pltpu.PrefetchScalarGridSpec(
            num_scalar_prefetch=2,
            grid=(1,),
            in_specs=[whole((rows, local)), whole(w_output.shape)] + anywhere(2 * len(key_parts) + len(deps)),
            out_specs=[whole(shape) for shape in outs],
            scratch_shapes=[
                pltpu.VMEM((length, local), BF16),
                pltpu.VMEM((length, local), BF16),
                pltpu.VMEM((groups, STACK * tile, length), F32),
                pltpu.SemaphoreType.DMA,
            ],
        ),
        out_shape=[shape_of(*shape) for shape in outs[:3]] + [shape_of(*outs[3], dtype=F32)],
        compiler_params=params_of(),
        cost_estimate=cost(12 * rows * length * local, 2 * length * local * 4),
        name="attend",
    )(places, limits, queries, w_output, *key_parts, *value_parts, *deps)


def attend_back_kernel(
    block, tile, remote, places_ref, limits_ref, q_ref, g0_ref, g1_ref, mix_ref, lse_ref, wo_ref, cos_ref, sin_ref, *refs
):
    key_refs, value_refs = refs[: 1 + remote], refs[1 + remote : 2 + 2 * remote]
    (dq_ref, dk_ref, dv_ref, sums_ref, keys, values, keys_t, d_keys, d_values, d_mixture, inner, total, d_queries, sem) = refs[
        2 + 2 * remote :
    ]
    groups = q_ref.shape[1] // GROUP
    rows = q_ref.shape[0]
    half = g0_ref.shape[0]
    lanes = [slice(g * GROUP, (g + 1) * GROUP) for g in range(groups)]
    copies = start_sorted(places_ref, (key_refs, value_refs), (keys, values), sem, block)
    d_keys[...] = jnp.zeros_like(d_keys)
    d_values[...] = jnp.zeros_like(d_values)
    head_of = lax.broadcasted_iota(jnp.int32, (8, GROUP), 1) // HEAD
    picker = jnp.where(lax.broadcasted_iota(jnp.int32, (8, GROUP), 0) == head_of, 1.0, 0.0).astype(BF16)
    for index, ref in enumerate((g0_ref, g1_ref)):
        cut = pl.ds(index * half, half)
        low = dot_nt(ref[...], wo_ref[...]).astype(BF16)
        d_mixture[cut, :] = low
        product = low.astype(F32) * mix_ref[cut, :].astype(F32)
        high = product.astype(BF16)
        rest = (product - high.astype(F32)).astype(BF16)
        for g, lane in enumerate(lanes):
            inner[g * 8 : (g + 1) * 8, cut] = dot_nt(picker, high[:, lane]) + dot_nt(picker, rest[:, lane])
    for copy in copies:
        copy.wait()
    transpose_into(keys, keys_t)

    def query_step(step, _):
        mine = pl.ds(pl.multiple_of(step * tile, tile), tile)
        spots = spots_of(places_ref, step, tile, block, (1, STACK * tile), 1)
        heads = [stacked(q_ref[mine, lane]) for lane in lanes]
        sides = [stacked(d_mixture[mine, lane]) for lane in lanes]
        sums = [
            jnp.concatenate([inner[g * 8 + a : g * 8 + a + 1, mine] for a in range(STACK)], axis=1) for g in range(groups)
        ]
        lse = [lse_ref[step, g : g + 1, :] for g in range(groups)]
        total[...] = jnp.zeros_like(total)

        def key_step(masked, index, carry):
            start = pl.multiple_of(index * KEY_TILE, KEY_TILE)
            cut = pl.ds(start, KEY_TILE)
            for g, lane in enumerate(lanes):
                scores = dot_nt(keys[cut, lane], heads[g])
                if masked:
                    spot = start + lax.broadcasted_iota(jnp.int32, scores.shape, 0)
                    scores = jnp.where(spot <= spots, scores, NEGATIVE)
                weights = jnp.exp(scores - lse[g])
                d_weights = dot_nt(values[cut, lane], sides[g])
                d_scores = (weights * (d_weights - sums[g])).astype(BF16)
                d_values[cut, lane] += dot(weights.astype(BF16), sides[g])
                d_keys[cut, lane] += dot(d_scores, heads[g])
                total[lane, :] += dot(keys_t[lane, cut], d_scores)
            return carry

        lax.fori_loop(0, limits_ref[step, 0], functools.partial(key_step, False), 0)
        lax.fori_loop(limits_ref[step, 0], limits_ref[step, 1], functools.partial(key_step, True), 0)
        for lane in lanes:
            picked = [total[lane, :][a * HEAD : (a + 1) * HEAD, a * tile : (a + 1) * tile] for a in range(STACK)]
            d_queries[mine, lane] = jnp.concatenate(picked, axis=0).T
        return 0

    lax.fori_loop(0, rows // tile, query_step, 0)
    turned = turn(d_queries[...] * HEAD ** (-0.5), cos_ref[:rows], -sin_ref[:rows]).astype(BF16)
    dq_ref[...] = turned
    sums_ref[...] = jnp.zeros_like(sums_ref)
    sums_ref[0:1, :] = jnp.sum(turned.astype(F32), axis=0, keepdims=True)

    def block_step(index, _):
        place = pl.ds(pl.multiple_of(places_ref[index] * block, block), block)
        mine = pl.ds(pl.multiple_of(index * block, block), block)
        turned = turn(d_keys[place, :], cos_ref[mine, :], -sin_ref[mine, :]).astype(BF16)
        dk_ref[mine, :] = turned
        low = d_values[place, :].astype(BF16)
        dv_ref[mine, :] = low
        sums_ref[1:2, :] += jnp.sum(turned.astype(F32), axis=0, keepdims=True)
        sums_ref[2:3, :] += jnp.sum(low.astype(F32), axis=0, keepdims=True)
        return 0

    lax.fori_loop(0, dk_ref.shape[0] // block, block_step, 0)


def attend_back_call(
    queries, g_pair, mixture, lse, key_parts, value_parts, places, limits, w_output, table, block, deps=()
):
    rows, local = queries.shape
    width = w_output.shape[1]
    tile = rows // limits.shape[0]
    length = sum(part.shape[0] for part in key_parts)
    groups = local // GROUP
    ins = (queries, *g_pair, mixture, lse, w_output, *table)
    return pl.pallas_call(
        waiting(
            functools.partial(attend_back_kernel, block, tile, len(key_parts) - 1), 2 + len(ins) + 2 * len(key_parts), deps
        ),
        grid_spec=pltpu.PrefetchScalarGridSpec(
            num_scalar_prefetch=2,
            grid=(1,),
            in_specs=[whole(x.shape) for x in ins] + anywhere(2 * len(key_parts) + len(deps)),
            out_specs=[whole((rows, local)), whole((length, local)), whole((length, local)), whole((8, local))],
            scratch_shapes=[
                pltpu.VMEM((length, local), BF16),
                pltpu.VMEM((length, local), BF16),
                pltpu.VMEM((local, length), BF16),
                pltpu.VMEM((length, local), F32),
                pltpu.VMEM((length, local), F32),
                pltpu.VMEM((rows, local), BF16),
                pltpu.VMEM((8 * groups, rows), F32),
                pltpu.VMEM((local, STACK * tile), F32),
                pltpu.VMEM((rows, local), F32),
                pltpu.SemaphoreType.DMA,
            ],
        ),
        out_shape=[shape_of(rows, local), shape_of(length, local), shape_of(length, local), shape_of(8, local, dtype=F32)],
        compiler_params=params_of(),
        cost_estimate=cost(24 * rows * length * local, 2 * length * local * 8),
        name="attend_back",
    )(places, limits, *ins, *key_parts, *value_parts, *deps)


def joint_back_kernel(count, *refs):
    w_ref = refs[count]
    total = None
    for index in range(count):
        term = dot_nt(refs[index][...], w_ref[3 - count + index])
        total = term if total is None else total + term
    put(refs[count + 1 :], total.astype(BF16))


def joint_back_call(grads, offset, rows, w_joint, deps=()):
    width, local = w_joint.shape[1:]
    half = rows // 2
    tile = min(512, half)
    first = offset // tile
    return pl.pallas_call(
        waiting(functools.partial(joint_back_kernel, len(grads)), len(grads) + 1, deps),
        grid=(rows // tile,),
        in_specs=[pl.BlockSpec((tile, local), lambda r: (first + r, 0))] * len(grads)
        + [whole(w_joint.shape)]
        + anywhere(len(deps)),
        out_specs=halves_of(tile, half // tile, width),
        out_shape=[shape_of(half, width)] * 2,
        compiler_params=params_of(),
        cost_estimate=cost(2 * rows * width * local * len(grads), 2 * rows * (width + 3 * local) + 2 * w_joint.size),
        name="joint_projection_back",
    )(*grads, w_joint, *deps)


def rear_kernel(q_ref, k_ref, v_ref, w_ref, g0_ref, g1_ref, slope_ref, up_ref, down_ref, first0_ref, first1_ref, part0_ref, part1_ref):
    total = dot_nt(q_ref[...], w_ref[0]) + dot_nt(k_ref[...], w_ref[1]) + dot_nt(v_ref[...], w_ref[2])
    put((first0_ref, first1_ref), total.astype(BF16))
    upstream = pick((g0_ref, g1_ref))
    total = None
    for start in range(0, up_ref.shape[1], 512):
        cut = pl.ds(start, 512)
        d_active = dot_nt(upstream, down_ref[cut, :])
        d_hidden = (d_active * slope_ref[:, cut].astype(F32)).astype(BF16)
        term = dot_nt(d_hidden, up_ref[:, cut])
        total = term if total is None else total + term
    put((part0_ref, part1_ref), total.astype(BF16))


def rear_call(grads, w_joint, pair, slope, w_up, w_down, moves, moved, name, number):
    rows, width = pair[0].shape
    local = w_joint.shape[2]
    units = w_up.shape[1]
    tile = min(512, rows)
    halves = halves_of(tile, rows // tile, width)
    outs = pl.pallas_call(
        carrying(rear_kernel, 9, 4, moves),
        grid=(2 * rows // tile,),
        in_specs=[rows_of(tile, local)] * 3
        + [whole(w_joint.shape)]
        + halves
        + [rows_of(tile, units), whole(w_up.shape), whole(w_down.shape)]
        + anywhere(len(moves)),
        out_specs=halves + halves + anywhere(len(moves)),
        out_shape=[shape_of(rows, width)] * 4 + [shape_of(*x.shape) for x in moved],
        scratch_shapes=carrier_semaphores(len(moves)),
        compiler_params=params_of(collective_id=number, has_side_effects=True),
        cost_estimate=cost(4 * rows * width * (3 * local + 2 * units), 4 * w_up.size + 16 * rows * width),
        name=name,
    )(*grads, w_joint, *pair, slope, w_up, w_down, *moved)
    return outs[:2], outs[2:4], outs[4:]


def norm_back_kernel(firsts, h_ref, g_ref, gains_ref, *refs):
    first_refs, second_refs, (out_ref, sums_ref) = refs[:firsts], refs[firsts:-2], refs[-2:]

    @pl.when(pl.program_id(0) == 0)
    def _():
        sums_ref[...] = jnp.zeros_like(sums_ref)

    scaled, inverse = normalize(h_ref[...].astype(F32))
    upstream = g_ref[...].astype(F32)
    d_first = sum(ref[...].astype(F32) for ref in first_refs)
    d_second = sum(ref[...].astype(F32) for ref in second_refs)
    for row, term in enumerate((d_first * scaled, d_first, d_second * scaled, d_second, upstream)):
        sums_ref[row : row + 1, :] += jnp.sum(term, axis=0, keepdims=True)
    d_scaled = d_first * gains_ref[0:1] + d_second * gains_ref[1:2]
    middle = jnp.mean(d_scaled, axis=-1, keepdims=True)
    along = jnp.mean(d_scaled * scaled, axis=-1, keepdims=True)
    out_ref[...] = (upstream + inverse * (d_scaled - middle - scaled * along)).astype(BF16)


def norm_back_call(h, g, firsts, seconds, gains, deps=()):
    rows, width = h.shape
    tile = min(128, rows)
    one = rows_of(tile, width)
    return pl.pallas_call(
        waiting(functools.partial(norm_back_kernel, len(firsts)), 3 + len(firsts) + len(seconds), deps),
        grid=(rows // tile,),
        in_specs=[one, one, whole(gains.shape)] + [one] * (len(firsts) + len(seconds)) + anywhere(len(deps)),
        out_specs=[one, whole((8, width))],
        out_shape=[shape_of(rows, width), shape_of(8, width, dtype=F32)],
        compiler_params=params_of(),
        cost_estimate=cost(20 * rows * width, 2 * rows * width * 8),
        name="norm_back",
    )(h, g, gains, *firsts, *seconds, *deps)


def merge_kernel(h_ref, a0_ref, a1_ref, f0_ref, f1_ref, shifts_ref, out_ref, sums_ref):
    @pl.when(pl.program_id(0) == 0)
    def _():
        sums_ref[...] = jnp.zeros_like(sums_ref)

    state = h_ref[...].astype(F32)
    attention = a0_ref[...].astype(F32) + a1_ref[...].astype(F32) + shifts_ref[0:1]
    feedforward = f0_ref[...].astype(F32) + f1_ref[...].astype(F32) + shifts_ref[1:2]
    out_ref[...] = (state + attention + feedforward).astype(BF16)
    for row, term in enumerate((state, attention, feedforward)):
        sums_ref[row : row + 1, :] += jnp.sum(term * term, axis=0, keepdims=True)


def merge_call(h, attn_pair, ffn_pair, shifts, deps=()):
    rows, width = h.shape
    tile = min(128, rows)
    one = rows_of(tile, width)
    return pl.pallas_call(
        waiting(merge_kernel, 6, deps),
        grid=(rows // tile,),
        in_specs=[one] * 5 + [whole(shifts.shape)] + anywhere(len(deps)),
        out_specs=[one, whole((8, width))],
        out_shape=[shape_of(rows, width), shape_of(8, width, dtype=F32)],
        compiler_params=params_of(),
        cost_estimate=cost(10 * rows * width, 2 * rows * width * 6),
        name="merge",
    )(h, *attn_pair, *ffn_pair, shifts, *deps)


def tn(a, b):
    return lax.dot_general(a, b, (((0,), (0,)), ((), ())), preferred_element_type=F32)


def slope_kernel(count, terms, *refs):
    lefts = [jnp.concatenate([ref[...] for ref in refs[t * count : (t + 1) * count]], axis=1) for t in range(terms)]
    rights = refs[terms * count : terms * (count + 1)]
    out_ref = refs[-1]
    share = lefts[0].shape[1] // count
    total = sum(tn(left, right[...]) for left, right in zip(lefts, rights)).astype(BF16)
    for index in range(count):
        out_ref[index] = total[index * share : (index + 1) * share]


def slope_call(owners, terms, width, place, name, buffer=None, deps=()):
    share = terms[0][0].shape[1] // owners
    columns = terms[0][1].shape[1]
    count = 4
    steps = owners // count
    ins, specs = [], []
    for left, _, _ in terms:
        for index in range(count):
            ins.append(left)
            specs.append(pl.BlockSpec((left.shape[0], share), functools.partial(lambda i, r: (0, count * r + i), index)))
    for left, right, row in terms:
        ins.append(right)
        specs.append(pl.BlockSpec((left.shape[0], columns), functools.partial(lambda i, r: (i, 0), row)))
    behind = ((buffer,) if buffer is not None else ()) + tuple(deps)
    return pl.pallas_call(
        waiting(functools.partial(slope_kernel, count, len(terms)), len(ins), behind),
        grid=(steps,),
        in_specs=specs + anywhere(len(behind)),
        out_specs=pl.BlockSpec((count, share, columns), lambda r: (r, 0, place // columns)),
        out_shape=shape_of(owners, share, width),
        input_output_aliases={len(ins): 0} if buffer is not None else {},
        compiler_params=params_of(),
        cost_estimate=cost(
            sum(2 * a.size * columns for a, _, _ in terms),
            sum(2 * (a.size + a.shape[0] * columns) for a, _, _ in terms) + 2 * owners * share * columns,
        ),
        name=name,
    )(*ins, *behind)


def joint_slope_kernel(count, owners_ref, *refs):
    near = jnp.concatenate([ref[...] for ref in refs[:count]], axis=1)
    far = jnp.concatenate([ref[...] for ref in refs[count : 2 * count]], axis=1)
    q_ref, k0_ref, k1_ref, v0_ref, v1_ref = refs[2 * count : 2 * count + 5]
    outs = refs[2 * count + 5 :]
    share = near.shape[1] // count
    totals = (
        tn(near, q_ref[...]),
        tn(near, k0_ref[...]) + tn(far, k1_ref[...]),
        tn(near, v0_ref[...]) + tn(far, v1_ref[...]),
    )
    for out0_ref, out1_ref, total in zip(outs[0::2], outs[1::2], totals):
        low = total.astype(BF16)
        first = pl.program_id(0) < pl.num_programs(0) // 2
        for ref, here in ((out0_ref, first), (out1_ref, jnp.logical_not(first))):

            @pl.when(here)
            def _():
                for index in range(count):
                    ref[index] = low[index * share : (index + 1) * share]


def joint_slope_call(owners, normals, grads, deps):
    total = owners.shape[0]
    rows, width = normals[0].shape
    share = width // total
    local = grads[0].shape[1]
    count = 2
    ins, specs = [], []
    for normal in normals:
        for index in range(count):
            ins.append(normal)
            specs.append(pl.BlockSpec((rows, share), functools.partial(lambda i, r, o: (0, o[count * r + i]), index)))
    for grad, row in ((grads[0], 0), (grads[1], 0), (grads[1], 1), (grads[2], 0), (grads[2], 1)):
        ins.append(grad)
        specs.append(pl.BlockSpec((rows, local), functools.partial(lambda i, r, o: (i, 0), row)))
    outs = pl.pallas_call(
        waiting(functools.partial(joint_slope_kernel, count), 1 + len(ins), deps),
        grid_spec=pltpu.PrefetchScalarGridSpec(
            num_scalar_prefetch=1,
            grid=(total // count,),
            in_specs=specs + anywhere(len(deps)),
            out_specs=halves_of(count, total // count // 2, share, local) * 3,
        ),
        out_shape=[shape_of(total // 2, share, local)] * 6,
        compiler_params=params_of(),
        cost_estimate=cost(10 * rows * width * local, 16 * rows * width),
        name="joint_slope",
    )(owners, *ins, *deps)
    return [(outs[2 * t], outs[2 * t + 1]) for t in range(3)]


def swap_core(shard):
    return lax.ppermute(shard, "tp", [(0, 1), (1, 0)])


def swap_ctx(shard, mask):
    return lax.ppermute(shard, "ctx", [(c, c ^ mask) for c in range(lax.axis_size("ctx"))])


def next_section(shard, by):
    size = lax.axis_size("section")
    return lax.ppermute(shard, "section", [(s, s + by) for s in range(size) if 0 <= s + by < size])


def mask_order(masks):
    order = [0]
    for mask in reversed(masks):
        order = order + [value ^ mask for value in order]
    return order


class Reduction:
    def __init__(self, kept, sent, masks):
        self.kept, self.masks = kept, list(masks)
        self.total = None
        self.sent = sent
        self.arrived = swap_ctx(sent, self.masks[0])

    def go_on(self):
        if self.total is not None:
            return self
        total = self.kept.astype(F32) + self.arrived.astype(F32)
        self.masks = self.masks[1:]
        if not self.masks:
            self.total = total[0]
            self.sent = self.arrived = self.total
            return self
        half = total.shape[0] // 2
        self.kept = total[:half].astype(BF16)
        self.sent = total[half:].astype(BF16)
        self.arrived = swap_ctx(self.sent, self.masks[0])
        return self


def on_device(
    tokens,
    cotangent,
    block_order,
    first_gain,
    first_bias,
    second_gain,
    second_bias,
    joint_weight,
    joint_bias,
    output_weight,
    output_bias,
    up_weight,
    up_bias,
    down_weight,
    down_bias,
):
    section = lax.axis_index("section")
    sections = lax.axis_size("section")
    ctx = lax.axis_index("ctx")
    ctx_size = lax.axis_size("ctx")
    core = lax.axis_index("tp")
    seqs, local_len, width = tokens.shape
    block = local_len // 2
    chips = ctx_size // seqs
    seq, member = ctx // chips, ctx % chips
    rows = seqs * block
    chip_rows = 2 * rows
    length = chips * chip_rows
    seq_masks = [chips << b for b in range((seqs - 1).bit_length())]
    member_masks = [1 << b for b in range((chips - 1).bit_length())]

    k, u, a = jnp.meshgrid(jnp.arange(chips), jnp.arange(2), jnp.arange(seqs), indexing="ij")
    stored = (2 * ((seq ^ a) * chips + (member ^ k)) + (core ^ u)).reshape(-1)
    places = block_order[stored]
    spots = (places[:, None] * block + jnp.arange(block, dtype=jnp.int32)).reshape(-1)
    exponent = jnp.arange(ROT // 2, dtype=F32) * (2.0 / ROT)
    inverse = jnp.power(jnp.float32(ROTARY_BASE), -exponent)
    turns = spots.astype(F32)[:, None] * inverse[None, :]
    cosine, sine = jnp.cos(turns), jnp.sin(turns)
    rest = jnp.zeros((length, HEAD - ROT), F32)
    table = (
        jnp.tile(jnp.concatenate([cosine, cosine, rest + 1.0], 1), (1, 128 // HEAD)),
        jnp.tile(jnp.concatenate([sine, sine, rest], 1), (1, 128 // HEAD)),
    )

    tile = max(block, 128)
    tile_places = places[: chip_rows // block].reshape(-1, tile // block)
    lowest, highest = jnp.min(tile_places, 1), jnp.max(tile_places, 1)
    limits = jnp.stack([(lowest * block + 1) // KEY_TILE, (highest * block + block - 1) // KEY_TILE + 1], 1)

    gain_one, shift_one, gain_two, shift_two = first_gain, first_bias, second_gain, second_bias
    w_joint, b_joint = joint_weight[0], joint_bias[0]
    w_output, b_output = output_weight[0], output_bias
    w_up, b_up = up_weight[0], up_bias
    w_down, b_down = down_weight[0], down_bias
    gains = jnp.concatenate([gain_one, gain_two], 0)
    norms = jnp.concatenate([gain_one, shift_one, gain_two, shift_two], 0)
    shifts = jnp.concatenate([b_output, b_down], 0)

    def plane_parts(values):
        mine = lax.dynamic_slice_in_dim(values, core * block, block, 1)
        return [lax.dynamic_index_in_dim(mine, seq ^ shift, 0, keepdims=False) for shift in range(seqs)]

    def from_planes(values):
        parts = values.reshape(seqs, block, width)
        return [parts[s] if s == 0 else swap_ctx(parts[s], s * chips) for s in range(seqs)]

    def in_order(parts):
        parts = jnp.stack(parts)
        both = jnp.stack([parts, swap_core(parts)], 1)
        ordered = [
            lax.dynamic_index_in_dim(lax.dynamic_index_in_dim(both, s ^ seq, 0, False), v ^ core, 0, False)
            for s in range(seqs)
            for v in range(2)
        ]
        return jnp.stack(ordered).reshape(1, seqs, local_len, width)

    def paired(parts):
        count = len(parts) // 2
        return tuple(x[0] if count == 1 else jnp.concatenate(x, 0) for x in (parts[:count], parts[count:]))

    def forward(own, save, moves, moved, name, number):
        chip = (own, swap_core(own))
        moves = [("ctx", k) for k in range(1, chips)] + moves
        outs, arrived = front_call(
            chip, norms, w_joint, b_joint, table, w_up, b_up, w_down, save, moves, [own] * (chips - 1) + moved, name, number
        )
        normal, keys, values, queries, ffn0, ffn1, *kept_ffn = outs
        others, arrived = arrived[: chips - 1], arrived[chips - 1 :]
        key_parts, value_parts, normal_parts = [keys], [values], [normal]
        if chips > 1:
            rest = paired([x for other in others for x in (other, swap_core(other))])
            far_normal, far_keys, far_values = joint_call(
                rest, gain_one, shift_one, w_joint, b_joint, table, chip_rows
            )
            key_parts.append(far_keys)
            value_parts.append(far_values)
            normal_parts.append(far_normal)
        attn0, attn1, mixture, lse = attend_call(queries, key_parts, value_parts, places, limits, w_output, block)
        result, moments = merge_call(own, (attn0, swap_core(attn1)), (ffn0, swap_core(ffn1)), shifts)
        return result, moments, (normal_parts, queries, key_parts, value_parts, mixture, lse, *kept_ffn), arrived

    def attention_back(g_pair, kept, deps=()):
        normal_parts, queries, key_parts, value_parts, mixture, lse, second_in, active, slope = kept
        return attend_back_call(
            queries, g_pair, mixture, lse, key_parts, value_parts, places, limits, w_output, table, block, deps
        )

    def far_back(d_keys, d_values, deps=()):
        if chips == 1:
            return []
        far = joint_back_call([d_keys, d_values], chip_rows, length - chip_rows, w_joint, deps)
        if chips > 2:
            far = jnp.concatenate(far, 0).reshape(chips - 1, 2, rows, width)
            far = far[:, 0], far[:, 1]
        sums = (far[0].astype(F32) + swap_core(far[1]).astype(F32)).astype(BF16).reshape(chips - 1, rows, width)
        return [sums[k - 1] for k in range(1, chips)]

    others = [("ctx", k) for k in range(1, chips)]
    planes = [("ctx", s * chips) for s in range(1, seqs)]
    token_parts = plane_parts(tokens)
    token_rows = jnp.concatenate([token_parts[0]] + [swap_ctx(token_parts[s], s * chips) for s in range(1, seqs)], 0)
    g_parts = plane_parts(cotangent)
    own = token_rows
    for tick in range(sections):
        first = tick == 0
        result, moments, kept, arrived = forward(
            own, tick == sections - 1, planes if first else [], g_parts[1:] if first else [], "front" + str(tick), tick
        )
        if first:
            g_rows = jnp.concatenate([g_parts[0], *arrived], 0)
        if tick < sections - 1:
            own = jnp.where(section == 0, token_rows, next_section(result, 1))
    out_parts = from_planes(result)
    moments = jnp.sum(moments[:3], axis=1)
    normal_parts, queries, key_parts, value_parts, mixture, lse, second_in, active, slope = kept
    g_own = g_rows
    for tick in range(sections - 1):
        g_pair = (g_own, swap_core(g_own))
        d_queries, d_keys, d_values, _ = attention_back(g_pair, kept)
        sums = far_back(d_keys, d_values, tuple(out_parts) if tick == 0 else ())
        near, second, arrivals = rear_call(
            (d_queries, d_keys, d_values), w_joint, g_pair, slope, w_up, w_down, others, sums, "rear" + str(tick), sections + tick
        )
        firsts = [near[0], swap_core(near[1]), *arrivals]
        d_own, _ = norm_back_call(own, g_own, firsts, [second[0], swap_core(second[1])], gains)
        g_own = jnp.where(section == sections - 1, g_rows, next_section(d_own, -1))
    section_out = in_order(out_parts)

    masks = member_masks + seq_masks
    owners = jnp.stack([ctx ^ m for m in mask_order(masks)]).astype(jnp.int32)
    local = w_output.shape[0]
    units = w_up.shape[1]
    share = width // ctx_size
    g_pair = (g_own, swap_core(g_own))
    by_blocks = share % 128 == 0 and chips == 2
    g_chip = g_pair if by_blocks else jnp.concatenate(g_pair, 0)
    if by_blocks:
        terms = [(g_pair[0], active, 0), (g_pair[1], active, 1)]
        slopes = slope_call(ctx_size, terms, 2 * units + local, 0, "down_slope")
        terms = [(g_pair[0], mixture, 0), (g_pair[1], mixture, 1)]
        slopes = slope_call(ctx_size, terms, 2 * units + local, 2 * units, "output_slope", slopes)
    second0, second1, d_hidden, up_sums = ffn_back_call(g_pair, slope, w_up, w_down, (slopes,) if by_blocks else ())
    if by_blocks:
        slopes = slope_call(ctx_size, [(second_in, d_hidden, 0)], 2 * units + local, units, "up_slope", slopes)
    else:
        pairs = ((g_chip, active), (second_in, d_hidden), (g_chip, mixture))
        slopes = jnp.concatenate([tn(a, b).astype(BF16).reshape(ctx_size, share, -1) for a, b in pairs], 2)
    slope_total = lax.psum_scatter(slopes, "ctx", scatter_dimension=0, tiled=False).astype(F32)
    d_queries, d_keys, d_values, joint_sums = attention_back(g_pair, kept, (slopes,))
    sums = far_back(d_keys, d_values)
    near = joint_back_call([d_queries, d_keys, d_values], 0, chip_rows, w_joint, tuple(sums))
    arrivals = [swap_ctx(part, k + 1) for k, part in enumerate(sums)]
    if by_blocks:
        halves = joint_slope_call(owners, normal_parts, (d_queries, d_keys, d_values), (near[0],))
    else:
        halves = []
        for grad in (d_queries, d_keys, d_values):
            piece = tn(normal_parts[0], grad[:chip_rows])
            if chips > 1 and grad is not d_queries:
                piece = piece + tn(normal_parts[1], grad[chip_rows:])
            piece = jnp.take(piece.astype(BF16).reshape(ctx_size, share, local), owners, axis=0)
            halves.append((piece[: ctx_size // 2], piece[ctx_size // 2 :]))
    joints = [Reduction(*pair, masks) for pair in halves]
    firsts = [near[0], swap_core(near[1]), *arrivals]
    seconds = [second0, swap_core(second1)]
    d_own, norm_sums = norm_back_call(own, g_own, firsts, seconds, gains, (joints[0].sent,))
    section_in_grad = in_order(from_planes(d_own))
    for _ in masks:
        for reduction in joints:
            reduction.go_on()
    down_total = slope_total[:, :units].T
    up_total = slope_total[:, units : 2 * units]
    output_total = slope_total[:, 2 * units :].T
    joint_total = jnp.stack([r.total for r in joints])

    both = jnp.concatenate([norm_sums[:5].reshape(-1), moments])
    both = both + swap_core(both)
    small = jnp.concatenate([both, joint_sums[:3].reshape(-1), up_sums.reshape(-1)])
    for mask in masks:
        small = small + swap_ctx(small, mask)
    norm_total = small[: 5 * width].reshape(5, 1, width)
    moment_total = small[5 * width : 5 * width + 3]
    joint_shift = small[5 * width + 3 : 5 * width + 3 + 3 * local].reshape(1, 3, local)
    up_shift = small[5 * width + 3 + 3 * local :].reshape(1, units)
    root_means = jnp.sqrt(moment_total / (length * seqs * width))
    return (
        section_out,
        section_in_grad,
        norm_total[0],
        norm_total[1],
        norm_total[2],
        norm_total[3],
        joint_total[None],
        joint_shift,
        output_total[None],
        norm_total[4],
        up_total[None],
        up_shift,
        down_total[None],
        norm_total[4],
        root_means[None],
    )


def solution(mesh):
    in_specs = (
        P(None, "ctx", None),
        P(None, "ctx", None),
        P(),
        P("section", None),
        P("section", None),
        P("section", None),
        P("section", None),
        P("section", None, None, "tp"),
        P("section", None, "tp"),
        P("section", "tp", None),
        P("section", None),
        P("section", None, "tp"),
        P("section", "tp"),
        P("section", "tp", None),
        P("section", None),
    )
    out_specs = (
        P("section", None, "ctx", None),
        P("section", None, "ctx", None),
        P("section", None),
        P("section", None),
        P("section", None),
        P("section", None),
        P("section", None, "ctx", "tp"),
        P("section", None, "tp"),
        P("section", "tp", "ctx"),
        P("section", None),
        P("section", "ctx", "tp"),
        P("section", "tp"),
        P("section", "tp", "ctx"),
        P("section", None),
        P("section", None),
    )
    return jax.shard_map(
        on_device, mesh=mesh, in_specs=in_specs, out_specs=out_specs, check_vma=False
    )
```

time: 847 us -> 716 us (0.85)
  local copies, waits for them, and re-layouts: 107 us -> 33.3 us
  Pallas kernels: 335 us -> 367 us
  matrix products: 31.3 us -> 0 us
  other arithmetic: 61.3 us -> 32.7 us
  waiting for transfers between devices: 252 us -> 225 us
  starting transfers between devices: 49.6 us -> 32.9 us
  between operations: 2.14 us -> 15.1 us
    ppermute x31 -> x22, waiting for transfers between devices: 248 us -> 155 us  [swap_ctx(): lax.ppermute(shard, 'ctx', [(c, c ^ mask) for c in range(lax.axis_size('c...]
    ppermute x2, waiting for transfers between devices: 0.76 us -> 48.9 us  [next_section(): lax.ppermute(shard, 'section', [(s, s + by) for s in range(size) if 0 <=...]
    pallas_call x18 -> x21, Pallas kernels: 335 us -> 367 us  [the longest x2 99.5 us: attend_back_call(): pl.pallas_call(waiting(functools.partial(attend_back_kernel, block, tile,...]
    dot_general x8 -> x0, matrix products: 31.3 us -> none  [tn(): lax.dot_general(a, b, (((0,), (0,)), ((), ())), preferred_element_type=F32)]
    slice x22 -> x6, local copies, waits for them, and re-layouts: 25.7 us -> 2.15 us  [go_on(): self.sent = total[half:].astype(BF16)]
    another operation x23 -> x5, local copies, waits for them, and re-layouts: 25.8 us -> 3.43 us  [the longest x2 1.41 us: on_device(): jnp.tile(jnp.concatenate([sine, sine, rest], 1), (1, 128 // HEAD))]
    ppermute x19, waiting for transfers between devices: 3.27 us -> 21.8 us  [swap_core(): return lax.ppermute(shard, 'tp', [(0, 1), (1, 0)])]
    ppermute x31 -> x22, starting transfers between devices: 39.7 us -> 24.9 us  [swap_ctx(): lax.ppermute(shard, 'ctx', [(c, c ^ mask) for c in range(lax.axis_size('c...]
  transfers between devices with their start and end apart: 52 -> 44, of which waited for: 22 -> 25; matrix products, arithmetic and copies ran while one was open for 21% -> 6% of each run, Pallas kernels for 30% -> 29%
where the time goes in v2:
time: 716 us; the launch traced here: 707 us
  Pallas kernels  367 us (51%)
  waiting for transfers between devices  225 us (31%)
  local copies, waits for them, and re-layouts  33.3 us (5%)
  starting transfers between devices  32.9 us (5%)
  other arithmetic  32.7 us (5%)
  between operations  15.1 us (2%)
    ppermute x22, waiting for transfers between devices, swap_ctx(): lax.ppermute(shard, 'ctx', [(c, c ^ mask) for c in range(lax.axis_size('c...  155 us
    pallas_call x2, Pallas kernels, attend_back_call(): pl.pallas_call(waiting(functools.partial(attend_back_kernel, block, tile,...  99.5 us
    pallas_call x2, Pallas kernels, front_call(): pl.pallas_call(carrying(functools.partial(front_kernel, save), 2 + len(in...  73.3 us
    pallas_call x2, Pallas kernels, attend_call(): pl.pallas_call(waiting(functools.partial(attend_kernel, block, tile, len(...  52 us
    ppermute x2, waiting for transfers between devices, next_section(): lax.ppermute(shard, 'section', [(s, s + by) for s in range(size) if 0 <=...  48.9 us
    pallas_call x1, Pallas kernels, rear_call(): pl.pallas_call(carrying(rear_kernel, 9, 4, moves), grid=(2 * rows // tile...  34 us
    ppermute x22, starting transfers between devices, swap_ctx(): lax.ppermute(shard, 'ctx', [(c, c ^ mask) for c in range(lax.axis_size('c...  24.9 us
    pallas_call x3, Pallas kernels, slope_call(): pl.pallas_call(waiting(functools.partial(slope_kernel, count, len(terms))...  22.5 us
  transfers between devices with their start and end apart: 44, of which 25 were waited for; matrix products, arithmetic and copies ran while one was open for 6% of the time, Pallas kernels for 29%

profile of v2, /device:TPU:0, one launch (start us, length us, event | category | flops | bytes accessed | tf_op | source)
XLA Modules:
  0.0 706.8 jit_solution(13438437329779186146)
XLA Ops:
  15.8 7.2 %collective-permute-done = bf16[128,1024]{1,0:T(8,128)(2,1)S(1)} collective-permute-done((bf16[128,1024]{1,0:T(8,128)(2,1)S(1)}, bf16[128,1024]{1,0:T(8,128)(2,1)S(1)}, u32[]{:S(2)}, u32[]{:S(2)}) %collective-permute-start) | collective-permute-done | bytes 262176 | tf_op jit(solution)/shard_map/ppermute | solution.py:756
  23.0 10.3 %collective-permute-done.1 = bf16[128,1024]{1,0:T(8,128)(2,1)S(1)} collective-permute-done((bf16[128,1024]{1,0:T(8,128)(2,1)S(1)}, bf16[128,1024]{1,0:T(8,128)(2,1)S(1)}, u32[]{:S(2)}, u32[]{:S(2)}) %collective-permute-start.1) | collective-permute-done | bytes 262176 | tf_op jit(solution)/shard_map/ppermute | solution.py:756
  40.1 38.6 %front0.1 = (bf16[1024,1024]{1,0:T(8,128)(2,1)}, bf16[1024,512]{1,0:T(8,128)(2,1)}, bf16[1024,512]{1,0:T(8,128)(2,1)}, bf16[1024,512]{1,0:T(8,128)(2,1)}, bf16[5...) custom-call(bf16[512,1024]{1,0:T(8,128)(2,1)} %copy-done.5, ...), custom_call_target="tpu_custom_call" | custom-call | flops 11811160064 | bytes 16777216 | tf_op jit(solution)/shard_map/front0/pallas_call | solution.py:224
  82.6 7.6 %joint_projection.2 = (bf16[1024,1024]{1,0:T(8,128)(2,1)}, bf16[1024,512]{1,0:T(8,128)(2,1)}, bf16[1024,512]{1,0:T(8,128)(2,1)}) custom-call(bf16[512,1024]{1,0:T(8,128)(2,1)} %get-tuple-element.81.refs_0_, bf16[512,1024]{1,0:T(8,128)(2,1)} %copy-done.48, f32[1,1024]{1,0:T(1,128)} %refs_2_.3, f32[1,1024]{1,0:T(1,128)} %refs_3_.3, ...), custom_call_target="tpu_custom_call" | custom-call | flops 2147483648 | bytes 7340032 | tf_op jit(solution)/shard_map/joint_projection/pallas_call | solution.py:162
  90.2 25.9 %attend.2 = (bf16[512,1024]{1,0:T(8,128)(2,1)}, bf16[512,1024]{1,0:T(8,128)(2,1)}, bf16[1024,512]{1,0:T(8,128)(2,1)}, f32[8,2,512]{2,1,0:T(2,128)}) custom-call(s32[16]{0:T(128)} %copy-done.46, s32[8,2]{1,0:T(8,128)} %copy.56.refs_1_, bf16[1024,512]{1,0:T(8,128)(2,1)} %get-tuple-element.79.refs_2_, bf16[512,1024]{1,0:T(8,128)(2,1)} %bitcast.162, ...), custom_call_target="tpu_custom_call" | custom-call | flops 12884901888 | bytes 8388608 | tf_op jit(solution)/shard_map/attend/pallas_call | solution.py:383
  120.0 4.6 merge.2
  128.0 22.9 %collective-permute-done.7 = bf16[512,1024]{1,0:T(8,128)(2,1)S(1)} collective-permute-done((bf16[512,1024]{1,0:T(8,128)(2,1)}, bf16[512,1024]{1,0:T(8,128)(2,1)S(1)}, u32[]{:S(2)}, u32[]{:S(2)}) %collective-permute-start.7) | collective-permute-done | bytes 1048608 | tf_op jit(solution)/shard_map/ppermute | solution.py:761
  155.2 34.7 %front1.1 = (bf16[1024,1024]{1,0:T(8,128)(2,1)}, bf16[1024,512]{1,0:T(8,128)(2,1)}, bf16[1024,512]{1,0:T(8,128)(2,1)}, bf16[1024,512]{1,0:T(8,128)(2,1)}, bf16[5...) custom-call(bf16[512,1024]{1,0:T(8,128)(2,1)} %copy-done.4, ...), custom_call_target="tpu_custom_call" | custom-call | flops 11811160064 | bytes 16777216 | tf_op jit(solution)/shard_map/front1/pallas_call | solution.py:224
  193.8 7.6 %joint_projection.3 = (bf16[1024,1024]{1,0:T(8,128)(2,1)}, bf16[1024,512]{1,0:T(8,128)(2,1)}, bf16[1024,512]{1,0:T(8,128)(2,1)}) custom-call(bf16[512,1024]{1,0:T(8,128)(2,1)} %get-tuple-element.92.refs_0_, bf16[512,1024]{1,0:T(8,128)(2,1)} %copy-done.50, f32[1,1024]{1,0:T(1,128)} %refs_2_.3, f32[1,1024]{1,0:T(1,128)} %refs_3_.3, ...), custom_call_target="tpu_custom_call" | custom-call | flops 2147483648 | bytes 7340032 | tf_op jit(solution)/shard_map/joint_projection/pallas_call | solution.py:162
  201.4 26.1 %attend.3 = (bf16[512,1024]{1,0:T(8,128)(2,1)}, bf16[512,1024]{1,0:T(8,128)(2,1)}, bf16[1024,512]{1,0:T(8,128)(2,1)}, f32[8,2,512]{2,1,0:T(2,128)}) custom-call(s32[16]{0:T(128)} %copy-done.46, s32[8,2]{1,0:T(8,128)} %copy.56.refs_1_, bf16[1024,512]{1,0:T(8,128)(2,1)} %get-tuple-element.90.refs_2_, bf16[512,1024]{1,0:T(8,128)(2,1)} %bitcast.163, ...), custom_call_target="tpu_custom_call" | custom-call | flops 12884901888 | bytes 8388608 | tf_op jit(solution)/shard_map/attend/pallas_call | solution.py:383
  231.4 4.8 merge.3
  243.6 49.4 %attend_back.2 = (bf16[1024,512]{1,0:T(8,128)(2,1)}, bf16[2048,512]{1,0:T(8,128)(2,1)}, bf16[2048,512]{1,0:T(8,128)(2,1)}, f32[8,512]{1,0:T(8,128)}) custom-call(s32[16]{0:T(128)} %copy-done.46, s32[8,2]{1,0:T(8,128)} %copy.56.refs_1_, bf16[1024,512]{1,0:T(8,128)(2,1)} %get-tuple-element.90.refs_2_, bf16[512,1024]{1,0:T(8,128)(2,1)} %copy-done.6, ...), custom_call_target="tpu_custom_call" | custom-call | flops 25769803776 | bytes 16777216 | tf_op jit(solution)/shard_map/attend_back/pallas_call | solution.py:496
  294.0 6.4 joint_projection_back.3
  305.7 34.0 %rear0.1 = (bf16[512,1024]{1,0:T(8,128)(2,1)}, bf16[512,1024]{1,0:T(8,128)(2,1)}, bf16[512,1024]{1,0:T(8,128)(2,1)}, bf16[512,1024]{1,0:T(8,128)(2,1)}, bf16[512,1024]{1,0:T(8,128)(2,1)}) custom-call(bf16[1024,512]{1,0:T(8,128)(2,1)} %get-tuple-element.106.refs_0_, bf16[2048,512]{1,0:T(8,128)(2,1)} %get-tuple-element.107.refs_0_.refs_1_, ...), custom_call_target="tpu_custom_call" | custom-call | flops 11811160064 | bytes 16777216 | tf_op jit(solution)/shard_map/rear0/pallas_call | solution.py:573
  345.2 6.1 norm_back.2
  352.6 26.0 %collective-permute-done.20 = bf16[512,1024]{1,0:T(8,128)(2,1)S(1)} collective-permute-done((bf16[512,1024]{1,0:T(8,128)(2,1)}, bf16[512,1024]{1,0:T(8,128)(2,1)S(1)}, u32[]{:S(2)}, u32[]{:S(2)}) %collective-permute-start.20) | collective-permute-done | bytes 1048608 | tf_op jit(solution)/shard_map/ppermute | solution.py:761
  382.8 9.4 %down_slope.1.refs_10_ = bf16[8,128,4608]{2,1,0:T(8,128)(2,1)} custom-call(bf16[512,1024]{1,0:T(8,128)(2,1)} %copy-done.2, bf16[512,1024]{1,0:T(8,128)(2,1)} %copy-done.2, bf16[512,1024]{1,0:T(8,128)(2,1)} %copy-done.2, bf16[512,1024]{1,0:T(8,128)(2,1)} %copy-done.2, bf16[512,1024]{1,0:T(8,128)(2,1)} %copy-done.3, bf16[512,1024]{1,0:T(8,128)(2,1)} %copy-done.3, ...), custom_call_target="tpu_custom_call" | custom-call | flops 4294967296 | bytes 10485760 | tf_op jit(solution)/shard_map/down_slope/pallas_call | solution.py:683
  396.4 16.5 %feed_forward_back.1 = (bf16[512,1024]{1,0:T(8,128)(2,1)}, bf16[512,1024]{1,0:T(8,128)(2,1)}, bf16[1024,2048]{1,0:T(8,128)(2,1)}, f32[1,2048]{1,0:T(1,128)}) custom-call(bf16[512,1024]{1,0:T(8,128)(2,1)} %copy-done.2, bf16[512,1024]{1,0:T(8,128)(2,1)} %copy-done.3, bf16[1024,2048]{1,0:T(8,128)(2,1)} %get-tuple-element.109.refs_6_.refs_2_, ...), custom_call_target="tpu_custom_call" | custom-call | flops 8589934592 | bytes 20971520 | tf_op jit(solution)/shard_map/feed_forward_back/pallas_call | solution.py:262
  413.0 8.8 %up_slope.1.refs_14_ = bf16[8,128,4608]{2,1,0:T(8,128)(2,1)} custom-call(bf16[1024,1024]{1,0:T(8,128)(2,1)} %get-tuple-element.118.refs_0_.refs_1_.refs_2_.refs_3_, bf16[1024,1024]{1,0:T(8,128)(2,1)} %get-tuple-element.118.refs_0_.refs_1_.refs_2_.refs_3_, ...), custom_call_target="tpu_custom_call", output_to_operand_aliasing={{}: (5, {})} | custom-call | flops 4294967296 | bytes 10485760 | tf_op jit(solution)/shard_map/up_slope/pallas_call | solution.py:683
  421.8 50.1 %attend_back.3 = (bf16[1024,512]{1,0:T(8,128)(2,1)}, bf16[2048,512]{1,0:T(8,128)(2,1)}, bf16[2048,512]{1,0:T(8,128)(2,1)}, f32[8,512]{1,0:T(8,128)}) custom-call(s32[16]{0:T(128)} %copy-done.46, s32[8,2]{1,0:T(8,128)} %copy.56.refs_1_, bf16[1024,512]{1,0:T(8,128)(2,1)} %get-tuple-element.90.refs_2_, bf16[512,1024]{1,0:T(8,128)(2,1)} %copy-done.2, ...), custom_call_target="tpu_custom_call" | custom-call | flops 25769803776 | bytes 16777216 | tf_op jit(solution)/shard_map/attend_back/pallas_call | solution.py:496
  471.9 6.5 joint_projection_back.4
  483.8 7.9 %joint_projection_back.5 = (bf16[512,1024]{1,0:T(8,128)(2,1)}, bf16[512,1024]{1,0:T(8,128)(2,1)}) custom-call(bf16[1024,512]{1,0:T(8,128)(2,1)} %get-tuple-element.121.refs_0_.refs_5_, bf16[2048,512]{1,0:T(8,128)(2,1)} %get-tuple-element.122.refs_0_.refs_1_.refs_6_.refs_7_, bf16[2048,512]{1,0:T(8,128)(2,1)} %get-tuple-element.123.refs_1_.refs_2_.refs_8_.refs_9_, ...), custom_call_target="tpu_custom_call" | custom-call | flops 3221225472 | bytes 8388608 | tf_op jit(solution)/shard_map/joint_projection_back/pallas_call | solution.py:539
  491.7 11.9 %joint_slope.1 = (bf16[4,128,512]{2,1,0:T(8,128)(2,1)}, bf16[4,128,512]{2,1,0:T(8,128)(2,1)}, bf16[4,128,512]{2,1,0:T(8,128)(2,1)}, bf16[4,128,512]{2,1,0:T(8,12...) custom-call(s32[8]{0:T(128)} %stack.116.refs_0_, ...), custom_call_target="tpu_custom_call" | custom-call | flops 5368709120 | bytes 16777216 | tf_op jit(solution)/shard_map/joint_slope/pallas_call | solution.py:735
  509.2 15.5 %collective-permute-done.34 = bf16[4,128,512]{2,1,0:T(8,128)(2,1)} collective-permute-done((bf16[4,128,512]{2,1,0:T(8,128)(2,1)}, bf16[4,128,512]{2,1,0:T(8,128)(2,1)}, u32[]{:S(2)}, u32[]{:S(2)}) %collective-permute-start.34) | collective-permute-done | bytes 524320 | tf_op jit(solution)/shard_map/ppermute | solution.py:756
  526.1 21.0 %collective-permute-done.37 = bf16[4,128,512]{2,1,0:T(8,128)(2,1)} collective-permute-done((bf16[4,128,512]{2,1,0:T(8,128)(2,1)}, bf16[4,128,512]{2,1,0:T(8,128)(2,1)}, u32[]{:S(2)}, u32[]{:S(2)}) %collective-permute-start.37) | collective-permute-done | bytes 524320 | tf_op jit(solution)/shard_map/ppermute | solution.py:756
  548.5 45.4 %collective-permute-done.40 = bf16[4,128,512]{2,1,0:T(8,128)(2,1)S(1)} collective-permute-done((bf16[4,128,512]{2,1,0:T(8,128)(2,1)}, bf16[4,128,512]{2,1,0:T(8,128)(2,1)S(1)}, u32[]{:S(2)}, u32[]{:S(2)}) %collective-permute-start.40) | collective-permute-done | bytes 524320 | tf_op jit(solution)/shard_map/ppermute | solution.py:756
  596.9 17.0 %collective-permute-done.38 = bf16[2,128,512]{2,1,0:T(8,128)(2,1)S(1)} collective-permute-done((bf16[2,128,512]{2,1,0:T(8,128)(2,1)S(1)}, bf16[2,128,512]{2,1,0:T(8,128)(2,1)S(1)}, u32[]{:S(2)}, u32[]{:S(2)}) %collective-permute-start.38) | collective-permute-done | bytes 262176 | tf_op jit(solution)/shard_map/ppermute | solution.py:756
  614.9 4.7 collective-permute-done.41
  623.1 6.4 norm_back.3
  639.3 6.6 collective-permute-done.26
  646.1 15.2 %collective-permute-done.27 = bf16[128,1024]{1,0:T(8,128)(2,1)S(1)} collective-permute-done((bf16[128,1024]{1,0:T(8,128)(2,1)}, bf16[128,1024]{1,0:T(8,128)(2,1)S(1)}, u32[]{:S(2)}, u32[]{:S(2)}) %collective-permute-start.27) | collective-permute-done | bytes 262176 | tf_op jit(solution)/shard_map/ppermute | solution.py:756
  664.9 4.9 collective-permute-done.39
  (274 shorter events, 131.8 us)
Async XLA Ops:
  7.2 687.1 %reduce-scatter.2.cloned.1.call-start = ((), (), s32[]{:S(2)}) async-start(), calls=%async_computation.1 | async-start | bytes 10616832 | tf_op jit(solution)/shard_map/reduce_scatter | solution.py:963
  8.8 14.2 %collective-permute-start = (bf16[128,1024]{1,0:T(8,128)(2,1)S(1)}, bf16[128,1024]{1,0:T(8,128)(2,1)S(1)}, u32[]{:S(2)}, u32[]{:S(2)}) collective-permute-start(bf16[128,1024]{1,0:T(8,128)(2,1)S(1)} %get-tuple-element.195), channel_id=1, source_target_pairs={{0,4},{2,6},{4,0},{6,2},{8,12},{10,14},{12,8},{14,10},{1,5},{3,7},... | collective-permute-start | bytes 786440 | tf_op jit(solution)/shard_map/ppermute | solution.py:756
  11.9 21.4 %collective-permute-start.1 = (bf16[128,1024]{1,0:T(8,128)(2,1)S(1)}, bf16[128,1024]{1,0:T(8,128)(2,1)S(1)}, u32[]{:S(2)}, u32[]{:S(2)}) collective-permute-start(bf16[128,1024]{1,0:T(8,128)(2,1)S(1)} %get-tuple-element.197), channel_id=1, source_target_pairs={{0,8},{2,10},{4,12},{6,14},{8,0},{10,2},{12,4},{14,6},{1,9},{3,11}... | collective-permute-start | bytes 786440 | tf_op jit(solution)/shard_map/ppermute | solution.py:756
  14.5 18.8 %collective-permute-start.2 = (bf16[128,1024]{1,0:T(8,128)(2,1)S(1)}, bf16[128,1024]{1,0:T(8,128)(2,1)S(1)}, u32[]{:S(2)}, u32[]{:S(2)}) collective-permute-start(bf16[128,1024]{1,0:T(8,128)(2,1)S(1)} %get-tuple-element.196), channel_id=1, source_target_pairs={{0,12},{2,14},{4,8},{6,10},{8,4},{10,6},{12,0},{14,2},{1,13},{3,15... | collective-permute-start | bytes 786440 | tf_op jit(solution)/shard_map/ppermute | solution.py:756
  33.3 6.7 collective-permute-start.3
  79.5 37.4 %collective-permute-start.6 = (bf16[512,1024]{1,0:T(8,128)(2,1)}, bf16[512,1024]{1,0:T(8,128)(2,1)S(1)}, u32[]{:S(2)}, u32[]{:S(2)}) collective-permute-start(bf16[512,1024]{1,0:T(8,128)(2,1)} %get-tuple-element.88), channel_id=1, source_target_pairs={{0,1},{1,0},{2,3},{3,2},{4,5},{5,4},{6,7},{7,6},{8,9},{9,8},{10,11... | collective-permute-start | bytes 3145736 | tf_op jit(solution)/shard_map/ppermute | solution.py:752
  124.6 26.4 %collective-permute-start.7 = (bf16[512,1024]{1,0:T(8,128)(2,1)}, bf16[512,1024]{1,0:T(8,128)(2,1)S(1)}, u32[]{:S(2)}, u32[]{:S(2)}) collective-permute-start(bf16[512,1024]{1,0:T(8,128)(2,1)} %get-tuple-element.89), channel_id=1, source_target_pairs={{0,16},{1,17},{2,18},{3,19},{4,20},{5,21},{6,22},{7,23},{8,24},{9,... | collective-permute-start | bytes 3145736 | tf_op jit(solution)/shard_map/ppermute | solution.py:761
  189.9 38.3 %collective-permute-start.11 = (bf16[512,1024]{1,0:T(8,128)(2,1)}, bf16[512,1024]{1,0:T(8,128)(2,1)S(1)}, u32[]{:S(2)}, u32[]{:S(2)}) collective-permute-start(bf16[512,1024]{1,0:T(8,128)(2,1)} %get-tuple-element.99), channel_id=1, source_target_pairs={{0,1},{1,0},{2,3},{3,2},{4,5},{5,4},{6,7},{7,6},{8,9},{9,8},{10,11... | collective-permute-start | bytes 3145736 | tf_op jit(solution)/shard_map/ppermute | solution.py:752
  227.8 14.9 %collective-permute-start.16 = (bf16[512,1024]{1,0:T(8,128)(2,1)S(1)}, bf16[512,1024]{1,0:T(8,128)(2,1)S(1)}, u32[]{:S(2)}, u32[]{:S(2)}) collective-permute-start(bf16[512,1024]{1,0:T(8,128)(2,1)S(1)} %pad_maximum_fusion.2.refs_3_.refs_4_.refs_1_), channel_id=1, source_target_pairs={{0,1},{1,0},{2,3},{3,2},{4,5},{5,4},{6,7},{7,6},{8,9},{9,8},{10,11... | collective-permute-start | bytes 3145736 | tf_op jit(solution)/shard_map/ppermute | solution.py:752
  238.3 54.8 %collective-permute-start.12 = (bf16[128,1024]{1,0:T(8,128)(2,1)S(1)}, bf16[128,1024]{1,0:T(8,128)(2,1)S(1)}, u32[]{:S(2)}, u32[]{:S(2)}) collective-permute-start(bf16[128,1024]{1,0:T(8,128)(2,1)S(1)} %get-tuple-element.208), channel_id=1, source_target_pairs={{0,4},{2,6},{4,0},{6,2},{8,12},{10,14},{12,8},{14,10},{1,5},{3,7},... | collective-permute-start | bytes 786440 | tf_op jit(solution)/shard_map/ppermute | solution.py:756
  238.9 54.2 %collective-permute-start.13 = (bf16[128,1024]{1,0:T(8,128)(2,1)S(1)}, bf16[128,1024]{1,0:T(8,128)(2,1)S(1)}, u32[]{:S(2)}, u32[]{:S(2)}) collective-permute-start(bf16[128,1024]{1,0:T(8,128)(2,1)S(1)} %get-tuple-element.207), channel_id=1, source_target_pairs={{0,8},{2,10},{4,12},{6,14},{8,0},{10,2},{12,4},{14,6},{1,9},{3,11}... | collective-permute-start | bytes 786440 | tf_op jit(solution)/shard_map/ppermute | solution.py:756
  240.3 52.8 %collective-permute-start.14 = (bf16[128,1024]{1,0:T(8,128)(2,1)S(1)}, bf16[128,1024]{1,0:T(8,128)(2,1)S(1)}, u32[]{:S(2)}, u32[]{:S(2)}) collective-permute-start(bf16[128,1024]{1,0:T(8,128)(2,1)S(1)} %get-tuple-element.206), channel_id=1, source_target_pairs={{0,12},{2,14},{4,8},{6,10},{8,4},{10,6},{12,0},{14,2},{1,13},{3,15... | collective-permute-start | bytes 786440 | tf_op jit(solution)/shard_map/ppermute | solution.py:756
  351.3 27.3 %collective-permute-start.20 = (bf16[512,1024]{1,0:T(8,128)(2,1)}, bf16[512,1024]{1,0:T(8,128)(2,1)S(1)}, u32[]{:S(2)}, u32[]{:S(2)}) collective-permute-start(bf16[512,1024]{1,0:T(8,128)(2,1)} %get-tuple-element.117), channel_id=1, source_target_pairs={{16,0},{17,1},{18,2},{19,3},{20,4},{21,5},{22,6},{23,7},{24,8},{25... | collective-permute-start | bytes 3145736 | tf_op jit(solution)/shard_map/ppermute | solution.py:761
  503.7 21.0 %collective-permute-start.34 = (bf16[4,128,512]{2,1,0:T(8,128)(2,1)}, bf16[4,128,512]{2,1,0:T(8,128)(2,1)}, u32[]{:S(2)}, u32[]{:S(2)}) collective-permute-start(bf16[4,128,512]{2,1,0:T(8,128)(2,1)} %get-tuple-element.132.refs_8_), channel_id=1, source_target_pairs={{0,2},{2,0},{4,6},{6,4},{8,10},{10,8},{12,14},{14,12},{1,3},{3,1},... | collective-permute-start | bytes 1572872 | tf_op jit(solution)/shard_map/ppermute | solution.py:756
  503.8 43.3 %collective-permute-start.37 = (bf16[4,128,512]{2,1,0:T(8,128)(2,1)}, bf16[4,128,512]{2,1,0:T(8,128)(2,1)}, u32[]{:S(2)}, u32[]{:S(2)}) collective-permute-start(bf16[4,128,512]{2,1,0:T(8,128)(2,1)} %get-tuple-element.140), channel_id=1, source_target_pairs={{0,2},{2,0},{4,6},{6,4},{8,10},{10,8},{12,14},{14,12},{1,3},{3,1},... | collective-permute-start | bytes 1572872 | tf_op jit(solution)/shard_map/ppermute | solution.py:756
  507.0 114.7 %collective-permute-start.25 = (bf16[512,1024]{1,0:T(8,128)(2,1)}, bf16[512,1024]{1,0:T(8,128)(2,1)}, u32[]{:S(2)}, u32[]{:S(2)}) collective-permute-start(bf16[512,1024]{1,0:T(8,128)(2,1)} %get-tuple-element.129), channel_id=1, source_target_pairs={{0,1},{1,0},{2,3},{3,2},{4,5},{5,4},{6,7},{7,6},{8,9},{9,8},{10,11... | collective-permute-start | bytes 3145736 | tf_op jit(solution)/shard_map/ppermute | solution.py:752
  507.1 114.7 %collective-permute-start.24 = (bf16[512,1024]{1,0:T(8,128)(2,1)S(1)}, bf16[512,1024]{1,0:T(8,128)(2,1)S(1)}, u32[]{:S(2)}, u32[]{:S(2)}) collective-permute-start(bf16[512,1024]{1,0:T(8,128)(2,1)S(1)} %copy-done.7), channel_id=1, source_target_pairs={{0,2},{2,0},{4,6},{6,4},{8,10},{10,8},{12,14},{14,12},{1,3},{3,1},... | collective-permute-start | bytes 3145736 | tf_op jit(solution)/shard_map/ppermute | solution.py:756
  507.2 86.6 %collective-permute-start.40 = (bf16[4,128,512]{2,1,0:T(8,128)(2,1)}, bf16[4,128,512]{2,1,0:T(8,128)(2,1)S(1)}, u32[]{:S(2)}, u32[]{:S(2)}) collective-permute-start(bf16[4,128,512]{2,1,0:T(8,128)(2,1)} %get-tuple-element.142), channel_id=1, source_target_pairs={{0,2},{2,0},{4,6},{6,4},{8,10},{10,8},{12,14},{14,12},{1,3},{3,1},... | collective-permute-start | bytes 1572872 | tf_op jit(solution)/shard_map/ppermute | solution.py:756
  524.6 97.1 %collective-permute-start.23 = (bf16[512,1024]{1,0:T(8,128)(2,1)}, bf16[512,1024]{1,0:T(8,128)(2,1)S(1)}, u32[]{:S(2)}, u32[]{:S(2)}) collective-permute-start(bf16[512,1024]{1,0:T(8,128)(2,1)} %get-tuple-element.127), channel_id=1, source_target_pairs={{0,1},{1,0},{2,3},{3,2},{4,5},{5,4},{6,7},{7,6},{8,9},{9,8},{10,11... | collective-permute-start | bytes 3145736 | tf_op jit(solution)/shard_map/ppermute | solution.py:752
  547.1 46.9 %collective-permute-start.35 = (bf16[2,128,512]{2,1,0:T(8,128)(2,1)S(1)}, bf16[2,128,512]{2,1,0:T(8,128)(2,1)S(1)}, u32[]{:S(2)}, u32[]{:S(2)}) collective-permute-start(bf16[2,128,512]{2,1,0:T(8,128)(2,1)S(1)} %slice.185), channel_id=1, source_target_pairs={{0,4},{2,6},{4,0},{6,2},{8,12},{10,14},{12,8},{14,10},{1,5},{3,7},... | collective-permute-start | bytes 786440 | tf_op jit(solution)/shard_map/ppermute | solution.py:756
  593.8 20.1 %collective-permute-start.38 = (bf16[2,128,512]{2,1,0:T(8,128)(2,1)S(1)}, bf16[2,128,512]{2,1,0:T(8,128)(2,1)S(1)}, u32[]{:S(2)}, u32[]{:S(2)}) collective-permute-start(bf16[2,128,512]{2,1,0:T(8,128)(2,1)S(1)} %slice.189), channel_id=1, source_target_pairs={{0,4},{2,6},{4,0},{6,2},{8,12},{10,14},{12,8},{14,10},{1,5},{3,7},... | collective-permute-start | bytes 786440 | tf_op jit(solution)/shard_map/ppermute | solution.py:756
  594.0 25.6 %collective-permute-start.41 = (bf16[2,128,512]{2,1,0:T(8,128)(2,1)S(1)}, bf16[2,128,512]{2,1,0:T(8,128)(2,1)S(1)}, u32[]{:S(2)}, u32[]{:S(2)}) collective-permute-start(bf16[2,128,512]{2,1,0:T(8,128)(2,1)S(1)} %slice.193), channel_id=1, source_target_pairs={{0,4},{2,6},{4,0},{6,2},{8,12},{10,14},{12,8},{14,10},{1,5},{3,7},... | collective-permute-start | bytes 786440 | tf_op jit(solution)/shard_map/ppermute | solution.py:756
  613.9 68.8 %collective-permute-start.15 = (bf16[4,128,1024]{2,1,0:T(8,128)(2,1)}, bf16[4,128,1024]{2,1,0:T(8,128)(2,1)S(1)}, u32[]{:S(2)}, u32[]{:S(2)}) collective-permute-start(bf16[4,128,1024]{2,1,0:T(8,128)(2,1)} %get-tuple-element.210), channel_id=1, source_target_pairs={{0,1},{1,0},{2,3},{3,2},{4,5},{5,4},{6,7},{7,6},{8,9},{9,8},{10,11... | collective-permute-start | bytes 3145736 | tf_op jit(solution)/shard_map/ppermute | solution.py:752
  619.6 14.5 %collective-permute-start.36 = (bf16[1,128,512]{2,1,0:T(8,128)(2,1)}, bf16[1,128,512]{2,1,0:T(8,128)(2,1)}, u32[]{:S(2)}, u32[]{:S(2)}) collective-permute-start(bf16[1,128,512]{2,1,0:T(8,128)(2,1)} %slice.187), channel_id=1, source_target_pairs={{0,8},{2,10},{4,12},{6,14},{8,0},{10,2},{12,4},{14,6},{1,9},{3,11}... | collective-permute-start | bytes 393224 | tf_op jit(solution)/shard_map/ppermute | solution.py:756
  630.3 8.3 %collective-permute-start.30 = (f32[5123]{0:T(1024)S(1)}, f32[5123]{0:T(1024)S(1)}, u32[]{:S(2)}, u32[]{:S(2)}) collective-permute-start(f32[5123]{0:T(1024)S(1)} %pad_maximum_fusion.4), channel_id=1, source_target_pairs={{0,1},{1,0},{2,3},{3,2},{4,5},{5,4},{6,7},{7,6},{8,9},{9,8},{10,11... | collective-permute-start | bytes 61484 | tf_op jit(solution)/shard_map/ppermute | solution.py:752
  632.5 13.4 %collective-permute-start.26 = (bf16[128,1024]{1,0:T(8,128)(2,1)}, bf16[128,1024]{1,0:T(8,128)(2,1)S(1)}, u32[]{:S(2)}, u32[]{:S(2)}) collective-permute-start(bf16[128,1024]{1,0:T(8,128)(2,1)} %get-tuple-element.203), channel_id=1, source_target_pairs={{0,4},{2,6},{4,0},{6,2},{8,12},{10,14},{12,8},{14,10},{1,5},{3,7},... | collective-permute-start | bytes 786440 | tf_op jit(solution)/shard_map/ppermute | solution.py:756
  634.1 27.1 %collective-permute-start.27 = (bf16[128,1024]{1,0:T(8,128)(2,1)}, bf16[128,1024]{1,0:T(8,128)(2,1)S(1)}, u32[]{:S(2)}, u32[]{:S(2)}) collective-permute-start(bf16[128,1024]{1,0:T(8,128)(2,1)} %get-tuple-element.202), channel_id=1, source_target_pairs={{0,8},{2,10},{4,12},{6,14},{8,0},{10,2},{12,4},{14,6},{1,9},{3,11}... | collective-permute-start | bytes 786440 | tf_op jit(solution)/shard_map/ppermute | solution.py:756
  634.1 27.7 %collective-permute-start.28 = (bf16[128,1024]{1,0:T(8,128)(2,1)}, bf16[128,1024]{1,0:T(8,128)(2,1)S(1)}, u32[]{:S(2)}, u32[]{:S(2)}) collective-permute-start(bf16[128,1024]{1,0:T(8,128)(2,1)} %get-tuple-element.201), channel_id=1, source_target_pairs={{0,12},{2,14},{4,8},{6,10},{8,4},{10,6},{12,0},{14,2},{1,13},{3,15... | collective-permute-start | bytes 786440 | tf_op jit(solution)/shard_map/ppermute | solution.py:756
  638.6 31.2 %collective-permute-start.39 = (bf16[1,128,512]{2,1,0:T(8,128)(2,1)}, bf16[1,128,512]{2,1,0:T(8,128)(2,1)}, u32[]{:S(2)}, u32[]{:S(2)}) collective-permute-start(bf16[1,128,512]{2,1,0:T(8,128)(2,1)} %slice.191), channel_id=1, source_target_pairs={{0,8},{2,10},{4,12},{6,14},{8,0},{10,2},{12,4},{14,6},{1,9},{3,11}... | collective-permute-start | bytes 393224 | tf_op jit(solution)/shard_map/ppermute | solution.py:756
  645.9 25.9 %collective-permute-start.42 = (bf16[1,128,512]{2,1,0:T(8,128)(2,1)}, bf16[1,128,512]{2,1,0:T(8,128)(2,1)S(1)}, u32[]{:S(2)}, u32[]{:S(2)}) collective-permute-start(bf16[1,128,512]{2,1,0:T(8,128)(2,1)} %slice.195), channel_id=1, source_target_pairs={{0,8},{2,10},{4,12},{6,14},{8,0},{10,2},{12,4},{14,6},{1,9},{3,11}... | collective-permute-start | bytes 393224 | tf_op jit(solution)/shard_map/ppermute | solution.py:756
  661.3 9.5 %collective-permute-start.31 = (f32[8707]{0:T(1024)S(1)}, f32[8707]{0:T(1024)S(1)}, u32[]{:S(2)}, u32[]{:S(2)}) collective-permute-start(f32[8707]{0:T(1024)S(1)} %concatenate.35), channel_id=1, source_target_pairs={{0,2},{2,0},{4,6},{6,4},{8,10},{10,8},{12,14},{14,12},{1,3},{3,1},... | collective-permute-start | bytes 104492 | tf_op jit(solution)/shard_map/ppermute | solution.py:756
  664.9 17.7 %collective-permute-start.29 = (bf16[4,128,1024]{2,1,0:T(8,128)(2,1)}, bf16[4,128,1024]{2,1,0:T(8,128)(2,1)}, u32[]{:S(2)}, u32[]{:S(2)}) collective-permute-start(bf16[4,128,1024]{2,1,0:T(8,128)(2,1)} %get-tuple-element.199), channel_id=1, source_target_pairs={{0,1},{1,0},{2,3},{3,2},{4,5},{5,4},{6,7},{7,6},{8,9},{9,8},{10,11... | collective-permute-start | bytes 3145736 | tf_op jit(solution)/shard_map/ppermute | solution.py:752
  (63 other events, 556.9 us)
Sparse Core Ops, SparseCore 0:
  421.9 197.2 reduce-scatter.1
